TPU v7x, 32 devices: a whole 2x2x4 slice. The times are simulated.
32 devices in a mesh: groups: 2 (over x), shard: 8 (over z, y), mp: 2 (over core).
Axes of the slice: x: 2, y: 2, z: 4, core: 2. Of those that a mesh axis runs over, the one named last changes fastest.
Arguments:
- image_tokens: bfloat16 [4096, 16, 512], P(('groups', 'shard'), None, 'mp'), parts along dimension 0, may hold values from -8 to 8
- pair_owner: int32 [1024, 2], P(('groups', 'shard')), parts along dimension 0, may hold values from 0 to 7, all different within a row; in each aligned block of 64 rows (0 to 63, 64 to 127, ...) at most 32 rows name the same one
- pair_slot: int32 [1024, 2], P(('groups', 'shard')), parts along dimension 0, may hold values from 0 to 255
- gain_attn: float32 [512], replicated, may hold values from 0.1 to 1.9
- w_qk: bfloat16 [512, 512], P(None, 'mp'), may hold values from -0.25 to 0.25
- w_value: bfloat16 [512, 512], P(None, 'mp'), may hold values from -0.25 to 0.25
- logit_scale: float32 [8], P('mp'), may hold values from 0.5 to 30
- w_out: bfloat16 [512, 512], P('mp'), may hold values from -0.25 to 0.25
- gain_mlp: float32 [512], replicated, may hold values from 0.1 to 1.9
- w_in: bfloat16 [512, 2048], P(None, 'mp'), may hold values from -0.25 to 0.25
- bias_in: float32 [2048], P('mp'), may hold values from -3 to 3
- w_back: bfloat16 [2048, 512], P('mp'), may hold values from -0.125 to 0.125
Outputs:
- pair_features: bfloat16 [1024, 512], P(('groups', 'shard')), parts along dimension 0
There are 2 independent parts, one for each index of `groups`. A program takes and returns all parts, laid end to end along the dimension named above; an argument that names none is the same for every part. Nothing has to cross between parts.
Inputs may be any that keep to these rules, and one draw needn't show every extreme that they name: `pair_owner`: the two images of a pair have different owners. Among the 128 images named by the pairs of one index of shard, at most 32 have the same owner; some owner is named exactly 32 times.
All inputs are finite; a program needn't handle non-finite values.
Results may differ from a plain program's by a relative error of at most 0.0095.
Values may be sent and summed in bfloat16 or wider, within the bound.
No kernel may reach another device: no remote copies, remote signals or barrier semaphores. Data moves between devices by JAX's collectives and lax.ppermute only.
A program may use at most 64 MiB of HBM per device.

v0:
```python
import jax
import jax.numpy as jnp
from jax import lax
from jax.sharding import PartitionSpec as P


def norm_rows(values, gain):
    center = values - jnp.mean(values, axis=-1, keepdims=True)
    spread = jnp.mean(center * center, axis=-1, keepdims=True)
    return center * lax.rsqrt(spread + 1e-05) * gain


def attend(tokens, gain_attn, w_qk, w_value, logit_scale, w_out):
    count, sides, length, width = tokens.shape
    heads = logit_scale.shape[0]
    inputs = tokens.astype(jnp.float32)
    normed = norm_rows(inputs, gain_attn).astype(jnp.bfloat16)
    query = jnp.einsum("pstd,dk->pstk", normed, w_qk, preferred_element_type=jnp.float32).astype(
        jnp.bfloat16
    )
    value = jnp.einsum("pstd,dk->pstk", normed, w_value, preferred_element_type=jnp.float32).astype(
        jnp.bfloat16
    )
    head_dim = query.shape[-1] // heads
    query = query.reshape(count, sides, length, heads, head_dim)
    value = value.reshape(count, sides, length, heads, head_dim)
    factor = logit_scale / jnp.sqrt(jnp.float32(head_dim))
    scores = jnp.einsum(
        "psihe,psjhe->pshij", query, query[:, ::-1], preferred_element_type=jnp.float32
    )
    scores = scores * factor[:, None, None]
    probs = jax.nn.softmax(scores, axis=-1).astype(jnp.bfloat16)
    mixed = jnp.einsum(
        "pshij,psjhe->psihe", probs, value[:, ::-1], preferred_element_type=jnp.float32
    )
    mixed = mixed.astype(jnp.bfloat16).reshape(count, sides, length, heads * head_dim)
    return (inputs, jnp.einsum("pstk,kd->pstd", mixed, w_out, preferred_element_type=jnp.float32))


def expand(hidden, gain_mlp, w_in, bias_in, w_back):
    normed = norm_rows(hidden, gain_mlp).astype(jnp.bfloat16)
    inner = jnp.einsum("pstd,df->pstf", normed, w_in, preferred_element_type=jnp.float32) + bias_in
    inner = jax.nn.gelu(inner, approximate=True).astype(jnp.bfloat16)
    back = jnp.einsum("pstf,fd->pstd", inner, w_back, preferred_element_type=jnp.float32)
    return jnp.mean(back, axis=(1, 2))


def place_requests(owners, slots, owner_count, capacity):
    flat_owner = owners.reshape(-1)
    flat_slot = slots.reshape(-1)
    onehot = (flat_owner[:, None] == jnp.arange(owner_count, dtype=jnp.int32)[None, :]).astype(
        jnp.int32
    )
    rank = jnp.sum(jnp.cumsum(onehot, axis=0) * onehot, axis=1) - 1
    where = flat_owner * capacity + rank
    wanted = jnp.zeros((owner_count * capacity,), jnp.int32).at[where].set(flat_slot)
    return (where, wanted.reshape(owner_count, capacity))


def on_device(
    image_tokens,
    pair_owner,
    pair_slot,
    gain_attn,
    w_qk,
    w_value,
    logit_scale,
    w_out,
    gain_mlp,
    w_in,
    bias_in,
    w_back,
):
    owner_count = lax.axis_size("shard")
    pair_count = pair_owner.shape[0]
    length = image_tokens.shape[1]
    capacity = max(2, 4 * pair_count // owner_count)
    where, wanted = place_requests(pair_owner, pair_slot, owner_count, capacity)
    incoming = lax.all_to_all(wanted, "shard", split_axis=0, concat_axis=0, tiled=True)
    served = image_tokens[incoming]
    returned = lax.all_to_all(served, "shard", split_axis=0, concat_axis=0, tiled=True)
    fetched = lax.all_gather(returned, "mp", axis=3, tiled=True)
    width = fetched.shape[-1]
    tokens = fetched.reshape(owner_count * capacity, length, width)[where]
    tokens = tokens.reshape(pair_count, 2, length, width)
    inputs, partial_value = attend(tokens, gain_attn, w_qk, w_value, logit_scale, w_out)
    hidden = inputs + lax.psum(partial_value.astype(jnp.bfloat16), "mp").astype(jnp.float32)
    pooled_back = lax.psum(
        expand(hidden, gain_mlp, w_in, bias_in, w_back).astype(jnp.bfloat16), "mp"
    ).astype(jnp.float32)
    return (jnp.mean(hidden, axis=(1, 2)) + pooled_back).astype(jnp.bfloat16)


def solution(mesh):
    in_specs = (
        P(("groups", "shard"), None, "mp"),
        P(("groups", "shard"), None),
        P(("groups", "shard"), None),
        P(),
        P(None, "mp"),
        P(None, "mp"),
        P("mp"),
        P("mp", None),
        P(),
        P(None, "mp"),
        P("mp"),
        P("mp", None),
    )
    out_specs = P(("groups", "shard"), None)
    return jax.shard_map(
        on_device, mesh=mesh, in_specs=in_specs, out_specs=out_specs, check_vma=False
    )
```

profile of v0, /device:TPU:0, one launch (start us, length us, event | category | flops | bytes accessed | tf_op | source)
XLA Modules:
  0.0 195.2 jit_solution(15816384205887781665)
XLA Ops:
  11.0 13.5 %all_to_all.17 = s32[8,1,32]{2,1,0:T(1,128)S(1)} all-to-all(s32[8,1,32]{2,1,0:T(1,128)S(1)} %all_to_all.11), channel_id=1, replica_groups=mesh['groups'=2,'shard'=8,'mp'=2] {'shard'}, dimensions={0} | all-to-all | bytes 2048 | tf_op jit(solution)/shard_map/all_to_all | solution.py:79
  24.6 2.1 %gather_fusion = bf16[256,16,256]{2,1,0:T(8,128)(2,1)} fusion(bf16[256,16,256]{2,1,0:T(8,128)(2,1)S(1)} %copy-done, s32[1024]{0:T(1024)S(1)} %pad_clamp_fusion.1), kind=kCustom, calls=%fused_computation | custom fusion | bytes 4195328 | tf_op jit(solution)/shard_map/gather | solution.py:80
  26.7 51.5 %all_to_all.18 = bf16[8,32,16,256]{3,2,1,0:T(8,128)(2,1)} all-to-all(bf16[8,32,16,256]{3,2,1,0:T(8,128)(2,1)} %bitcast.54), channel_id=1, replica_groups=mesh['groups'=2,'shard'=8,'mp'=2] {'shard'}, dimensions={0} | all-to-all | bytes 4194304 | tf_op jit(solution)/shard_map/all_to_all | solution.py:81
  78.3 12.0 %all-gather.2.cloned.1.call-done = bf16[8,32,16,512]{3,2,1,0:T(8,128)(2,1)} async-done(((bf16[8,32,16,256]{3,2,1,0:T(8,128)(2,1)}), bf16[8,32,16,512]{3,2,1,0:T(8,128)(2,1)}) %all-gather.2.cloned.1.call-update) | async-done | bytes 4194320 | tf_op jit(solution)/shard_map/all_gather | solution.py:82
  90.4 4.2 %gather_fusion.1 = bf16[128,16,512]{2,1,0:T(8,128)(2,1)} fusion(bf16[256,16,512]{2,1,0:T(8,128)(2,1)} %bitcast.55, s32[1024]{0:T(1024)S(1)} %pad_clamp_fusion), kind=kCustom, calls=%fused_computation.1 | custom fusion | bytes 4194816 | tf_op jit(solution)/shard_map/gather | solution.py:84
  94.6 2.1 %convert_reduce_fusion = f32[128,16]{1,0:T(8,128)S(1)} fusion(bf16[128,16,512]{2,1,0:T(8,128)(2,1)} %gather_fusion.1), kind=kLoop, calls=%fused_computation.27 | loop fusion | flops 2095104 | bytes 2105344 | tf_op jit(solution)/shard_map/reduce_sum | solution.py:8
  96.7 2.7 %multiply_reduce_fusion.1 = f32[128,16]{1,0:T(8,128)S(1)} fusion(bf16[128,16,512]{2,1,0:T(8,128)(2,1)} %gather_fusion.1, f32[128,16]{1,0:T(8,128)S(1)} %broadcast_multiply_fusion.1), kind=kLoop, calls=%fused_computation.19 | loop fusion | flops 4192256 | bytes 2113536 | tf_op jit(solution)/shard_map/reduce_sum | solution.py:9
  99.5 1.1 convolution_convert_fusion.1
  100.6 1.8 reshape.135
  102.5 5.5 %fusion.16 = f32[64,2,4,16,16]{3,4,2,1,0:T(8,128)} fusion(bf16[64,2,16,4,64]{4,3,2,1,0:T(4,128)(2,1)} %reshape.135), kind=kOutput, calls=%fused_computation.25 | convolution fusion | flops 16777216 | bytes 1572864 | tf_op jit(solution)/shard_map/psihe,psjhe->pshij/dot_general | solution.py:28
  108.0 1.1 convolution_convert_fusion.2
  109.1 1.8 reshape.134
  110.9 3.6 %copy.23 = bf16[64,2,16,4,64]{4,2,3,1,0:T(8,128)(2,1)} copy(bf16[64,2,16,4,64]{4,3,2,1,0:T(4,128)(2,1)} %reshape.134) | data formatting | bytes 2097152 | tf_op jit(solution)/shard_map/reshape | solution.py:26
  114.5 3.4 %rev.6 = bf16[64,2,16,4,64]{4,2,3,1,0:T(8,128)(2,1)} reverse(bf16[64,2,16,4,64]{4,2,3,1,0:T(8,128)(2,1)} %copy.23), dimensions={1} | reverse | bytes 2097152 | tf_op jit(solution)/shard_map/rev | solution.py:34
  118.0 5.6 %fusion.42 = (f32[64,2,4,16]{3,2,1,0:T(4,128)S(1)}, f32[64,2,4,16,16]{3,4,2,1,0:T(8,128)S(1)}) fusion(f32[64,2,4,16,16]{3,4,2,1,0:T(8,128)} %fusion.16, f32[4]{0:T(128)S(1)} %broadcast_multiply_fusion.3), kind=kOutput, calls=%fused_computation.68 | output fusion | flops 524303 | bytes 1081360 | tf_op jit(solution)/shard_map/sub | solution.py:32
  124.7 2.6 %copy.27 = bf16[64,2,16,4,64]{4,3,2,1,0:T(4,128)(2,1)} copy(bf16[64,2,16,4,64]{4,2,3,1,0:T(8,128)(2,1)S(1)} %convert_bitcast_fusion) | data formatting | bytes 2097152 | tf_op jit(solution)/shard_map/convert_element_type | solution.py:36
  127.3 3.5 %reshape.136 = bf16[64,2,16,256]{3,2,1,0:T(8,128)(2,1)S(1)} reshape(bf16[64,2,16,4,64]{4,3,2,1,0:T(4,128)(2,1)} %copy.27) | data formatting | bytes 2097152 | tf_op jit(solution)/shard_map/reshape | solution.py:36
  130.8 2.0 %convolution_convert_fusion = bf16[64,2,16,512]{3,2,1,0:T(8,128)(2,1)} fusion(bf16[64,2,16,256]{3,2,1,0:T(8,128)(2,1)S(1)} %reshape.136, bf16[256,512]{1,0:T(8,128)(2,1)S(1)} %copy-done.6), kind=kOutput, calls=%fused_computation.34 | convolution fusion | flops 537919488 | bytes 3407872 | tf_op jit(solution)/shard_map/pstk,kd->pstd/dot_general | solution.py:37
  133.1 22.3 %all-reduce.3.cloned.1.call-done = bf16[64,2,16,512]{3,2,1,0:T(8,128)(2,1)} async-done(((bf16[64,2,16,512]{3,2,1,0:T(8,128)(2,1)}), bf16[64,2,16,512]{3,2,1,0:T(8,128)(2,1)}) %all-reduce.3.cloned.1.call-update) | async-done | bytes 2097168 | tf_op jit(solution)/shard_map/psum | solution.py:87
  155.4 3.4 %fusion.30 = (f32[64,512]{1,0:T(8,128)S(1)}, f32[64,2,16]{2,1,0:T(2,128)S(1)}) fusion(bf16[64,2,16,512]{3,2,1,0:T(8,128)(2,1)} %all-reduce.3.cloned.1.call-done, bf16[64,2,16,512]{3,2,1,0:T(8,128)(2,1)} %bitcast.49), kind=kLoop, calls=%fused_computation.41 | loop fusion | flops 5208064 | bytes 4333568 | tf_op jit(solution)/shard_map/reduce_sum | solution.py:91
  158.9 1.2 multiply_reduce_fusion
  160.2 7.2 %fusion.23 = f32[64,512]{1,0:T(8,128)S(1)} fusion(f32[1024]{0:T(1024)S(1)} %copy-done.10, f32[512]{0:T(512)S(1)} %copy-done.12, f32[64,2,16]{2,1,0:T(2,128)S(1)} %add_rsqrt_fusion, f32[64,2,16]{2,1,0:T(2,128)S(1)} %broadcast_multiply_fusion, bf16[1024,512]{1,0:T(8,128)(2,1)S(1)} %copy-done.7, bf16[512,1024]{1,0:T(8,128)(2,1)} %param.21, ...), kind=kOutput, calls=%fused_computation.35 | convolution fusion | flops 4324294656 | bytes 6445056 | tf_op jit(solution)/shard_map/pstf,fd->pstd/dot_general | solution.py:44
  168.1 19.0 %all-reduce.5.cloned.1.call-done = bf16[64,512]{1,0:T(8,128)(2,1)} async-done(((bf16[64,512]{1,0:T(8,128)(2,1)}), bf16[64,512]{1,0:T(8,128)(2,1)}) %all-reduce.5.cloned.1.call-update) | async-done | bytes 65552 | tf_op jit(solution)/shard_map/psum | solution.py:88
  187.1 1.5 add_convert_fusion
  (58 shorter events, 6.8 us)
Async XLA Ops:
  6.5 18.1 %copy-start = (bf16[256,16,256]{2,1,0:T(8,128)(2,1)S(1)}, bf16[256,16,256]{2,1,0:T(8,128)(2,1)}, u32[]{:S(2)}) copy-start(bf16[256,16,256]{2,1,0:T(8,128)(2,1)} %param.12) | copy-start | bytes 6291460
  6.5 83.8 %all-gather.2.cloned.1.call-start = ((), (), s32[]{:S(2)}) async-start(), calls=%async_computation.2 | async-start | bytes 6291456 | tf_op jit(solution)/shard_map/all_gather | solution.py:82
  26.7 51.6 %copy-start.13 = (f32[4]{0:T(128)S(1)}, f32[4]{0:T(128)}, u32[]{:S(2)}) copy-start(f32[4]{0:T(128)} %param.18) | copy-start | bytes 52
  78.3 77.2 %all-reduce.3.cloned.1.call-start = ((), (), s32[]{:S(2)}) async-start(), calls=%async_computation.3 | async-start | bytes 4194304 | tf_op jit(solution)/shard_map/psum | solution.py:87
  90.4 9.1 %copy-start.8 = (bf16[512,256]{1,0:T(8,128)(2,1)S(1)}, bf16[512,256]{1,0:T(8,128)(2,1)}, u32[]{:S(2)}) copy-start(bf16[512,256]{1,0:T(8,128)(2,1)} %param.16) | copy-start | bytes 786436
  90.4 9.1 %copy-start.11 = (f32[512]{0:T(512)S(1)}, f32[512]{0:T(512)}, u32[]{:S(2)}) copy-start(f32[512]{0:T(512)} %param.15) | copy-start | bytes 6148
  94.6 4.8 %copy-start.1 = (bf16[128,16,512]{2,1,0:T(8,128)(2,1)S(1)}, bf16[128,16,512]{2,1,0:T(8,128)(2,1)}, u32[]{:S(2)}) copy-start(bf16[128,16,512]{2,1,0:T(8,128)(2,1)} %gather_fusion.1) | copy-start | bytes 6291460
  100.6 7.3 %copy-start.9 = (bf16[512,256]{1,0:T(8,128)(2,1)S(1)}, bf16[512,256]{1,0:T(8,128)(2,1)}, u32[]{:S(2)}) copy-start(bf16[512,256]{1,0:T(8,128)(2,1)} %param.17) | copy-start | bytes 786436
  102.5 5.5 %copy-start.2 = (bf16[128,16,512]{2,1,0:T(8,128)(2,1)S(1)}, bf16[128,16,512]{2,1,0:T(8,128)(2,1)}, u32[]{:S(2)}) copy-start(bf16[128,16,512]{2,1,0:T(8,128)(2,1)} %gather_fusion.1) | copy-start | bytes 6291460
  118.0 5.7 %copy-start.5 = (bf16[64,2,16,4,64]{4,2,3,1,0:T(8,128)(2,1)S(1)}, bf16[64,2,16,4,64]{4,2,3,1,0:T(8,128)(2,1)}, u32[]{:S(2)}) copy-start(bf16[64,2,16,4,64]{4,2,3,1,0:T(8,128)(2,1)} %rev.6) | copy-start | bytes 3145732
  124.7 6.1 %copy-start.6 = (bf16[256,512]{1,0:T(8,128)(2,1)S(1)}, bf16[256,512]{1,0:T(8,128)(2,1)}, u32[]{:S(2)}) copy-start(bf16[256,512]{1,0:T(8,128)(2,1)} %param.19) | copy-start | bytes 786436
  132.8 27.3 %copy-start.7 = (bf16[1024,512]{1,0:T(8,128)(2,1)S(1)}, bf16[1024,512]{1,0:T(8,128)(2,1)}, u32[]{:S(2)}) copy-start(bf16[1024,512]{1,0:T(8,128)(2,1)} %param.23) | copy-start | bytes 3145732
  132.8 27.3 %copy-start.10 = (f32[1024]{0:T(1024)S(1)}, f32[1024]{0:T(1024)}, u32[]{:S(2)}) copy-start(f32[1024]{0:T(1024)} %param.22) | copy-start | bytes 12292
  132.9 27.3 %copy-start.12 = (f32[512]{0:T(512)S(1)}, f32[512]{0:T(512)}, u32[]{:S(2)}) copy-start(f32[512]{0:T(512)} %param.20) | copy-start | bytes 6148
  132.9 54.3 %all-reduce.5.cloned.1.call-start = ((), (), s32[]{:S(2)}) async-start(), calls=%async_computation.4 | async-start | bytes 131072 | tf_op jit(solution)/shard_map/psum | solution.py:88
  155.4 3.4 %copy-start.3 = (bf16[128,16,512]{2,1,0:T(8,128)(2,1)S(1)}, bf16[128,16,512]{2,1,0:T(8,128)(2,1)}, u32[]{:S(2)}) copy-start(bf16[128,16,512]{2,1,0:T(8,128)(2,1)} %gather_fusion.1) | copy-start | bytes 6291460
  155.4 3.5 %copy-start.4 = (bf16[64,2,16,512]{3,2,1,0:T(8,128)(2,1)S(1)}, bf16[64,2,16,512]{3,2,1,0:T(8,128)(2,1)}, u32[]{:S(2)}) copy-start(bf16[64,2,16,512]{3,2,1,0:T(8,128)(2,1)} %all-reduce.3.cloned.1.call-done) | copy-start | bytes 6291460
Sparse Core Ops, SparseCore 0:
  78.4 11.9 all-gather.1
  133.0 22.4 all-reduce.2
  168.2 18.8 all-reduce.4
where the time goes:
time: 196 us; the launch traced here: 195 us
  blocking collectives  65.1 us (33%)
  waiting for transfers between devices  53.5 us (27%)
  local copies, waits for them, and re-layouts  26.6 us (14%)
  other arithmetic  18.3 us (9%)
  matrix products  18.1 us (9%)
  between operations  13.4 us (7%)
    all_to_all x1, blocking collectives, on_device(): lax.all_to_all(served, 'shard', split_axis=0, concat_axis=0, tiled=True)  51.5 us
    psum x1, waiting for transfers between devices, on_device(): lax.psum(partial_value.astype(jnp.bfloat16), 'mp').astype(jnp.float32)  22.3 us
    psum x1, waiting for transfers between devices, on_device(): lax.psum(expand(hidden, gain_mlp, w_in, bias_in, w_back).astype(jnp.bfloa...  19 us
    all_to_all x1, blocking collectives, on_device(): lax.all_to_all(wanted, 'shard', split_axis=0, concat_axis=0, tiled=True)  13.5 us
    all_gather x1, waiting for transfers between devices, on_device(): fetched = lax.all_gather(returned, 'mp', axis=3, tiled=True)  12 us
    dot_general x1, matrix products, expand(): jnp.einsum('pstf,fd->pstd', inner, w_back, preferred_element_type=jnp.flo...  7.24 us
    sub x1, other arithmetic, attend(): probs = jax.nn.softmax(scores, axis=-1).astype(jnp.bfloat16)  5.65 us
    dot_general x1, matrix products, attend(): jnp.einsum('psihe,psjhe->pshij', query, query[:, ::-1], preferred_element...  5.5 us
  transfers between devices with their start and end apart: 3, of which 3 were waited for; matrix products, arithmetic and copies ran while one was open for 0% of the time, Pallas kernels for 0%

commit v1 on v0

v1 whole, which is shorter than its diff:
```python
import functools

import jax
import jax.numpy as jnp
from jax import lax
from jax.experimental import pallas as pl
from jax.experimental.pallas import tpu as pltpu
from jax.sharding import PartitionSpec as P

LOG2E = 1.4426950408889634


def norm_rows(values, gain):
    center = values - jnp.mean(values, axis=-1, keepdims=True)
    spread = jnp.mean(center * center, axis=-1, keepdims=True)
    return center * lax.rsqrt(spread + 1e-05) * gain


def dot_nt(a, b):
    return lax.dot_general(a, b, (((1,), (1,)), ((), ())), preferred_element_type=jnp.float32)


def dot(a, b):
    return jnp.dot(a, b, preferred_element_type=jnp.float32)


def compare_kernel(
    length,
    head_dim,
    core_ref,
    scale_ref,
    own_ref,
    far_ref,
    gain_attn_ref,
    qk_a_ref,
    qk_b_ref,
    value_a_ref,
    value_b_ref,
    out_a_ref,
    out_b_ref,
    gain_mlp_ref,
    in_a_ref,
    in_b_ref,
    bias_a_ref,
    bias_b_ref,
    back_a_ref,
    back_b_ref,
    result_ref,
    pooled_ref,
    hidden_ref,
):
    half = 8 * length
    rows = 2 * half
    blocks = own_ref.shape[0] // rows
    pair_dim = 2 * head_dim
    first = core_ref[0] == 0
    lane = lax.broadcasted_iota(jnp.int32, (half, pair_dim), 1)
    even = lane < head_dim
    same = (
        lax.broadcasted_iota(jnp.int32, (half, half), 0) // length
        == lax.broadcasted_iota(jnp.int32, (half, half), 1) // length
    )

    def split(values):
        zero = jnp.zeros_like(values)
        return jnp.concatenate(
            [jnp.where(even, values, zero), jnp.where(even, zero, values)], axis=0
        )

    def softmax(scores, factor):
        scores = jnp.where(same, scores, -1e30)
        top = jnp.max(scores, axis=1, keepdims=True)
        weights = jnp.exp2((scores - top) * factor)
        return (weights * (1.0 / jnp.sum(weights, axis=1, keepdims=True))).astype(jnp.bfloat16)

    def block(step, carry):
        span = pl.ds(pl.multiple_of(step * rows, rows), rows)
        own = own_ref[span, :].astype(jnp.float32)
        far = far_ref[span, :].astype(jnp.float32)
        tokens = jnp.concatenate(
            [jnp.where(first, own, far), jnp.where(first, far, own)], axis=1
        )
        normed = norm_rows(tokens, gain_attn_ref[...]).astype(jnp.bfloat16)
        hidden = tokens
        head = 0
        for qk_ref, value_ref, out_ref in (
            (qk_a_ref, value_a_ref, out_a_ref),
            (qk_b_ref, value_b_ref, out_b_ref),
        ):
            query = dot(normed, qk_ref[...]).astype(jnp.bfloat16)
            value = dot(normed, value_ref[...]).astype(jnp.bfloat16)
            mixed = []
            for start in range(0, query.shape[1], pair_dim):
                factors = [scale_ref[head + k] * (LOG2E / head_dim**0.5) for k in range(2)]
                head += 2
                q = query[:, start : start + pair_dim]
                v = value[:, start : start + pair_dim]
                sides = []
                for side in range(2):
                    here = slice(side * half, (side + 1) * half)
                    there = slice((1 - side) * half, (2 - side) * half)
                    scores = dot_nt(q[here], split(q[there]))
                    probs = [
                        softmax(scores[:, k * half : (k + 1) * half], factors[k]) for k in range(2)
                    ]
                    sides.append(
                        dot(jnp.concatenate(probs, axis=1), split(v[there])).astype(jnp.bfloat16)
                    )
                mixed.append(jnp.concatenate(sides, axis=0))
            hidden = hidden + dot(jnp.concatenate(mixed, axis=1), out_ref[...])
        at = pl.ds(pl.multiple_of(step * 8, 8), 8)
        hidden_ref[at, :] = jnp.sum(hidden.reshape(2, 8, length, -1), axis=(0, 2))
        normed = norm_rows(hidden, gain_mlp_ref[...]).astype(jnp.bfloat16)
        offset = 0
        for in_ref, bias_ref in ((in_a_ref, bias_a_ref), (in_b_ref, bias_b_ref)):
            units = in_ref.shape[1]
            tile = min(256, units)
            for start in range(0, units, tile):
                cut = slice(start, start + tile)
                inner = dot(normed, in_ref[:, cut]) + bias_ref[:, cut]
                bent = jnp.tanh(inner * (0.7978845608028654 + 0.035677408136300125 * (inner * inner)))
                inner = inner * bent + inner
                pooled_ref[at, offset + start : offset + start + tile] = jnp.sum(
                    inner.reshape(2, 8, length, -1), axis=(0, 2)
                )
            offset += units
        return carry

    lax.fori_loop(0, blocks, block, 0)
    pooled = pooled_ref[...] * (0.25 / length)
    coarse = pooled.astype(jnp.bfloat16)
    fine = (pooled - coarse.astype(jnp.float32)).astype(jnp.bfloat16)
    both = jnp.concatenate([coarse, fine], axis=0)
    units = back_a_ref.shape[0]
    back = dot(both[:, :units], back_a_ref[...]) + dot(both[:, units:], back_b_ref[...])
    count = result_ref.shape[0]
    mean = hidden_ref[...] * (0.5 / length)
    result_ref[...] = (mean + back[:count] + back[count:]).astype(jnp.bfloat16)


def place_requests(owners, slots, owner_count, capacity):
    flat_owner = owners.reshape(-1)
    flat_slot = slots.reshape(-1)
    onehot = (flat_owner[:, None] == jnp.arange(owner_count, dtype=jnp.int32)[None, :]).astype(
        jnp.int32
    )
    rank = jnp.sum(jnp.cumsum(onehot, axis=0) * onehot, axis=1) - 1
    where = flat_owner * capacity + rank
    wanted = jnp.zeros((owner_count * capacity,), jnp.int32).at[where].set(flat_slot)
    return (where, wanted.reshape(owner_count, capacity))


def on_device(
    image_tokens,
    pair_owner,
    pair_slot,
    gain_attn,
    w_qk,
    w_value,
    logit_scale,
    w_out,
    gain_mlp,
    w_in,
    bias_in,
    w_back,
):
    owner_count = lax.axis_size("shard")
    core = lax.axis_index("mp")
    pair_count = pair_owner.shape[0]
    _, length, features = image_tokens.shape
    width = 2 * features
    head_dim = w_qk.shape[1] // logit_scale.shape[0]
    capacity = max(2, 4 * pair_count // owner_count)
    mine = pair_count // 2

    def swap(values):
        return lax.ppermute(values, "mp", [(0, 1), (1, 0)])

    where, wanted = place_requests(pair_owner, pair_slot, owner_count, capacity)
    incoming = lax.all_to_all(wanted, "shard", split_axis=0, concat_axis=0, tiled=True)
    weights = (w_qk, w_value, w_out, w_in, w_back, bias_in, logit_scale)
    far_qk, far_value, far_out, far_in, far_back, far_bias, far_scale = [swap(w) for w in weights]
    served = image_tokens[incoming]
    returned = lax.all_to_all(served, "shard", split_axis=0, concat_axis=0, tiled=True)
    returned = returned.reshape(owner_count * capacity, length, features)
    order = where.reshape(2, mine // 8, 8, 2).transpose(0, 1, 3, 2).reshape(2, 2 * mine)
    far = swap(returned[order[1 - core]])
    own = returned[order[core]]

    smem = pl.BlockSpec(memory_space=pltpu.SMEM)
    vmem = pl.BlockSpec(memory_space=pltpu.VMEM)
    units = 2 * w_in.shape[1]
    flops = 4 * mine * length * width * (3 * width + units)
    features_here = pl.pallas_call(
        functools.partial(compare_kernel, length, head_dim),
        out_shape=jax.ShapeDtypeStruct((mine, width), jnp.bfloat16),
        in_specs=[smem, smem] + [vmem] * 16,
        out_specs=vmem,
        scratch_shapes=[
            pltpu.VMEM((mine, units), jnp.float32),
            pltpu.VMEM((mine, width), jnp.float32),
        ],
        compiler_params=pltpu.CompilerParams(vmem_limit_bytes=48 * 2**20),
        cost_estimate=pl.CostEstimate(
            flops=flops, bytes_accessed=8 * 2**20, transcendentals=2 * mine * length * units
        ),
    )(
        core.reshape(1),
        jnp.concatenate([logit_scale, far_scale]),
        own.reshape(-1, features),
        far.reshape(-1, features),
        gain_attn.reshape(1, -1),
        w_qk,
        far_qk,
        w_value,
        far_value,
        w_out,
        far_out,
        gain_mlp.reshape(1, -1),
        w_in,
        far_in,
        bias_in.reshape(1, -1),
        far_bias.reshape(1, -1),
        w_back,
        far_back,
    )
    features_there = swap(features_here)
    low = jnp.where(core == 0, features_here, features_there)
    high = jnp.where(core == 0, features_there, features_here)
    return jnp.concatenate([low, high], axis=0)


def solution(mesh):
    in_specs = (
        P(("groups", "shard"), None, "mp"),
        P(("groups", "shard"), None),
        P(("groups", "shard"), None),
        P(),
        P(None, "mp"),
        P(None, "mp"),
        P("mp"),
        P("mp", None),
        P(),
        P(None, "mp"),
        P("mp"),
        P("mp", None),
    )
    out_specs = P(("groups", "shard"), None)
    return jax.shard_map(
        on_device, mesh=mesh, in_specs=in_specs, out_specs=out_specs, check_vma=False
    )
```

time: 196 us -> 100 us (0.51)
  blocking collectives: 65.1 us -> 13.5 us
  matrix products: 18.1 us -> 0 us
  Pallas kernels: 0 us -> 16.3 us
  other arithmetic: 18.3 us -> 2.03 us
  local copies, waits for them, and re-layouts: 26.6 us -> 12.5 us
  between operations: 13.4 us -> 0.21 us
  starting transfers between devices: 0.27 us -> 6.87 us
  waiting for transfers between devices: 53.5 us -> 48.7 us
    all_to_all x1 -> x0, blocking collectives: 51.5 us -> none  [on_device(): lax.all_to_all(served, 'shard', split_axis=0, concat_axis=0, tiled=True)]
    all_to_all x0 -> x1, waiting for transfers between devices: none -> 45.9 us  [on_device(): lax.all_to_all(served, 'shard', split_axis=0, concat_axis=0, tiled=True)]
    psum x2 -> x0, waiting for transfers between devices: 41.4 us -> none  [the longest x1 22.3 us: on_device(): lax.psum(partial_value.astype(jnp.bfloat16), 'mp').astype(jnp.float32)]
    dot_general x6 -> x0, matrix products: 18.1 us -> none  [the longest x1 7.24 us: expand(): jnp.einsum('pstf,fd->pstd', inner, w_back, preferred_element_type=jnp.flo...]
    pallas_call x0 -> x1, Pallas kernels: none -> 16.3 us  [on_device(): pl.pallas_call(functools.partial(compare_kernel, length, head_dim), out_s...]
    all_gather x1 -> x0, waiting for transfers between devices: 12 us -> none  [on_device(): fetched = lax.all_gather(returned, 'mp', axis=3, tiled=True)]
    reshape x4 -> x1, local copies, waits for them, and re-layouts: 10.7 us -> 0.09 us  [on_device(): where.reshape(2, mine // 8, 8, 2).transpose(0, 1, 3, 2).reshape(2, 2 * mine)]
    reduce_sum x4 -> x0, other arithmetic: 9.31 us -> none  [the longest x2 3.86 us: norm_rows(): spread = jnp.mean(center * center, axis=-1, keepdims=True)]
  transfers between devices with their start and end apart: 3 -> 10, of which waited for: 3 -> 4; matrix products, arithmetic and copies ran while one was open for 0% -> 6% of each run, Pallas kernels for 0% -> 0%
where the time goes in v1:
time: 100 us
  waiting for transfers between devices  48.7 us (49%)
  Pallas kernels  16.3 us (16%)
  blocking collectives  13.5 us (14%)
  local copies, waits for them, and re-layouts  12.5 us (12%)
  starting transfers between devices  6.87 us (7%)
  other arithmetic  2.03 us (2%)
    all_to_all x1, waiting for transfers between devices, on_device(): lax.all_to_all(served, 'shard', split_axis=0, concat_axis=0, tiled=True)  45.9 us
    pallas_call x1, Pallas kernels, on_device(): pl.pallas_call(functools.partial(compare_kernel, length, head_dim), out_s...  16.3 us
    all_to_all x1, blocking collectives, on_device(): lax.all_to_all(wanted, 'shard', split_axis=0, concat_axis=0, tiled=True)  13.5 us
    all_to_all x1, starting transfers between devices, on_device(): lax.all_to_all(served, 'shard', split_axis=0, concat_axis=0, tiled=True)  4.47 us
    unnamed x18, local copies, waits for them, and re-layouts  3.22 us
    gather x1, local copies, waits for them, and re-layouts, on_device(): far = swap(returned[order[1 - core]])  2.98 us
    ppermute x9, waiting for transfers between devices, swap(): return lax.ppermute(values, 'mp', [(0, 1), (1, 0)])  2.75 us
    ppermute x9, starting transfers between devices, swap(): return lax.ppermute(values, 'mp', [(0, 1), (1, 0)])  2.4 us
  transfers between devices with their start and end apart: 10, of which 4 were waited for; matrix products, arithmetic and copies ran while one was open for 6% of the time, Pallas kernels for 0%

profile of v1, /device:TPU:0, one launch (start us, length us, event | category | flops | bytes accessed | tf_op | source)
XLA Modules:
  0.0 100.1 jit_solution(964859847535259906)
XLA Ops:
  0.0 0.8 broadcast_multiply_fusion
  0.8 0.8 copy.19
  2.1 0.2 reduce_window_sum.11
  2.4 0.8 copy.20
  3.4 1.0 scatter_custom_fusion
  4.4 13.5 %all_to_all.17 = s32[8,1,32]{2,1,0:T(1,128)S(1)} all-to-all(s32[8,1,32]{2,1,0:T(1,128)S(1)} %all_to_all.11), channel_id=1, replica_groups=mesh['groups'=2,'shard'=8,'mp'=2] {'shard'}, dimensions={0} | all-to-all | bytes 2048 | tf_op jit(solution)/shard_map/all_to_all | solution.py:180
  18.0 2.1 %gather_fusion = bf16[256,16,256]{2,1,0:T(8,128)(2,1)} fusion(bf16[256,16,256]{2,1,0:T(8,128)(2,1)S(1)} %copy-done, s32[1024]{0:T(1024)S(1)} %pad_clamp_fusion.2), kind=kCustom, calls=%fused_computation | custom fusion | bytes 4195328 | tf_op jit(solution)/shard_map/gather | solution.py:183
  20.1 4.5 %all-to-all-start.1 = ((bf16[8,32,16,256]{3,2,1,0:T(8,128)(2,1)}), bf16[8,32,16,256]{3,2,1,0:T(8,128)(2,1)}, u32[]{:S(2)}, u32[]{:S(2)}) async-start(bf16[8,32,16,256]{3,2,1,0:T(8,128)(2,1)} %bitcast.36), calls=%async_computation.1 | async-start | bytes 4194304 | tf_op jit(solution)/shard_map/all_to_all | solution.py:184
  24.7 0.5 collective-permute-start.5
  25.8 45.9 %all-to-all-done.1 = bf16[8,32,16,256]{3,2,1,0:T(8,128)(2,1)} async-done(((bf16[8,32,16,256]{3,2,1,0:T(8,128)(2,1)}), bf16[8,32,16,256]{3,2,1,0:T(8,128)(2,1)}, u32[]{:S(2)}, u32[]{:S(2)}) %all-to-all-start.1) | async-done | bytes 2097184 | tf_op jit(solution)/shard_map/all_to_all | solution.py:184
  71.7 3.0 %gather_fusion.2 = bf16[64,16,256]{2,1,0:T(8,128)(2,1)} fusion(bf16[256,16,256]{2,1,0:T(8,128)(2,1)} %bitcast.5, s32[1024]{0:T(1024)S(1)} %pad_clamp_fusion), kind=kCustom, calls=%fused_computation.2 | custom fusion | bytes 1048832 | tf_op jit(solution)/shard_map/gather | solution.py:187
  74.7 0.5 collective-permute-start
  75.2 1.0 %collective-permute-done = f32[4]{0:T(128)S(1)} collective-permute-done((f32[4]{0:T(128)S(1)}, f32[4]{0:T(128)S(1)}, u32[]{:S(2)}, u32[]{:S(2)}) %collective-permute-start) | collective-permute-done | bytes 48 | tf_op jit(solution)/shard_map/ppermute | solution.py:177
  76.2 0.3 collective-permute-start.6
  76.5 0.8 collective-permute-done.6
  77.4 0.3 collective-permute-start.3
  77.7 0.7 copy-done.2
  78.4 0.2 collective-permute-start.4
  78.7 2.2 %gather_fusion.1 = bf16[64,16,256]{2,1,0:T(8,128)(2,1)S(1)} fusion(bf16[256,16,256]{2,1,0:T(8,128)(2,1)} %bitcast.5, s32[1024]{0:T(1024)S(1)} %pad_clamp_fusion.1), kind=kCustom, calls=%fused_computation.1 | custom fusion | bytes 1048832 | tf_op jit(solution)/shard_map/gather | solution.py:188
  81.0 0.9 copy-done.3
  81.9 16.3 %shard_map.118 = bf16[32,512]{1,0:T(8,128)(2,1)S(1)} custom-call(s32[1]{0:T(128)} %bitcast.core_ref, f32[8]{0:T(128)S(1)} %pad_maximum_fusion.1.scale_ref, bf16[1024,256]{1,0:T(8,128)(2,1)S(1)} %bitcast.30, bf16[1024,256]{1,0:T(8,128)(2,1)S(1)} %bitcast.31, f32[1,512]{1,0:T(1,128)S(1)} %bitcast.34, bf16[512,256]{1,0:T(8,128)(2,1)S(1)} %copy-done.1, ...), custom_call_target="tpu_custom_call" | custom-call | flops 3758096384 | bytes 8388608 | tf_op jit(solution)/shard_map/pallas_call | solution.py:194
  98.2 0.4 collective-permute-start.8
  98.6 0.9 collective-permute-done.8
  99.4 0.6 pad_maximum_fusion
  (46 shorter events, 1.7 us)
Async XLA Ops:
  0.0 18.0 %copy-start = (bf16[256,16,256]{2,1,0:T(8,128)(2,1)S(1)}, bf16[256,16,256]{2,1,0:T(8,128)(2,1)}, u32[]{:S(2)}) copy-start(bf16[256,16,256]{2,1,0:T(8,128)(2,1)} %param.12) | copy-start | bytes 6291460
  20.1 4.5 %copy-start.1 = (bf16[512,256]{1,0:T(8,128)(2,1)S(1)}, bf16[512,256]{1,0:T(8,128)(2,1)}, u32[]{:S(2)}) copy-start(bf16[512,256]{1,0:T(8,128)(2,1)} %qk_a_ref.1) | copy-start | bytes 786436
  20.1 54.6 %copy-start.7 = (f32[4]{0:T(128)S(1)}, f32[4]{0:T(128)}, u32[]{:S(2)}) copy-start(f32[4]{0:T(128)} %param.18) | copy-start | bytes 52
  20.1 56.1 %copy-start.4 = (f32[1024]{0:T(1024)S(1)}, f32[1024]{0:T(1024)}, u32[]{:S(2)}) copy-start(f32[1024]{0:T(1024)} %param.22) | copy-start | bytes 12292
  20.1 51.6 %all-to-all-start.1 = ((bf16[8,32,16,256]{3,2,1,0:T(8,128)(2,1)}), bf16[8,32,16,256]{3,2,1,0:T(8,128)(2,1)}, u32[]{:S(2)}, u32[]{:S(2)}) async-start(bf16[8,32,16,256]{3,2,1,0:T(8,128)(2,1)} %bitcast.36), calls=%async_computation.1 | async-start | bytes 4194304 | tf_op jit(solution)/shard_map/all_to_all | solution.py:184
  24.6 56.3 %copy-start.5 = (f32[512]{0:T(512)S(1)}, f32[512]{0:T(512)}, u32[]{:S(2)}) copy-start(f32[512]{0:T(512)} %param.15) | copy-start | bytes 6148
  24.6 56.3 %copy-start.6 = (f32[512]{0:T(512)S(1)}, f32[512]{0:T(512)}, u32[]{:S(2)}) copy-start(f32[512]{0:T(512)} %param.20) | copy-start | bytes 6148
  24.6 53.1 %collective-permute-start.2 = (bf16[512,256]{1,0:T(8,128)(2,1)S(1)}, bf16[512,256]{1,0:T(8,128)(2,1)S(1)}, u32[]{:S(2)}, u32[]{:S(2)}) collective-permute-start(bf16[512,256]{1,0:T(8,128)(2,1)S(1)} %copy-done.1), channel_id=1, source_target_pairs={{0,1},{1,0},{2,3},{3,2},{4,5},{5,4},{6,7},{7,6},{8,9},{9,8},{10,11... | collective-permute-start | bytes 786440 | tf_op jit(solution)/shard_map/ppermute | solution.py:177
  24.7 56.2 %collective-permute-start.5 = (bf16[512,1024]{1,0:T(8,128)(2,1)}, bf16[512,1024]{1,0:T(8,128)(2,1)}, u32[]{:S(2)}, u32[]{:S(2)}) collective-permute-start(bf16[512,1024]{1,0:T(8,128)(2,1)} %in_a_ref.1), channel_id=1, source_target_pairs={{0,1},{1,0},{2,3},{3,2},{4,5},{5,4},{6,7},{7,6},{8,9},{9,8},{10,11... | collective-permute-start | bytes 3145736 | tf_op jit(solution)/shard_map/ppermute | solution.py:177
  25.2 55.7 %collective-permute-start.7 = (bf16[1024,512]{1,0:T(8,128)(2,1)}, bf16[1024,512]{1,0:T(8,128)(2,1)}, u32[]{:S(2)}, u32[]{:S(2)}) collective-permute-start(bf16[1024,512]{1,0:T(8,128)(2,1)} %back_a_ref.1), channel_id=1, source_target_pairs={{0,1},{1,0},{2,3},{3,2},{4,5},{5,4},{6,7},{7,6},{8,9},{9,8},{10,11... | collective-permute-start | bytes 3145736 | tf_op jit(solution)/shard_map/ppermute | solution.py:177
  74.7 6.2 %collective-permute-start.1 = (bf16[64,16,256]{2,1,0:T(8,128)(2,1)}, bf16[64,16,256]{2,1,0:T(8,128)(2,1)S(1)}, u32[]{:S(2)}, u32[]{:S(2)}) collective-permute-start(bf16[64,16,256]{2,1,0:T(8,128)(2,1)} %gather_fusion.2), channel_id=1, source_target_pairs={{0,1},{1,0},{2,3},{3,2},{4,5},{5,4},{6,7},{7,6},{8,9},{9,8},{10,11... | collective-permute-start | bytes 1572872 | tf_op jit(solution)/shard_map/ppermute | solution.py:177
  74.7 1.5 %collective-permute-start = (f32[4]{0:T(128)S(1)}, f32[4]{0:T(128)S(1)}, u32[]{:S(2)}, u32[]{:S(2)}) collective-permute-start(f32[4]{0:T(128)S(1)} %copy-done.7), channel_id=1, source_target_pairs={{0,1},{1,0},{2,3},{3,2},{4,5},{5,4},{6,7},{7,6},{8,9},{9,8},{10,11... | collective-permute-start | bytes 56 | tf_op jit(solution)/shard_map/ppermute | solution.py:177
  76.2 1.2 %collective-permute-start.6 = (f32[1024]{0:T(1024)S(1)}, f32[1024]{0:T(1024)S(1)}, u32[]{:S(2)}, u32[]{:S(2)}) collective-permute-start(f32[1024]{0:T(1024)S(1)} %copy-done.4), channel_id=1, source_target_pairs={{0,1},{1,0},{2,3},{3,2},{4,5},{5,4},{6,7},{7,6},{8,9},{9,8},{10,11... | collective-permute-start | bytes 12296 | tf_op jit(solution)/shard_map/ppermute | solution.py:177
  77.4 3.5 %collective-permute-start.3 = (bf16[512,256]{1,0:T(8,128)(2,1)}, bf16[512,256]{1,0:T(8,128)(2,1)}, u32[]{:S(2)}, u32[]{:S(2)}) collective-permute-start(bf16[512,256]{1,0:T(8,128)(2,1)} %value_a_ref.1), channel_id=1, source_target_pairs={{0,1},{1,0},{2,3},{3,2},{4,5},{5,4},{6,7},{7,6},{8,9},{9,8},{10,11... | collective-permute-start | bytes 786440 | tf_op jit(solution)/shard_map/ppermute | solution.py:177
  77.7 0.7 copy-start.2
  78.4 2.5 %collective-permute-start.4 = (bf16[256,512]{1,0:T(8,128)(2,1)}, bf16[256,512]{1,0:T(8,128)(2,1)}, u32[]{:S(2)}, u32[]{:S(2)}) collective-permute-start(bf16[256,512]{1,0:T(8,128)(2,1)} %out_a_ref.1), channel_id=1, source_target_pairs={{0,1},{1,0},{2,3},{3,2},{4,5},{5,4},{6,7},{7,6},{8,9},{9,8},{10,11... | collective-permute-start | bytes 786440 | tf_op jit(solution)/shard_map/ppermute | solution.py:177
  80.9 1.0 copy-start.3
  98.2 1.3 %collective-permute-start.8 = (bf16[32,512]{1,0:T(8,128)(2,1)S(1)}, bf16[32,512]{1,0:T(8,128)(2,1)S(1)}, u32[]{:S(2)}, u32[]{:S(2)}) collective-permute-start(bf16[32,512]{1,0:T(8,128)(2,1)S(1)} %shard_map.118), channel_id=1, source_target_pairs={{0,1},{1,0},{2,3},{3,2},{4,5},{5,4},{6,7},{7,6},{8,9},{9,8},{10,11... | collective-permute-start | bytes 98312 | tf_op jit(solution)/shard_map/ppermute | solution.py:177

commit v2 on v1

--- a/solution.py
+++ b/solution.py
@@ -29,7 +29,8 @@
     head_dim,
     core_ref,
     scale_ref,
-    own_ref,
+    list_ref,
+    returned_ref,
     far_ref,
     gain_attn_ref,
     qk_a_ref,
@@ -46,14 +47,24 @@
     back_a_ref,
     back_b_ref,
     result_ref,
+    own_ref,
     pooled_ref,
     hidden_ref,
+    sems,
 ):
     half = 8 * length
     rows = 2 * half
-    blocks = own_ref.shape[0] // rows
+    blocks = own_ref.shape[0] // 16
     pair_dim = 2 * head_dim
     first = core_ref[0] == 0
+    start = core_ref[0] * own_ref.shape[0]
+
+    def begin(index, carry):
+        source = returned_ref.at[list_ref[0, start + index]]
+        pltpu.make_async_copy(source, own_ref.at[index], sems.at[index // 16]).start()
+        return carry
+
+    lax.fori_loop(0, own_ref.shape[0], begin, 0, unroll=8)
     lane = lax.broadcasted_iota(jnp.int32, (half, pair_dim), 1)
     even = lane < head_dim
     same = (
@@ -74,9 +85,12 @@
         return (weights * (1.0 / jnp.sum(weights, axis=1, keepdims=True))).astype(jnp.bfloat16)
 
     def block(step, carry):
-        span = pl.ds(pl.multiple_of(step * rows, rows), rows)
-        own = own_ref[span, :].astype(jnp.float32)
-        far = far_ref[span, :].astype(jnp.float32)
+        span = pl.ds(pl.multiple_of(step * 16, 16), 16)
+        pltpu.make_async_copy(
+            returned_ref.at[pl.ds(0, 16)], own_ref.at[span], sems.at[step]
+        ).wait()
+        own = own_ref[span].reshape(rows, -1).astype(jnp.float32)
+        far = far_ref[span].reshape(rows, -1).astype(jnp.float32)
         tokens = jnp.concatenate(
             [jnp.where(first, own, far), jnp.where(first, far, own)], axis=1
         )
@@ -138,16 +152,60 @@
     result_ref[...] = (mean + back[:count] + back[count:]).astype(jnp.bfloat16)
 
 
-def place_requests(owners, slots, owner_count, capacity):
-    flat_owner = owners.reshape(-1)
-    flat_slot = slots.reshape(-1)
-    onehot = (flat_owner[:, None] == jnp.arange(owner_count, dtype=jnp.int32)[None, :]).astype(
-        jnp.int32
-    )
-    rank = jnp.sum(jnp.cumsum(onehot, axis=0) * onehot, axis=1) - 1
-    where = flat_owner * capacity + rank
-    wanted = jnp.zeros((owner_count * capacity,), jnp.int32).at[where].set(flat_slot)
-    return (where, wanted.reshape(owner_count, capacity))
+def place_kernel(count, capacity, owner_ref, slot_ref, wanted_ref, list_ref):
+    owners = wanted_ref.shape[0]
+    total = 2 * count
+    owner = jnp.concatenate([owner_ref[0:1, :], owner_ref[1:2, :]], axis=1)
+    slot = jnp.concatenate([slot_ref[0:1, :], slot_ref[1:2, :]], axis=1)
+
+    def place(dim, size):
+        return lax.broadcasted_iota(jnp.int32, (size, total), dim)
+
+    def as_bf16(values):
+        return values.astype(jnp.float32).astype(jnp.bfloat16)
+
+    named = place(0, owners) == owner
+    until = as_bf16(jnp.where(place(0, total) <= place(1, total), 1, 0))
+    tally = dot(as_bf16(jnp.where(named, 1, 0)), until).astype(jnp.int32)
+    rank = jnp.sum(jnp.where(named, tally, 0), axis=0, keepdims=True) - 1
+    ranked = as_bf16(jnp.where(place(0, total) == rank, 1, 0))
+    wanted = dot_nt(as_bf16(jnp.where(named, slot, 0)), ranked).astype(jnp.int32)
+    for index in range(owners):
+        wanted_ref[index] = wanted[index : index + 1, :capacity]
+    where = owner * capacity + rank
+    entry = place(1, 1)
+    side = entry // count
+    pair = entry % count
+    mine = count // 2
+    seat = pair // mine * count + pair % mine // 8 * 16 + side * 8 + pair % 8
+    seated = as_bf16(jnp.where(place(0, total) == seat, 1, 0))
+    parts = as_bf16(jnp.where(place(0, 8) == 0, where // 16, where % 16))
+    listed = dot_nt(parts, seated).astype(jnp.int32)
+    list_ref[...] = listed[0:1] * 16 + listed[1:2]
+
+
+def place_requests(pair_owner, pair_slot, owner_count, capacity):
+    count = pair_owner.shape[0]
+    return pl.pallas_call(
+        functools.partial(place_kernel, count, capacity),
+        out_shape=(
+            jax.ShapeDtypeStruct((owner_count, 1, capacity), jnp.int32),
+            jax.ShapeDtypeStruct((1, 2 * count), jnp.int32),
+        ),
+    )(pair_owner.T, pair_slot.T)
+
+
+def pick_kernel(core_ref, list_ref, returned_ref, picked_ref, sem):
+    count = picked_ref.shape[0]
+    start = (1 - core_ref[0]) * count
+
+    def begin(index, carry):
+        source = returned_ref.at[list_ref[0, start + index]]
+        pltpu.make_async_copy(source, picked_ref.at[index], sem).start()
+        return carry
+
+    lax.fori_loop(0, count, begin, 0, unroll=8)
+    pltpu.make_async_copy(returned_ref.at[pl.ds(0, count)], picked_ref, sem).wait()
 
 
 def on_device(
@@ -176,39 +234,53 @@
     def swap(values):
         return lax.ppermute(values, "mp", [(0, 1), (1, 0)])
 
-    where, wanted = place_requests(pair_owner, pair_slot, owner_count, capacity)
-    incoming = lax.all_to_all(wanted, "shard", split_axis=0, concat_axis=0, tiled=True)
-    weights = (w_qk, w_value, w_out, w_in, w_back, bias_in, logit_scale)
-    far_qk, far_value, far_out, far_in, far_back, far_bias, far_scale = [swap(w) for w in weights]
-    served = image_tokens[incoming]
-    returned = lax.all_to_all(served, "shard", split_axis=0, concat_axis=0, tiled=True)
-    returned = returned.reshape(owner_count * capacity, length, features)
-    order = where.reshape(2, mine // 8, 8, 2).transpose(0, 1, 3, 2).reshape(2, 2 * mine)
-    far = swap(returned[order[1 - core]])
-    own = returned[order[core]]
-
     smem = pl.BlockSpec(memory_space=pltpu.SMEM)
     vmem = pl.BlockSpec(memory_space=pltpu.VMEM)
+    hbm = pl.BlockSpec(memory_space=pl.ANY)
+
+    wanted, order = place_requests(pair_owner, pair_slot, owner_count, capacity)
+    incoming = lax.all_to_all(wanted, "shard", split_axis=0, concat_axis=0, tiled=True)
+    served = image_tokens[incoming.reshape(-1)]
+    served = served.reshape(owner_count, capacity, length, features)
+    weights = (w_qk, w_value, w_out, w_in, w_back, bias_in, logit_scale)
+    swapped = [swap(w) for w in weights]
+    returned = lax.all_to_all(served, "shard", split_axis=0, concat_axis=0, tiled=True)
+    returned, *swapped = lax.optimization_barrier((returned, *swapped))
+    far_qk, far_value, far_out, far_in, far_back, far_bias, far_scale = swapped
+    returned = returned.reshape(owner_count * capacity, length, features)
+    core = core.reshape(1)
+    picked = pl.pallas_call(
+        pick_kernel,
+        out_shape=jax.ShapeDtypeStruct((pair_count, length, features), jnp.bfloat16),
+        in_specs=[smem, smem, hbm],
+        out_specs=hbm,
+        scratch_shapes=[pltpu.SemaphoreType.DMA],
+    )(core, order, returned)
+    far = swap(picked)
+
     units = 2 * w_in.shape[1]
     flops = 4 * mine * length * width * (3 * width + units)
     features_here = pl.pallas_call(
         functools.partial(compare_kernel, length, head_dim),
         out_shape=jax.ShapeDtypeStruct((mine, width), jnp.bfloat16),
-        in_specs=[smem, smem] + [vmem] * 16,
+        in_specs=[smem, smem, smem, hbm] + [vmem] * 15,
         out_specs=vmem,
         scratch_shapes=[
+            pltpu.VMEM((pair_count, length, features), jnp.bfloat16),
             pltpu.VMEM((mine, units), jnp.float32),
             pltpu.VMEM((mine, width), jnp.float32),
+            pltpu.SemaphoreType.DMA((mine // 8,)),
         ],
         compiler_params=pltpu.CompilerParams(vmem_limit_bytes=48 * 2**20),
         cost_estimate=pl.CostEstimate(
             flops=flops, bytes_accessed=8 * 2**20, transcendentals=2 * mine * length * units
         ),
     )(
-        core.reshape(1),
+        core,
         jnp.concatenate([logit_scale, far_scale]),
-        own.reshape(-1, features),
-        far.reshape(-1, features),
+        order,
+        returned,
+        far,
         gain_attn.reshape(1, -1),
         w_qk,
         far_qk,

time: 100 us -> 112 us (1.12)
  Pallas kernels: 16.3 us -> 36 us
  local copies, waits for them, and re-layouts: 12.5 us -> 5.8 us
    pallas_call x0 -> x2, Pallas kernels: none -> 19.5 us  [the longest x1 17.7 us: on_device(): pl.pallas_call(pick_kernel, out_shape=jax.ShapeDtypeStruct((pair_count, l...]
    gather x3 -> x1, local copies, waits for them, and re-layouts: 7.23 us -> 2.06 us  [on_device(): served = image_tokens[incoming.reshape(-1)]]
    all_to_all x1, waiting for transfers between devices: 45.9 us -> 41.3 us  [on_device(): lax.all_to_all(served, 'shard', split_axis=0, concat_axis=0, tiled=True)]
    ppermute x9, waiting for transfers between devices: 2.75 us -> 7.11 us  [swap(): return lax.ppermute(values, 'mp', [(0, 1), (1, 0)])]
    unnamed x18 -> x22, local copies, waits for them, and re-layouts: 3.22 us -> 3.15 us
  transfers between devices with their start and end apart: 10 -> 10, of which waited for: 4 -> 7; matrix products, arithmetic and copies ran while one was open for 6% -> 0% of each run, Pallas kernels for 0% -> 0%
where the time goes in v2:
time: 112 us
  waiting for transfers between devices  48.4 us (43%)
  Pallas kernels  36 us (32%)
  blocking collectives  13.7 us (12%)
  starting transfers between devices  6.43 us (6%)
  local copies, waits for them, and re-layouts  5.8 us (5%)
  other arithmetic  1.4 us (1%)
    all_to_all x1, waiting for transfers between devices, on_device(): lax.all_to_all(served, 'shard', split_axis=0, concat_axis=0, tiled=True)  41.3 us
    pallas_call x1, Pallas kernels, on_device(): pl.pallas_call(pick_kernel, out_shape=jax.ShapeDtypeStruct((pair_count, l...  17.7 us
    pallas_call x1, Pallas kernels, on_device(): pl.pallas_call(functools.partial(compare_kernel, length, head_dim), out_s...  16.5 us
    all_to_all x1, blocking collectives, on_device(): lax.all_to_all(wanted, 'shard', split_axis=0, concat_axis=0, tiled=True)  13.7 us
    ppermute x9, waiting for transfers between devices, swap(): return lax.ppermute(values, 'mp', [(0, 1), (1, 0)])  7.11 us
    all_to_all x1, starting transfers between devices, on_device(): lax.all_to_all(served, 'shard', split_axis=0, concat_axis=0, tiled=True)  4.49 us
    unnamed x22, local copies, waits for them, and re-layouts  3.15 us
  transfers between devices with their start and end apart: 10, of which 7 were waited for; matrix products, arithmetic and copies ran while one was open for 0% of the time, Pallas kernels for 0%

profile of v2, /device:TPU:0, one launch (start us, length us, event | category | flops | bytes accessed | tf_op | source)
XLA Modules:
  0.0 111.9 jit_solution(10957131161255129000)
XLA Ops:
  0.0 1.8 %shard_map.118 = (s32[8,1,32]{2,1,0:T(1,128)}, s32[1,128]{1,0:T(1,128)}) custom-call(s32[2,64]{1,0:T(2,128)} %bitcast.17, s32[2,64]{1,0:T(2,128)} %bitcast.18), custom_call_target="tpu_custom_call" | custom-call | tf_op jit(solution)/shard_map/pallas_call | solution.py:189
  1.8 13.7 %all_to_all.10 = s32[8,1,32]{2,1,0:T(1,128)S(1)} all-to-all(s32[8,1,32]{2,1,0:T(1,128)} %get-tuple-element.15), channel_id=1, replica_groups=mesh['groups'=2,'shard'=8,'mp'=2] {'shard'}, dimensions={0} | all-to-all | bytes 2048 | tf_op jit(solution)/shard_map/all_to_all | solution.py:242
  15.5 0.5 broadcast.24
  16.0 0.7 reduce.3
  16.7 2.1 %gather_fusion = bf16[256,16,256]{2,1,0:T(8,128)(2,1)} fusion(bf16[256,16,256]{2,1,0:T(8,128)(2,1)S(1)} %copy-done, s32[1024]{0:T(1024)S(1)} %pad_clamp_fusion), kind=kCustom, calls=%fused_computation | custom fusion | bytes 4195328 | tf_op jit(solution)/shard_map/gather | solution.py:243
  18.8 4.5 %all-to-all-start.1 = ((bf16[8,32,16,256]{3,2,1,0:T(8,128)(2,1)}), bf16[8,32,16,256]{3,2,1,0:T(8,128)(2,1)}, u32[]{:S(2)}, u32[]{:S(2)}) async-start(bf16[8,32,16,256]{3,2,1,0:T(8,128)(2,1)} %bitcast.15), calls=%async_computation.1 | async-start | bytes 4194304 | tf_op jit(solution)/shard_map/all_to_all | solution.py:247
  23.4 0.5 collective-permute-start.4
  24.0 0.4 collective-permute-start
  24.5 2.3 %collective-permute-done.6 = f32[4]{0:T(128)S(1)} collective-permute-done((f32[4]{0:T(128)S(1)}, f32[4]{0:T(128)S(1)}, u32[]{:S(2)}, u32[]{:S(2)}) %collective-permute-start.6) | collective-permute-done | bytes 48 | tf_op jit(solution)/shard_map/ppermute | solution.py:235
  26.8 0.1 collective-permute-start.1
  26.9 0.4 collective-permute-start.2
  27.3 0.4 collective-permute-done.qk_b_ref
  27.7 1.0 collective-permute-done.1.value_b_ref
  28.7 0.4 collective-permute-done.2.out_b_ref
  29.1 41.3 %all-to-all-done.1 = bf16[8,32,16,256]{3,2,1,0:T(8,128)(2,1)} async-done(((bf16[8,32,16,256]{3,2,1,0:T(8,128)(2,1)}), bf16[8,32,16,256]{3,2,1,0:T(8,128)(2,1)}, u32[]{:S(2)}, u32[]{:S(2)}) %all-to-all-start.1) | async-done | bytes 2097184 | tf_op jit(solution)/shard_map/all_to_all | solution.py:247
  70.4 17.7 %shard_map.119 = bf16[64,16,256]{2,1,0:T(8,128)(2,1)} custom-call(s32[1]{0:T(128)} %bitcast.core_ref, s32[1,128]{1,0:T(1,128)} %get-tuple-element.17.list_ref, bf16[256,16,256]{2,1,0:T(8,128)(2,1)} %bitcast.6.returned_ref), custom_call_target="tpu_custom_call" | custom-call | tf_op jit(solution)/shard_map/pallas_call | solution.py:252
  88.2 2.0 %collective-permute-done.7.far_ref = bf16[64,16,256]{2,1,0:T(8,128)(2,1)S(1)} collective-permute-done((bf16[64,16,256]{2,1,0:T(8,128)(2,1)}, bf16[64,16,256]{2,1,0:T(8,128)(2,1)S(1)}, u32[]{:S(2)}, u32[]{:S(2)}) %collective-permute-start.7) | collective-permute-done | bytes 524320 | tf_op jit(solution)/shard_map/ppermute | solution.py:235
  90.3 1.2 %copy-done.3 = bf16[1024,512]{1,0:T(8,128)(2,1)S(1)} copy-done((bf16[1024,512]{1,0:T(8,128)(2,1)S(1)}, bf16[1024,512]{1,0:T(8,128)(2,1)}, u32[]{:S(2)}) %copy-start.3) | copy-done | bytes 1048600
  91.5 0.9 copy-done.5
  92.4 0.9 copy-done.6
  93.4 16.5 %shard_map.120 = bf16[32,512]{1,0:T(8,128)(2,1)S(1)} custom-call(s32[1]{0:T(128)} %bitcast.core_ref, f32[8]{0:T(128)S(1)} %pad_maximum_fusion.1.scale_ref, s32[1,128]{1,0:T(1,128)S(1)} %copy-done.1, bf16[256,16,256]{2,1,0:T(8,128)(2,1)} %bitcast.6.returned_ref, bf16[64,16,256]{2,1,0:T(8,128)(2,1)S(1)} %collective-permute-done.7.far_ref, ...), custom_call_target="tpu_custom_call" | custom-call | flops 3758096384 | bytes 8388608 | tf_op jit(solution)/shard_map/pallas_call | solution.py:263
  109.9 0.2 collective-permute-start.8
  110.1 1.1 collective-permute-done.8
  111.2 0.6 pad_maximum_fusion
  (31 shorter events, 0.5 us)
Async XLA Ops:
  0.0 16.7 %copy-start = (bf16[256,16,256]{2,1,0:T(8,128)(2,1)S(1)}, bf16[256,16,256]{2,1,0:T(8,128)(2,1)}, u32[]{:S(2)}) copy-start(bf16[256,16,256]{2,1,0:T(8,128)(2,1)} %param.12) | copy-start | bytes 6291460
  18.8 4.5 %copy-start.2 = (bf16[512,1024]{1,0:T(8,128)(2,1)S(1)}, bf16[512,1024]{1,0:T(8,128)(2,1)}, u32[]{:S(2)}) copy-start(bf16[512,1024]{1,0:T(8,128)(2,1)} %in_a_ref.1) | copy-start | bytes 3145732
  18.8 5.1 %copy-start.7 = (f32[1024]{0:T(1024)S(1)}, f32[1024]{0:T(1024)}, u32[]{:S(2)}) copy-start(f32[1024]{0:T(1024)} %param.22) | copy-start | bytes 12292
  18.8 5.2 %copy-start.4 = (bf16[512,256]{1,0:T(8,128)(2,1)S(1)}, bf16[512,256]{1,0:T(8,128)(2,1)}, u32[]{:S(2)}) copy-start(bf16[512,256]{1,0:T(8,128)(2,1)} %qk_a_ref.1) | copy-start | bytes 786436
  18.8 5.6 %copy-start.10 = (f32[4]{0:T(128)S(1)}, f32[4]{0:T(128)}, u32[]{:S(2)}) copy-start(f32[4]{0:T(128)} %param.18) | copy-start | bytes 52
  18.8 51.6 %all-to-all-start.1 = ((bf16[8,32,16,256]{3,2,1,0:T(8,128)(2,1)}), bf16[8,32,16,256]{3,2,1,0:T(8,128)(2,1)}, u32[]{:S(2)}, u32[]{:S(2)}) async-start(bf16[8,32,16,256]{3,2,1,0:T(8,128)(2,1)} %bitcast.15), calls=%async_computation.1 | async-start | bytes 4194304 | tf_op jit(solution)/shard_map/all_to_all | solution.py:247
  23.3 66.9 %copy-start.1 = (s32[1,128]{1,0:T(1,128)S(1)}, s32[1,128]{1,0:T(1,128)}, u32[]{:S(2)}) copy-start(s32[1,128]{1,0:T(1,128)} %get-tuple-element.17.list_ref) | copy-start | bytes 1540
  23.3 66.9 %copy-start.8 = (f32[512]{0:T(512)S(1)}, f32[512]{0:T(512)}, u32[]{:S(2)}) copy-start(f32[512]{0:T(512)} %param.15) | copy-start | bytes 6148
  23.3 66.9 %copy-start.9 = (f32[512]{0:T(512)S(1)}, f32[512]{0:T(512)}, u32[]{:S(2)}) copy-start(f32[512]{0:T(512)} %param.20) | copy-start | bytes 6148
  23.3 5.7 %collective-permute-start.3 = (bf16[512,1024]{1,0:T(8,128)(2,1)S(1)}, bf16[512,1024]{1,0:T(8,128)(2,1)}, u32[]{:S(2)}, u32[]{:S(2)}) collective-permute-start(bf16[512,1024]{1,0:T(8,128)(2,1)S(1)} %copy-done.2), channel_id=1, source_target_pairs={{0,1},{1,0},{2,3},{3,2},{4,5},{5,4},{6,7},{7,6},{8,9},{9,8},{10,11... | collective-permute-start | bytes 3145736 | tf_op jit(solution)/shard_map/ppermute | solution.py:235
  23.4 5.6 %collective-permute-start.4 = (bf16[1024,512]{1,0:T(8,128)(2,1)}, bf16[1024,512]{1,0:T(8,128)(2,1)}, u32[]{:S(2)}, u32[]{:S(2)}) collective-permute-start(bf16[1024,512]{1,0:T(8,128)(2,1)} %back_a_ref.1), channel_id=1, source_target_pairs={{0,1},{1,0},{2,3},{3,2},{4,5},{5,4},{6,7},{7,6},{8,9},{9,8},{10,11... | collective-permute-start | bytes 3145736 | tf_op jit(solution)/shard_map/ppermute | solution.py:235
  23.9 3.0 %collective-permute-start.5 = (f32[1024]{0:T(1024)S(1)}, f32[1024]{0:T(1024)S(1)}, u32[]{:S(2)}, u32[]{:S(2)}) collective-permute-start(f32[1024]{0:T(1024)S(1)} %copy-done.7), channel_id=1, source_target_pairs={{0,1},{1,0},{2,3},{3,2},{4,5},{5,4},{6,7},{7,6},{8,9},{9,8},{10,11... | collective-permute-start | bytes 12296 | tf_op jit(solution)/shard_map/ppermute | solution.py:235
  24.0 3.7 %collective-permute-start = (bf16[512,256]{1,0:T(8,128)(2,1)S(1)}, bf16[512,256]{1,0:T(8,128)(2,1)}, u32[]{:S(2)}, u32[]{:S(2)}) collective-permute-start(bf16[512,256]{1,0:T(8,128)(2,1)S(1)} %copy-done.4), channel_id=1, source_target_pairs={{0,1},{1,0},{2,3},{3,2},{4,5},{5,4},{6,7},{7,6},{8,9},{9,8},{10,11... | collective-permute-start | bytes 786440 | tf_op jit(solution)/shard_map/ppermute | solution.py:235
  24.4 2.3 %collective-permute-start.6 = (f32[4]{0:T(128)S(1)}, f32[4]{0:T(128)S(1)}, u32[]{:S(2)}, u32[]{:S(2)}) collective-permute-start(f32[4]{0:T(128)S(1)} %copy-done.10), channel_id=1, source_target_pairs={{0,1},{1,0},{2,3},{3,2},{4,5},{5,4},{6,7},{7,6},{8,9},{9,8},{10,11... | collective-permute-start | bytes 56 | tf_op jit(solution)/shard_map/ppermute | solution.py:235
  26.8 1.9 %collective-permute-start.1 = (bf16[512,256]{1,0:T(8,128)(2,1)}, bf16[512,256]{1,0:T(8,128)(2,1)}, u32[]{:S(2)}, u32[]{:S(2)}) collective-permute-start(bf16[512,256]{1,0:T(8,128)(2,1)} %value_a_ref.1), channel_id=1, source_target_pairs={{0,1},{1,0},{2,3},{3,2},{4,5},{5,4},{6,7},{7,6},{8,9},{9,8},{10,11... | collective-permute-start | bytes 786440 | tf_op jit(solution)/shard_map/ppermute | solution.py:235
  26.9 2.1 %collective-permute-start.2 = (bf16[256,512]{1,0:T(8,128)(2,1)}, bf16[256,512]{1,0:T(8,128)(2,1)}, u32[]{:S(2)}, u32[]{:S(2)}) collective-permute-start(bf16[256,512]{1,0:T(8,128)(2,1)} %out_a_ref.1), channel_id=1, source_target_pairs={{0,1},{1,0},{2,3},{3,2},{4,5},{5,4},{6,7},{7,6},{8,9},{9,8},{10,11... | collective-permute-start | bytes 786440 | tf_op jit(solution)/shard_map/ppermute | solution.py:235
  88.1 2.2 %collective-permute-start.7 = (bf16[64,16,256]{2,1,0:T(8,128)(2,1)}, bf16[64,16,256]{2,1,0:T(8,128)(2,1)S(1)}, u32[]{:S(2)}, u32[]{:S(2)}) collective-permute-start(bf16[64,16,256]{2,1,0:T(8,128)(2,1)} %shard_map.119), channel_id=1, source_target_pairs={{0,1},{1,0},{2,3},{3,2},{4,5},{5,4},{6,7},{7,6},{8,9},{9,8},{10,11... | collective-permute-start | bytes 1572872 | tf_op jit(solution)/shard_map/ppermute | solution.py:235
  90.3 1.2 %copy-start.3 = (bf16[1024,512]{1,0:T(8,128)(2,1)S(1)}, bf16[1024,512]{1,0:T(8,128)(2,1)}, u32[]{:S(2)}) copy-start(bf16[1024,512]{1,0:T(8,128)(2,1)} %back_a_ref.1) | copy-start | bytes 3145732
  91.5 0.9 copy-start.5
  92.4 0.9 copy-start.6
  109.9 1.3 %collective-permute-start.8 = (bf16[32,512]{1,0:T(8,128)(2,1)S(1)}, bf16[32,512]{1,0:T(8,128)(2,1)S(1)}, u32[]{:S(2)}, u32[]{:S(2)}) collective-permute-start(bf16[32,512]{1,0:T(8,128)(2,1)S(1)} %shard_map.120), channel_id=1, source_target_pairs={{0,1},{1,0},{2,3},{3,2},{4,5},{5,4},{6,7},{7,6},{8,9},{9,8},{10,11... | collective-permute-start | bytes 98312 | tf_op jit(solution)/shard_map/ppermute | solution.py:235

commit v3 on v2

--- a/solution.py
+++ b/solution.py
@@ -25,46 +25,46 @@
 
 
 def compare_kernel(
+    plan,
     length,
     head_dim,
     core_ref,
     scale_ref,
     list_ref,
-    returned_ref,
     far_ref,
     gain_attn_ref,
-    qk_a_ref,
-    qk_b_ref,
-    value_a_ref,
-    value_b_ref,
-    out_a_ref,
-    out_b_ref,
     gain_mlp_ref,
-    in_a_ref,
-    in_b_ref,
     bias_a_ref,
     bias_b_ref,
-    back_a_ref,
-    back_b_ref,
-    result_ref,
-    own_ref,
-    pooled_ref,
-    hidden_ref,
-    sems,
+    *refs,
 ):
+    held_refs, source_refs = refs[:10], refs[10:-16]
+    result_ref = refs[-16]
+    matrix_refs = refs[-15:-5]
+    own_ref, pooled_ref, hidden_ref, sems, matrix_sems = refs[-5:]
+    loads = [
+        pltpu.make_async_copy(held, ref, matrix_sems.at[k])
+        for k, (held, ref) in enumerate(zip(held_refs, matrix_refs))
+    ]
+    start = core_ref[0] * own_ref.shape[0]
+
+    def begin(index, carry):
+        where = list_ref[0, start + index]
+        fetch(plan, where, source_refs, own_ref.at[index], sems.at[index // 16])
+        return carry
+
+    for load in loads[:4]:
+        load.start()
+    lax.fori_loop(0, own_ref.shape[0], begin, 0, unroll=4)
+    for load in loads[4:]:
+        load.start()
+    qk_a_ref, qk_b_ref, value_a_ref, value_b_ref, out_a_ref, out_b_ref = matrix_refs[:6]
+    in_a_ref, in_b_ref, back_a_ref, back_b_ref = matrix_refs[6:]
     half = 8 * length
     rows = 2 * half
     blocks = own_ref.shape[0] // 16
     pair_dim = 2 * head_dim
     first = core_ref[0] == 0
-    start = core_ref[0] * own_ref.shape[0]
-
-    def begin(index, carry):
-        source = returned_ref.at[list_ref[0, start + index]]
-        pltpu.make_async_copy(source, own_ref.at[index], sems.at[index // 16]).start()
-        return carry
-
-    lax.fori_loop(0, own_ref.shape[0], begin, 0, unroll=8)
     lane = lax.broadcasted_iota(jnp.int32, (half, pair_dim), 1)
     even = lane < head_dim
     same = (
@@ -84,10 +84,16 @@
         weights = jnp.exp2((scores - top) * factor)
         return (weights * (1.0 / jnp.sum(weights, axis=1, keepdims=True))).astype(jnp.bfloat16)
 
+    def arrive(step, copies):
+        @pl.when(step == 0)
+        def _():
+            for copy in copies:
+                copy.wait()
+
     def block(step, carry):
         span = pl.ds(pl.multiple_of(step * 16, 16), 16)
         pltpu.make_async_copy(
-            returned_ref.at[pl.ds(0, 16)], own_ref.at[span], sems.at[step]
+            source_refs[0].at[pl.ds(0, 16)], own_ref.at[span], sems.at[step]
         ).wait()
         own = own_ref[span].reshape(rows, -1).astype(jnp.float32)
         far = far_ref[span].reshape(rows, -1).astype(jnp.float32)
@@ -95,6 +101,7 @@
             [jnp.where(first, own, far), jnp.where(first, far, own)], axis=1
         )
         normed = norm_rows(tokens, gain_attn_ref[...]).astype(jnp.bfloat16)
+        arrive(step, loads[:6])
         hidden = tokens
         head = 0
         for qk_ref, value_ref, out_ref in (
@@ -125,6 +132,7 @@
         at = pl.ds(pl.multiple_of(step * 8, 8), 8)
         hidden_ref[at, :] = jnp.sum(hidden.reshape(2, 8, length, -1), axis=(0, 2))
         normed = norm_rows(hidden, gain_mlp_ref[...]).astype(jnp.bfloat16)
+        arrive(step, loads[6:8])
         offset = 0
         for in_ref, bias_ref in ((in_a_ref, bias_a_ref), (in_b_ref, bias_b_ref)):
             units = in_ref.shape[1]
@@ -141,6 +149,7 @@
         return carry
 
     lax.fori_loop(0, blocks, block, 0)
+    arrive(0, loads[8:])
     pooled = pooled_ref[...] * (0.25 / length)
     coarse = pooled.astype(jnp.bfloat16)
     fine = (pooled - coarse.astype(jnp.float32)).astype(jnp.bfloat16)
@@ -152,9 +161,24 @@
     result_ref[...] = (mean + back[:count] + back[count:]).astype(jnp.bfloat16)
 
 
-def place_kernel(count, capacity, owner_ref, slot_ref, wanted_ref, list_ref):
-    owners = wanted_ref.shape[0]
+class Plan:
+    def __init__(self, pair_count, owner_count):
+        self.owners = owner_count
+        self.capacity = max(2, 4 * pair_count // owner_count)
+        self.half = owner_count // 2
+        split = self.capacity >= 32 and self.half & (self.half - 1) == 0 and self.half > 0
+        self.base = self.capacity // 2 if split else self.capacity
+        self.extra = self.capacity - self.base
+        self.chunk = 2 * self.extra
+        self.part = self.half * self.extra // 2
+        self.near_at = owner_count * self.base
+        self.far_at = self.near_at + self.half * self.chunk
+        self.row = self.capacity + (self.half if split else 0)
+
+
+def place_kernel(plan, count, shard_ref, owner_ref, slot_ref, wanted_ref, list_ref):
     total = 2 * count
+    owners = plan.owners
     owner = jnp.concatenate([owner_ref[0:1, :], owner_ref[1:2, :]], axis=1)
     slot = jnp.concatenate([slot_ref[0:1, :], slot_ref[1:2, :]], axis=1)
 
@@ -170,9 +194,25 @@
     rank = jnp.sum(jnp.where(named, tally, 0), axis=0, keepdims=True) - 1
     ranked = as_bf16(jnp.where(place(0, total) == rank, 1, 0))
     wanted = dot_nt(as_bf16(jnp.where(named, slot, 0)), ranked).astype(jnp.int32)
+    where = owner * plan.base + rank
+    if plan.extra:
+        me = shard_ref[0]
+        half = plan.half
+        over = jnp.maximum(jnp.max(tally, axis=1, keepdims=True) - plan.base, 0)
+        row = place(0, owners)
+        far_over = jnp.where(row // half != me // half, over, 0)
+        before = jnp.zeros((owners, total), jnp.int32)
+        for index in range(owners - 1):
+            before = before + jnp.where(row > index, far_over[index : index + 1], 0)
+        before = jnp.sum(jnp.where(named, before, 0), axis=0, keepdims=True)
+        rest = rank - plan.base
+        near = plan.near_at + ((owner % half) ^ (me % half)) * plan.chunk + rest
+        late = jnp.where(owner // half == me // half, near, plan.far_at + before + rest)
+        where = jnp.where(rest < 0, where, late)
+        told = place(1, owners) == plan.capacity + row % half
+        wanted = wanted + jnp.sum(jnp.where(told, far_over, 0), axis=0, keepdims=True)
     for index in range(owners):
-        wanted_ref[index] = wanted[index : index + 1, :capacity]
-    where = owner * capacity + rank
+        wanted_ref[index] = wanted[index : index + 1, : plan.row]
     entry = place(1, 1)
     side = entry // count
     pair = entry % count
@@ -184,28 +224,94 @@
     list_ref[...] = listed[0:1] * 16 + listed[1:2]
 
 
-def place_requests(pair_owner, pair_slot, owner_count, capacity):
-    count = pair_owner.shape[0]
-    return pl.pallas_call(
-        functools.partial(place_kernel, count, capacity),
-        out_shape=(
-            jax.ShapeDtypeStruct((owner_count, 1, capacity), jnp.int32),
-            jax.ShapeDtypeStruct((1, 2 * count), jnp.int32),
-        ),
-    )(pair_owner.T, pair_slot.T)
-
-
-def pick_kernel(core_ref, list_ref, returned_ref, picked_ref, sem):
+def serve_base_kernel(plan, incoming_ref, tokens_ref, served_ref):
+    for requester in range(plan.owners):
+
+        def copy(index, carry):
+            served_ref[requester, index] = tokens_ref[incoming_ref[requester, 0, index]]
+            return carry
+
+        lax.fori_loop(0, plan.base, copy, 0, unroll=min(16, plan.base))
+
+
+def serve_rest_kernel(plan, shard_ref, incoming_ref, tokens_ref, *chunk_refs):
+    me = shard_ref[0]
+    side = me // plan.half
+    for distance, chunk_ref in enumerate(chunk_refs):
+        peer = (me % plan.half) ^ distance
+        for part in range(2):
+            requester = (side ^ part) * plan.half + peer
+
+            def copy(index, carry):
+                slot = incoming_ref[requester, 0, plan.base + index]
+                chunk_ref[part * plan.extra + index] = tokens_ref[slot]
+                return carry
+
+            lax.fori_loop(0, plan.extra, copy, 0, unroll=16)
+
+
+def relay_kernel(plan, shard_ref, incoming_ref, *refs):
+    chunk_refs = refs[: plan.half]
+    first_ref, second_ref, sem = refs[plan.half :]
+    me = shard_ref[0]
+    client = me ^ plan.half
+    position = 0
+    for owner in range(plan.half):
+        amount = incoming_ref[client, 0, plan.capacity + owner]
+        for distance, chunk_ref in enumerate(chunk_refs):
+
+            @pl.when((me % plan.half) ^ distance == owner)
+            def _():
+                def begin(index, carry):
+                    source = chunk_ref.at[plan.extra + index]
+                    at = position + index
+
+                    @pl.when(at < plan.part)
+                    def _():
+                        pltpu.make_async_copy(source, first_ref.at[at], sem).start()
+
+                    @pl.when(at >= plan.part)
+                    def _():
+                        pltpu.make_async_copy(source, second_ref.at[at - plan.part], sem).start()
+
+                    return carry
+
+                lax.fori_loop(0, amount, begin, 0)
+
+        position = position + amount
+
+    def finish(index, carry):
+        pltpu.make_async_copy(chunk_refs[0].at[0], first_ref.at[0], sem).wait()
+        return carry
+
+    lax.fori_loop(0, position, finish, 0)
+
+
+def fetch(plan, where, source_refs, target_ref, sem):
+    if not plan.extra:
+        pltpu.make_async_copy(source_refs[0].at[where], target_ref, sem).start()
+        return
+    starts = [0] + [plan.near_at + k * plan.chunk for k in range(plan.half)]
+    starts += [plan.far_at, plan.far_at + plan.part, plan.far_at + 2 * plan.part]
+    for ref, low, high in zip(source_refs, starts[:-1], starts[1:]):
+
+        @pl.when((where >= low) & (where < high))
+        def _():
+            pltpu.make_async_copy(ref.at[where - low], target_ref, sem).start()
+
+
+def pick_kernel(plan, core_ref, list_ref, *refs):
+    source_refs = refs[:-2]
+    picked_ref, sem = refs[-2:]
     count = picked_ref.shape[0]
     start = (1 - core_ref[0]) * count
 
     def begin(index, carry):
-        source = returned_ref.at[list_ref[0, start + index]]
-        pltpu.make_async_copy(source, picked_ref.at[index], sem).start()
+        fetch(plan, list_ref[0, start + index], source_refs, picked_ref.at[index], sem)
         return carry
 
-    lax.fori_loop(0, count, begin, 0, unroll=8)
-    pltpu.make_async_copy(returned_ref.at[pl.ds(0, count)], picked_ref, sem).wait()
+    lax.fori_loop(0, count, begin, 0, unroll=4)
+    pltpu.make_async_copy(source_refs[0].at[pl.ds(0, count)], picked_ref, sem).wait()
 
 
 def on_device(
@@ -223,55 +329,102 @@
     w_back,
 ):
     owner_count = lax.axis_size("shard")
+    groups = lax.axis_size("groups")
     core = lax.axis_index("mp")
+    shard = lax.axis_index("shard").reshape(1)
     pair_count = pair_owner.shape[0]
     _, length, features = image_tokens.shape
     width = 2 * features
     head_dim = w_qk.shape[1] // logit_scale.shape[0]
-    capacity = max(2, 4 * pair_count // owner_count)
     mine = pair_count // 2
+    plan = Plan(pair_count, owner_count)
 
     def swap(values):
         return lax.ppermute(values, "mp", [(0, 1), (1, 0)])
+
+    def across(values, distance):
+        return lax.ppermute(values, "shard", [(k, k ^ distance) for k in range(owner_count)])
+
+    def images(count):
+        return jax.ShapeDtypeStruct((count, length, features), jnp.bfloat16)
 
     smem = pl.BlockSpec(memory_space=pltpu.SMEM)
     vmem = pl.BlockSpec(memory_space=pltpu.VMEM)
     hbm = pl.BlockSpec(memory_space=pl.ANY)
 
-    wanted, order = place_requests(pair_owner, pair_slot, owner_count, capacity)
+    wanted, order = pl.pallas_call(
+        functools.partial(place_kernel, plan, pair_count),
+        out_shape=(
+            jax.ShapeDtypeStruct((owner_count, 1, plan.row), jnp.int32),
+            jax.ShapeDtypeStruct((1, 2 * pair_count), jnp.int32),
+        ),
+        in_specs=[smem, vmem, vmem],
+    )(shard, pair_owner.T, pair_slot.T)
     incoming = lax.all_to_all(wanted, "shard", split_axis=0, concat_axis=0, tiled=True)
-    served = image_tokens[incoming.reshape(-1)]
-    served = served.reshape(owner_count, capacity, length, features)
+    served = pl.pallas_call(
+        functools.partial(serve_base_kernel, plan),
+        out_shape=jax.ShapeDtypeStruct(
+            (owner_count, plan.base, length, features), jnp.bfloat16
+        ),
+        in_specs=[smem, vmem],
+    )(incoming, image_tokens)
+    returned = lax.all_to_all(served, "shard", split_axis=0, concat_axis=0, tiled=True)
+    returned = returned.reshape(-1, length, features)
+    sources = [returned]
+    if plan.extra:
+        chunks = pl.pallas_call(
+            functools.partial(serve_rest_kernel, plan),
+            out_shape=[images(plan.chunk)] * plan.half,
+            in_specs=[smem, smem, vmem],
+        )(shard, incoming, image_tokens)
+        chunks = [chunks[0]] + [across(chunks[k], k) for k in range(1, plan.half)]
+        first, second = pl.pallas_call(
+            functools.partial(relay_kernel, plan),
+            out_shape=[images(plan.part)] * 2,
+            in_specs=[smem, smem] + [hbm] * plan.half,
+            scratch_shapes=[pltpu.SemaphoreType.DMA],
+        )(shard, incoming, *chunks)
+        first = across(first, plan.half)
+        crowded = jnp.max(jnp.sum(incoming[:, 0, plan.capacity :], axis=1)) > plan.part
+        crowded = crowded.astype(jnp.int32)
+        passed = crowded
+        for _ in range(groups - 1):
+            passed = lax.ppermute(passed, "groups", [(k, (k + 1) % groups) for k in range(groups)])
+            crowded = jnp.maximum(crowded, passed)
+        second = lax.cond(
+            crowded > 0, lambda part: across(part, plan.half), lambda part: part, second
+        )
+        sources += [*chunks, first, second]
     weights = (w_qk, w_value, w_out, w_in, w_back, bias_in, logit_scale)
     swapped = [swap(w) for w in weights]
-    returned = lax.all_to_all(served, "shard", split_axis=0, concat_axis=0, tiled=True)
-    returned, *swapped = lax.optimization_barrier((returned, *swapped))
+    sources, swapped = lax.optimization_barrier((sources, swapped))
     far_qk, far_value, far_out, far_in, far_back, far_bias, far_scale = swapped
-    returned = returned.reshape(owner_count * capacity, length, features)
     core = core.reshape(1)
     picked = pl.pallas_call(
-        pick_kernel,
-        out_shape=jax.ShapeDtypeStruct((pair_count, length, features), jnp.bfloat16),
-        in_specs=[smem, smem, hbm],
-        out_specs=hbm,
+        functools.partial(pick_kernel, plan),
+        out_shape=images(pair_count),
+        in_specs=[smem, smem] + [hbm] * len(sources),
         scratch_shapes=[pltpu.SemaphoreType.DMA],
-    )(core, order, returned)
+    )(core, order, *sources)
     far = swap(picked)
 
     units = 2 * w_in.shape[1]
     flops = 4 * mine * length * width * (3 * width + units)
+    matrices = [w_qk, far_qk, w_value, far_value, w_out, far_out, w_in, far_in, w_back, far_back]
     features_here = pl.pallas_call(
-        functools.partial(compare_kernel, length, head_dim),
+        functools.partial(compare_kernel, plan, length, head_dim),
         out_shape=jax.ShapeDtypeStruct((mine, width), jnp.bfloat16),
-        in_specs=[smem, smem, smem, hbm] + [vmem] * 15,
+        in_specs=[smem] * 3 + [vmem] * 5 + [hbm] * (10 + len(sources)),
         out_specs=vmem,
-        scratch_shapes=[
+        scratch_shapes=[pltpu.VMEM(m.shape, m.dtype) for m in matrices]
+        + [
             pltpu.VMEM((pair_count, length, features), jnp.bfloat16),
             pltpu.VMEM((mine, units), jnp.float32),
             pltpu.VMEM((mine, width), jnp.float32),
             pltpu.SemaphoreType.DMA((mine // 8,)),
+            pltpu.SemaphoreType.DMA((10,)),
         ],
-        compiler_params=pltpu.CompilerParams(vmem_limit_bytes=48 * 2**20),
+        compiler_params=pltpu.CompilerParams(vmem_limit_bytes=32 * 2**20),
         cost_estimate=pl.CostEstimate(
             flops=flops, bytes_accessed=8 * 2**20, transcendentals=2 * mine * length * units
         ),
@@ -279,22 +432,13 @@
         core,
         jnp.concatenate([logit_scale, far_scale]),
         order,
-        returned,
         far,
         gain_attn.reshape(1, -1),
-        w_qk,
-        far_qk,
-        w_value,
-        far_value,
-        w_out,
-        far_out,
         gain_mlp.reshape(1, -1),
-        w_in,
-        far_in,
         bias_in.reshape(1, -1),
         far_bias.reshape(1, -1),
-        w_back,
-        far_back,
+        *matrices,
+        *sources,
     )
     features_there = swap(features_here)
     low = jnp.where(core == 0, features_here, features_there)

time: 112 us -> 105 us (0.938)
  waiting for transfers between devices: 48.4 us -> 35.4 us
  starting transfers between devices: 6.43 us -> 13.7 us
  Pallas kernels: 36 us -> 32 us
  between operations: 0.12 us -> 1.59 us
    all_to_all x1, waiting for transfers between devices: 41.3 us -> 0.01 us  [on_device(): lax.all_to_all(served, 'shard', split_axis=0, concat_axis=0, tiled=True)]
    ppermute x0 -> x5, waiting for transfers between devices: none -> 31.2 us  [the longest x4 30.5 us: across(): lax.ppermute(values, 'shard', [(k, k ^ distance) for k in range(owner_cou...]
    ppermute x0 -> x5, starting transfers between devices: none -> 8.57 us  [the longest x4 5.72 us: across(): lax.ppermute(values, 'shard', [(k, k ^ distance) for k in range(owner_cou...]
    pallas_call x3 -> x6, Pallas kernels: 36 us -> 32 us  [the longest x1 18.9 us: on_device(): pl.pallas_call(functools.partial(compare_kernel, plan, length, head_dim),...]
    unnamed x22 -> x44, local copies, waits for them, and re-layouts: 3.15 us -> 6.84 us
    ppermute x9, waiting for transfers between devices: 7.11 us -> 4.24 us  [swap(): return lax.ppermute(values, 'mp', [(0, 1), (1, 0)])]
    gather x1 -> x0, local copies, waits for them, and re-layouts: 2.06 us -> none  [on_device(): served = image_tokens[incoming.reshape(-1)]]
  transfers between devices with their start and end apart: 10 -> 15, of which waited for: 7 -> 8; matrix products, arithmetic and copies ran while one was open for 0% -> 1% of each run, Pallas kernels for 0% -> 5%
where the time goes in v3:
time: 105 us
  waiting for transfers between devices  35.4 us (34%)
  Pallas kernels  32 us (30%)
  starting transfers between devices  13.7 us (13%)
  blocking collectives  13.6 us (13%)
  local copies, waits for them, and re-layouts  6.84 us (7%)
  other arithmetic  1.67 us (2%)
  between operations  1.59 us (2%)
    ppermute x4, waiting for transfers between devices, across(): lax.ppermute(values, 'shard', [(k, k ^ distance) for k in range(owner_cou...  30.5 us
    pallas_call x1, Pallas kernels, on_device(): pl.pallas_call(functools.partial(compare_kernel, plan, length, head_dim),...  18.9 us
    all_to_all x1, blocking collectives, on_device(): lax.all_to_all(wanted, 'shard', split_axis=0, concat_axis=0, tiled=True)  13.6 us
    unnamed x44, local copies, waits for them, and re-layouts  6.84 us
    ppermute x4, starting transfers between devices, across(): lax.ppermute(values, 'shard', [(k, k ^ distance) for k in range(owner_cou...  5.72 us
    ppermute x9, waiting for transfers between devices, swap(): return lax.ppermute(values, 'mp', [(0, 1), (1, 0)])  4.24 us
    all_to_all x1, starting transfers between devices, on_device(): lax.all_to_all(served, 'shard', split_axis=0, concat_axis=0, tiled=True)  3.69 us
    pallas_call x1, Pallas kernels, on_device(): pl.pallas_call(functools.partial(pick_kernel, plan), out_shape=images(pai...  3.26 us
  transfers between devices with their start and end apart: 15, of which 8 were waited for; matrix products, arithmetic and copies ran while one was open for 1% of the time, Pallas kernels for 5%

profile of v3, /device:TPU:0, one launch (start us, length us, event | category | flops | bytes accessed | tf_op | source)
XLA Modules:
  0.0 104.9 jit_solution(3605610402966529803)
XLA Ops:
  0.0 1.8 %shard_map.118 = (s32[8,1,36]{2,1,0:T(1,128)}, s32[1,128]{1,0:T(1,128)}) custom-call(s32[1]{0:T(128)} %bitcast.2.shard_ref, s32[2,64]{1,0:T(2,128)} %bitcast.16, s32[2,64]{1,0:T(2,128)} %bitcast.17), custom_call_target="tpu_custom_call" | custom-call | tf_op jit(solution)/shard_map/pallas_call | solution.py:355
  1.8 13.6 %all_to_all.10.incoming_ref = s32[8,1,36]{2,1,0:T(1,128)} all-to-all(s32[8,1,36]{2,1,0:T(1,128)} %get-tuple-element.32), channel_id=1, replica_groups=mesh['groups'=2,'shard'=8,'mp'=2] {'shard'}, dimensions={0} | all-to-all | bytes 2304 | tf_op jit(solution)/shard_map/all_to_all | solution.py:363
  15.4 2.8 %shard_map.119 = bf16[8,16,16,256]{3,2,1,0:T(8,128)(2,1)} custom-call(s32[8,1,36]{2,1,0:T(1,128)} %all_to_all.10.incoming_ref, bf16[256,16,256]{2,1,0:T(8,128)(2,1)} %tokens_ref.3), custom_call_target="tpu_custom_call" | custom-call | tf_op jit(solution)/shard_map/pallas_call | solution.py:364
  18.2 3.7 %all-to-all-start.1 = ((bf16[8,16,16,256]{3,2,1,0:T(8,128)(2,1)}), bf16[8,16,16,256]{3,2,1,0:T(8,128)(2,1)S(1)}, u32[]{:S(2)}, u32[]{:S(2)}) async-start(bf16[8,16,16,256]{3,2,1,0:T(8,128)(2,1)} %shard_map.119), calls=%async_computation.1 | async-start | bytes 2097152 | tf_op jit(solution)/shard_map/all_to_all | solution.py:371
  22.5 2.7 %shard_map.120 = (bf16[32,16,256]{2,1,0:T(8,128)(2,1)}, bf16[32,16,256]{2,1,0:T(8,128)(2,1)}, bf16[32,16,256]{2,1,0:T(8,128)(2,1)}, bf16[32,16,256]{2,1,0:T(8,128)(2,1)}) custom-call(s32[1]{0:T(128)} %bitcast.2.shard_ref, s32[8,1,36]{2,1,0:T(1,128)} %all_to_all.10.incoming_ref, bf16[256,16,256]{2,1,0:T(8,128)(2,1)} %tokens_ref.3), custom_call_target="tpu_custom_call" | custom-call | tf_op jit(solution)/shard_map/pallas_call | solution.py:375
  25.2 1.8 %collective-permute-start.1 = (bf16[32,16,256]{2,1,0:T(8,128)(2,1)}, bf16[32,16,256]{2,1,0:T(8,128)(2,1)S(1)}, u32[]{:S(2)}, u32[]{:S(2)}) collective-permute-start(bf16[32,16,256]{2,1,0:T(8,128)(2,1)} %get-tuple-element.34), channel_id=1, source_target_pairs={{0,2},{2,0},{4,6},{6,4},{8,10},{10,8},{12,14},{14,12},{1,3},{3,1},... | collective-permute-start | bytes 786440 | tf_op jit(solution)/shard_map/ppermute | solution.py:346
  27.0 1.5 %collective-permute-start.2 = (bf16[32,16,256]{2,1,0:T(8,128)(2,1)}, bf16[32,16,256]{2,1,0:T(8,128)(2,1)S(1)}, u32[]{:S(2)}, u32[]{:S(2)}) collective-permute-start(bf16[32,16,256]{2,1,0:T(8,128)(2,1)} %get-tuple-element.35), channel_id=1, source_target_pairs={{0,4},{2,6},{4,0},{6,2},{8,12},{10,14},{12,8},{14,10},{1,5},{3,7},... | collective-permute-start | bytes 786440 | tf_op jit(solution)/shard_map/ppermute | solution.py:346
  30.1 2.9 %collective-permute-start.5 = (s32[]{:T(128)}, s32[]{:T(128)}, u32[]{:S(2)}, u32[]{:S(2)}) collective-permute-start(s32[]{:T(128)} %convert_element_type.6), channel_id=1, source_target_pairs={{0,16},{16,0},{1,17},{17,1},{2,18},{18,2},{3,19},{19,3},{4,20},{20... | collective-permute-start | bytes 20 | tf_op jit(solution)/shard_map/ppermute | solution.py:392
  33.8 5.3 %collective-permute-done.1.refs_1_.refs_2_.refs_12_ = bf16[32,16,256]{2,1,0:T(8,128)(2,1)S(1)} collective-permute-done((bf16[32,16,256]{2,1,0:T(8,128)(2,1)}, bf16[32,16,256]{2,1,0:T(8,128)(2,1)S(1)}, u32[]{:S(2)}, u32[]{:S(2)}) %collective-permute-start.1) | collective-permute-done | bytes 262176 | tf_op jit(solution)/shard_map/ppermute | solution.py:346
  39.1 6.7 %collective-permute-done.2.refs_2_.refs_3_.refs_13_ = bf16[32,16,256]{2,1,0:T(8,128)(2,1)S(1)} collective-permute-done((bf16[32,16,256]{2,1,0:T(8,128)(2,1)}, bf16[32,16,256]{2,1,0:T(8,128)(2,1)S(1)}, u32[]{:S(2)}, u32[]{:S(2)}) %collective-permute-start.2) | collective-permute-done | bytes 262176 | tf_op jit(solution)/shard_map/ppermute | solution.py:346
  46.5 5.6 %collective-permute-done.3.refs_3_.refs_4_.refs_14_ = bf16[32,16,256]{2,1,0:T(8,128)(2,1)S(1)} collective-permute-done((bf16[32,16,256]{2,1,0:T(8,128)(2,1)}, bf16[32,16,256]{2,1,0:T(8,128)(2,1)S(1)}, u32[]{:S(2)}, u32[]{:S(2)}) %collective-permute-start.3) | collective-permute-done | bytes 262176 | tf_op jit(solution)/shard_map/ppermute | solution.py:346
  52.8 2.6 %shard_map.121 = (bf16[32,16,256]{2,1,0:T(8,128)(2,1)}, bf16[32,16,256]{2,1,0:T(8,128)(2,1)}) custom-call(s32[1]{0:T(128)} %bitcast.2.shard_ref, s32[8,1,36]{2,1,0:T(1,128)} %all_to_all.10.incoming_ref, bf16[32,16,256]{2,1,0:T(8,128)(2,1)} %get-tuple-element.42.refs_0_.refs_1_.refs_11_, bf16[32,16,256]{2,1,0:T(8,128)(2,1)} %copy-done.3, ...), custom_call_target="tpu_custom_call" | custom-call | tf_op jit(solution)/shard_map/pallas_call | solution.py:381
  55.6 1.1 %collective-permute-done.12 = f32[4]{0:T(128)S(1)} collective-permute-done((f32[4]{0:T(128)S(1)}, f32[4]{0:T(128)S(1)}, u32[]{:S(2)}, u32[]{:S(2)}) %collective-permute-start.12) | collective-permute-done | bytes 48 | tf_op jit(solution)/shard_map/ppermute | solution.py:343
  57.3 2.2 %collective-permute-start.4 = (bf16[32,16,256]{2,1,0:T(8,128)(2,1)}, bf16[32,16,256]{2,1,0:T(8,128)(2,1)S(1)}, u32[]{:S(2)}, u32[]{:S(2)}) collective-permute-start(bf16[32,16,256]{2,1,0:T(8,128)(2,1)} %get-tuple-element.37), channel_id=1, source_target_pairs={{0,8},{2,10},{4,12},{6,14},{8,0},{10,2},{12,4},{14,6},{1,9},{3,11}... | collective-permute-start | bytes 786440 | tf_op jit(solution)/shard_map/ppermute | solution.py:346
  59.5 12.9 %collective-permute-done.4.refs_5_.refs_15_ = bf16[32,16,256]{2,1,0:T(8,128)(2,1)S(1)} collective-permute-done((bf16[32,16,256]{2,1,0:T(8,128)(2,1)}, bf16[32,16,256]{2,1,0:T(8,128)(2,1)S(1)}, u32[]{:S(2)}, u32[]{:S(2)}) %collective-permute-start.4) | collective-permute-done | bytes 262176 | tf_op jit(solution)/shard_map/ppermute | solution.py:346
  73.5 3.3 %shard_map.122 = bf16[64,16,256]{2,1,0:T(8,128)(2,1)} custom-call(s32[1]{0:T(128)} %bitcast.core_ref, s32[1,128]{1,0:T(1,128)} %get-tuple-element.40.list_ref, bf16[128,16,256]{2,1,0:T(8,128)(2,1)} %bitcast.10, bf16[32,16,256]{2,1,0:T(8,128)(2,1)} %get-tuple-element.42.refs_0_.refs_1_.refs_11_, bf16[32,16,256]{2,1,0:T(8,128)(2,1)} %copy-done.3, ...), custom_call_target="tpu_custom_call" | custom-call | tf_op jit(solution)/shard_map/pallas_call | solution.py:403
  76.9 2.0 %collective-permute-done.13.far_ref = bf16[64,16,256]{2,1,0:T(8,128)(2,1)S(1)} collective-permute-done((bf16[64,16,256]{2,1,0:T(8,128)(2,1)}, bf16[64,16,256]{2,1,0:T(8,128)(2,1)S(1)}, u32[]{:S(2)}, u32[]{:S(2)}) %collective-permute-start.13) | collective-permute-done | bytes 524320 | tf_op jit(solution)/shard_map/ppermute | solution.py:343
  79.0 1.2 %copy-done.1 = bf16[8,16,16,256]{3,2,1,0:T(8,128)(2,1)S(1)} copy-done((bf16[8,16,16,256]{3,2,1,0:T(8,128)(2,1)S(1)}, bf16[8,16,16,256]{3,2,1,0:T(8,128)(2,1)}, u32[]{:S(2)}) %copy-start.1) | copy-done | bytes 1048600
  80.2 0.9 copy-done.10
  81.2 0.9 copy-done.14
  82.1 0.9 copy-done.15
  83.1 0.9 copy-done.16
  84.0 18.9 %shard_map.123 = bf16[32,512]{1,0:T(8,128)(2,1)S(1)} custom-call(s32[1]{0:T(128)} %bitcast.core_ref, f32[8]{0:T(128)S(1)} %pad_maximum_fusion.1.scale_ref, s32[1,128]{1,0:T(1,128)S(1)} %copy-done.11, bf16[64,16,256]{2,1,0:T(8,128)(2,1)S(1)} %collective-permute-done.13.far_ref, f32[1,512]{1,0:T(1,128)S(1)} %bitcast.14, f32[1,512]{1,0:T(1,128)S(1)} %bitcast.15, ...), custom_call_target="tpu_custom_call" | custom-call | flops 3758096384 | bytes 8388608 | tf_op jit(solution)/shard_map/pallas_call | solution.py:414
  103.1 1.1 %collective-permute-done.14 = bf16[32,512]{1,0:T(8,128)(2,1)S(1)} collective-permute-done((bf16[32,512]{1,0:T(8,128)(2,1)S(1)}, bf16[32,512]{1,0:T(8,128)(2,1)S(1)}, u32[]{:S(2)}, u32[]{:S(2)}) %collective-permute-start.14) | collective-permute-done | bytes 32800 | tf_op jit(solution)/shard_map/ppermute | solution.py:343
  (63 shorter events, 5.8 us)
Async XLA Ops:
  18.2 27.7 %copy-start.17 = (f32[1024]{0:T(1024)S(1)}, f32[1024]{0:T(1024)}, u32[]{:S(2)}) copy-start(f32[1024]{0:T(1024)} %param.24) | copy-start | bytes 12292
  18.2 54.2 %all-to-all-start.1 = ((bf16[8,16,16,256]{3,2,1,0:T(8,128)(2,1)}), bf16[8,16,16,256]{3,2,1,0:T(8,128)(2,1)S(1)}, u32[]{:S(2)}, u32[]{:S(2)}) async-start(bf16[8,16,16,256]{3,2,1,0:T(8,128)(2,1)} %shard_map.119), calls=%async_computation.1 | async-start | bytes 2097152 | tf_op jit(solution)/shard_map/all_to_all | solution.py:371
  21.9 33.7 %copy-start.21 = (f32[4]{0:T(128)S(1)}, f32[4]{0:T(128)}, u32[]{:S(2)}) copy-start(f32[4]{0:T(128)} %param.20) | copy-start | bytes 52
  21.9 50.5 %collective-permute-start.10 = (bf16[1024,512]{1,0:T(8,128)(2,1)}, bf16[1024,512]{1,0:T(8,128)(2,1)}, u32[]{:S(2)}, u32[]{:S(2)}) collective-permute-start(bf16[1024,512]{1,0:T(8,128)(2,1)} %refs_8_.1), channel_id=1, source_target_pairs={{0,1},{1,0},{2,3},{3,2},{4,5},{5,4},{6,7},{7,6},{8,9},{9,8},{10,11... | collective-permute-start | bytes 3145736 | tf_op jit(solution)/shard_map/ppermute | solution.py:343
  22.0 50.4 %collective-permute-start.9 = (bf16[512,1024]{1,0:T(8,128)(2,1)S(1)}, bf16[512,1024]{1,0:T(8,128)(2,1)}, u32[]{:S(2)}, u32[]{:S(2)}) collective-permute-start(bf16[512,1024]{1,0:T(8,128)(2,1)S(1)} %copy-done.12), channel_id=1, source_target_pairs={{0,1},{1,0},{2,3},{3,2},{4,5},{5,4},{6,7},{7,6},{8,9},{9,8},{10,11... | collective-permute-start | bytes 3145736 | tf_op jit(solution)/shard_map/ppermute | solution.py:343
  25.2 13.9 %collective-permute-start.1 = (bf16[32,16,256]{2,1,0:T(8,128)(2,1)}, bf16[32,16,256]{2,1,0:T(8,128)(2,1)S(1)}, u32[]{:S(2)}, u32[]{:S(2)}) collective-permute-start(bf16[32,16,256]{2,1,0:T(8,128)(2,1)} %get-tuple-element.34), channel_id=1, source_target_pairs={{0,2},{2,0},{4,6},{6,4},{8,10},{10,8},{12,14},{14,12},{1,3},{3,1},... | collective-permute-start | bytes 786440 | tf_op jit(solution)/shard_map/ppermute | solution.py:346
  27.0 18.8 %collective-permute-start.2 = (bf16[32,16,256]{2,1,0:T(8,128)(2,1)}, bf16[32,16,256]{2,1,0:T(8,128)(2,1)S(1)}, u32[]{:S(2)}, u32[]{:S(2)}) collective-permute-start(bf16[32,16,256]{2,1,0:T(8,128)(2,1)} %get-tuple-element.35), channel_id=1, source_target_pairs={{0,4},{2,6},{4,0},{6,2},{8,12},{10,14},{12,8},{14,10},{1,5},{3,7},... | collective-permute-start | bytes 786440 | tf_op jit(solution)/shard_map/ppermute | solution.py:346
  30.1 3.6 %collective-permute-start.5 = (s32[]{:T(128)}, s32[]{:T(128)}, u32[]{:S(2)}, u32[]{:S(2)}) collective-permute-start(s32[]{:T(128)} %convert_element_type.6), channel_id=1, source_target_pairs={{0,16},{16,0},{1,17},{17,1},{2,18},{18,2},{3,19},{19,3},{4,20},{20... | collective-permute-start | bytes 20 | tf_op jit(solution)/shard_map/ppermute | solution.py:392
  33.7 18.5 %collective-permute-start.3 = (bf16[32,16,256]{2,1,0:T(8,128)(2,1)}, bf16[32,16,256]{2,1,0:T(8,128)(2,1)S(1)}, u32[]{:S(2)}, u32[]{:S(2)}) collective-permute-start(bf16[32,16,256]{2,1,0:T(8,128)(2,1)} %get-tuple-element.36), channel_id=1, source_target_pairs={{0,6},{2,4},{4,2},{6,0},{8,14},{10,12},{12,10},{14,8},{1,7},{3,5},... | collective-permute-start | bytes 786440 | tf_op jit(solution)/shard_map/ppermute | solution.py:346
  39.1 18.2 %collective-permute-start.6 = (bf16[512,256]{1,0:T(8,128)(2,1)S(1)}, bf16[512,256]{1,0:T(8,128)(2,1)}, u32[]{:S(2)}, u32[]{:S(2)}) collective-permute-start(bf16[512,256]{1,0:T(8,128)(2,1)S(1)} %copy-done.13), channel_id=1, source_target_pairs={{0,1},{1,0},{2,3},{3,2},{4,5},{5,4},{6,7},{7,6},{8,9},{9,8},{10,11... | collective-permute-start | bytes 786440 | tf_op jit(solution)/shard_map/ppermute | solution.py:343
  45.8 11.1 %collective-permute-start.11 = (f32[1024]{0:T(1024)S(1)}, f32[1024]{0:T(1024)S(1)}, u32[]{:S(2)}, u32[]{:S(2)}) collective-permute-start(f32[1024]{0:T(1024)S(1)} %copy-done.17), channel_id=1, source_target_pairs={{0,1},{1,0},{2,3},{3,2},{4,5},{5,4},{6,7},{7,6},{8,9},{9,8},{10,11... | collective-permute-start | bytes 12296 | tf_op jit(solution)/shard_map/ppermute | solution.py:343
  55.4 23.5 %copy-start.2 = (bf16[32,16,256]{2,1,0:T(8,128)(2,1)S(1)}, bf16[32,16,256]{2,1,0:T(8,128)(2,1)}, u32[]{:S(2)}) copy-start(bf16[32,16,256]{2,1,0:T(8,128)(2,1)} %get-tuple-element.42.refs_0_.refs_1_.refs_11_) | copy-start | bytes 786436
  55.5 23.5 %copy-start.4 = (bf16[32,16,256]{2,1,0:T(8,128)(2,1)S(1)}, bf16[32,16,256]{2,1,0:T(8,128)(2,1)}, u32[]{:S(2)}) copy-start(bf16[32,16,256]{2,1,0:T(8,128)(2,1)} %copy-done.3) | copy-start | bytes 786436
  55.5 23.5 %copy-start.6 = (bf16[32,16,256]{2,1,0:T(8,128)(2,1)S(1)}, bf16[32,16,256]{2,1,0:T(8,128)(2,1)}, u32[]{:S(2)}) copy-start(bf16[32,16,256]{2,1,0:T(8,128)(2,1)} %copy-done.5) | copy-start | bytes 786436
  55.5 23.5 %copy-start.8 = (bf16[32,16,256]{2,1,0:T(8,128)(2,1)S(1)}, bf16[32,16,256]{2,1,0:T(8,128)(2,1)}, u32[]{:S(2)}) copy-start(bf16[32,16,256]{2,1,0:T(8,128)(2,1)} %copy-done.7) | copy-start | bytes 786436
  55.5 23.5 %copy-start.11 = (s32[1,128]{1,0:T(1,128)S(1)}, s32[1,128]{1,0:T(1,128)}, u32[]{:S(2)}) copy-start(s32[1,128]{1,0:T(1,128)} %get-tuple-element.40.list_ref) | copy-start | bytes 1540
  55.5 23.5 %copy-start.18 = (f32[512]{0:T(512)S(1)}, f32[512]{0:T(512)}, u32[]{:S(2)}) copy-start(f32[512]{0:T(512)} %param.17) | copy-start | bytes 6148
  55.5 23.5 %copy-start.19 = (f32[512]{0:T(512)S(1)}, f32[512]{0:T(512)}, u32[]{:S(2)}) copy-start(f32[512]{0:T(512)} %param.22) | copy-start | bytes 6148
  55.6 1.2 %collective-permute-start.12 = (f32[4]{0:T(128)S(1)}, f32[4]{0:T(128)S(1)}, u32[]{:S(2)}, u32[]{:S(2)}) collective-permute-start(f32[4]{0:T(128)S(1)} %copy-done.21), channel_id=1, source_target_pairs={{0,1},{1,0},{2,3},{3,2},{4,5},{5,4},{6,7},{7,6},{8,9},{9,8},{10,11... | collective-permute-start | bytes 56 | tf_op jit(solution)/shard_map/ppermute | solution.py:343
  56.7 2.8 %collective-permute-start.7 = (bf16[512,256]{1,0:T(8,128)(2,1)}, bf16[512,256]{1,0:T(8,128)(2,1)}, u32[]{:S(2)}, u32[]{:S(2)}) collective-permute-start(bf16[512,256]{1,0:T(8,128)(2,1)} %refs_2_.1), channel_id=1, source_target_pairs={{0,1},{1,0},{2,3},{3,2},{4,5},{5,4},{6,7},{7,6},{8,9},{9,8},{10,11... | collective-permute-start | bytes 786440 | tf_op jit(solution)/shard_map/ppermute | solution.py:343
  57.0 2.5 %collective-permute-start.8 = (bf16[256,512]{1,0:T(8,128)(2,1)}, bf16[256,512]{1,0:T(8,128)(2,1)}, u32[]{:S(2)}, u32[]{:S(2)}) collective-permute-start(bf16[256,512]{1,0:T(8,128)(2,1)} %refs_4_.1), channel_id=1, source_target_pairs={{0,1},{1,0},{2,3},{3,2},{4,5},{5,4},{6,7},{7,6},{8,9},{9,8},{10,11... | collective-permute-start | bytes 786440 | tf_op jit(solution)/shard_map/ppermute | solution.py:343
  57.3 15.1 %collective-permute-start.4 = (bf16[32,16,256]{2,1,0:T(8,128)(2,1)}, bf16[32,16,256]{2,1,0:T(8,128)(2,1)S(1)}, u32[]{:S(2)}, u32[]{:S(2)}) collective-permute-start(bf16[32,16,256]{2,1,0:T(8,128)(2,1)} %get-tuple-element.37), channel_id=1, source_target_pairs={{0,8},{2,10},{4,12},{6,14},{8,0},{10,2},{12,4},{14,6},{1,9},{3,11}... | collective-permute-start | bytes 786440 | tf_op jit(solution)/shard_map/ppermute | solution.py:346
  76.8 2.2 %collective-permute-start.13 = (bf16[64,16,256]{2,1,0:T(8,128)(2,1)}, bf16[64,16,256]{2,1,0:T(8,128)(2,1)S(1)}, u32[]{:S(2)}, u32[]{:S(2)}) collective-permute-start(bf16[64,16,256]{2,1,0:T(8,128)(2,1)} %shard_map.122), channel_id=1, source_target_pairs={{0,1},{1,0},{2,3},{3,2},{4,5},{5,4},{6,7},{7,6},{8,9},{9,8},{10,11... | collective-permute-start | bytes 1572872 | tf_op jit(solution)/shard_map/ppermute | solution.py:343
  102.9 1.3 %collective-permute-start.14 = (bf16[32,512]{1,0:T(8,128)(2,1)S(1)}, bf16[32,512]{1,0:T(8,128)(2,1)S(1)}, u32[]{:S(2)}, u32[]{:S(2)}) collective-permute-start(bf16[32,512]{1,0:T(8,128)(2,1)S(1)} %shard_map.123), channel_id=1, source_target_pairs={{0,1},{1,0},{2,3},{3,2},{4,5},{5,4},{6,7},{7,6},{8,9},{9,8},{10,11... | collective-permute-start | bytes 98312 | tf_op jit(solution)/shard_map/ppermute | solution.py:343
  (13 other events, 64.7 us)

commit v4 on v0

v4 whole, which is shorter than its diff:
```python
import functools

import jax
import jax.numpy as jnp
from jax import lax
from jax.experimental import pallas as pl
from jax.experimental.pallas import tpu as pltpu
from jax.sharding import PartitionSpec as P

LOG2E = 1.4426950408889634
BLOCK = 8


def norm_rows(values, gain):
    center = values - jnp.mean(values, axis=-1, keepdims=True)
    spread = jnp.mean(center * center, axis=-1, keepdims=True)
    return center * lax.rsqrt(spread + 1e-05) * gain


def dot_nt(a, b):
    return lax.dot_general(a, b, (((1,), (1,)), ((), ())), preferred_element_type=jnp.float32)


def dot(a, b):
    return jnp.dot(a, b, preferred_element_type=jnp.float32)


class Plan:
    def __init__(self, pair_count, owner_count):
        self.owners = owner_count
        self.capacity = max(2, 4 * pair_count // owner_count)
        self.half = owner_count // 2
        split = self.capacity >= 32 and self.half & (self.half - 1) == 0 and self.half > 0
        self.base = self.capacity // 2 if split else self.capacity
        self.extra = self.capacity - self.base
        self.part = self.half * self.extra // 2
        self.far_at = self.half * self.capacity
        self.rest_at = self.far_at + self.half * self.base
        self.row = self.capacity + (self.half if split else 0)
        if split:
            self.starts = [k * self.capacity for k in range(self.half)]
            self.starts += [self.far_at + k * self.base for k in range(self.half)]
            self.starts += [self.rest_at, self.rest_at + self.part]
        else:
            self.starts = [0]


def place_kernel(plan, count, shard_ref, owner_ref, slot_ref, wanted_ref, info_ref, seats_ref):
    total = 2 * count
    owners = plan.owners
    owner = jnp.concatenate([owner_ref[0:1, :], owner_ref[1:2, :]], axis=1)
    slot = jnp.concatenate([slot_ref[0:1, :], slot_ref[1:2, :]], axis=1)

    def place(dim, size):
        return lax.broadcasted_iota(jnp.int32, (size, total), dim)

    def as_bf16(values):
        return values.astype(jnp.float32).astype(jnp.bfloat16)

    row = place(0, owners)
    named = row == owner
    until = as_bf16(jnp.where(place(0, total) <= place(1, total), 1, 0))
    tally = dot(as_bf16(jnp.where(named, 1, 0)), until).astype(jnp.int32)
    rank = jnp.sum(jnp.where(named, tally, 0), axis=0, keepdims=True) - 1
    ranked = as_bf16(jnp.where(place(0, total) == rank, 1, 0))
    wanted = dot_nt(as_bf16(jnp.where(named, slot, 0)), ranked).astype(jnp.int32)
    entry = place(1, 1)
    side = entry // count
    pair = entry % count
    mine = count // 2
    if plan.extra:
        me = shard_ref[0]
        half = plan.half
        over = jnp.maximum(jnp.max(tally, axis=1, keepdims=True) - plan.base, 0)
        far_over = jnp.where(row // half != me // half, over, 0)
        before = jnp.zeros((owners, total), jnp.int32)
        for index in range(owners - 1):
            before = before + jnp.where(row > index, far_over[index : index + 1], 0)
        before = jnp.sum(jnp.where(named, before, 0), axis=0, keepdims=True)
        distance = (owner % half) ^ (me % half)
        rest = plan.rest_at + before + rank - plan.base
        direct = plan.far_at + distance * plan.base + rank
        far = owner // half != me // half
        late = jnp.where(far & (rank >= plan.base), 1, 0)
        where = jnp.where(far, jnp.where(late > 0, rest, direct), distance * plan.capacity + rank)
        told = place(1, owners) == plan.capacity + row % half
        wanted = wanted + jnp.sum(jnp.where(told, far_over, 0), axis=0, keepdims=True)
        late = jnp.maximum(late, jnp.concatenate([late[:, count:], late[:, :count]], axis=1))
        older = (place(0, total) < place(1, total)) & (
            place(0, total) // count == place(1, total) // count
        )
        prompt = as_bf16(jnp.broadcast_to(1 - late, (8, total)))
        ahead = dot(prompt, as_bf16(jnp.where(older, 1, 0))).astype(jnp.int32)[0:1]
        prompt_count = jnp.sum(1 - late, axis=1, keepdims=True) // 2
        seat = jnp.where(late > 0, prompt_count + pair - ahead, ahead)
        full = prompt_count // 2 // BLOCK
    else:
        where = owner * plan.base + rank
        seat = pair
        full = jnp.zeros((1, 1), jnp.int32)
    for index in range(owners):
        wanted_ref[index] = wanted[index : index + 1, : plan.row]
    core = seat % 2
    local = seat // 2
    position = core * count + local // BLOCK * (2 * BLOCK) + side * BLOCK + local % BLOCK
    seated = as_bf16(jnp.where(place(0, total) == position, 1, 0))
    parts = as_bf16(jnp.where(place(0, 8) == 0, where // 16, where % 16))
    listed = dot_nt(parts, seated).astype(jnp.int32)
    info_ref[...] = jnp.where(place(0, 8) == 0, listed[0:1] * 16 + listed[1:2], full)
    lines = place(0, count)
    taken = as_bf16(jnp.where(lines == core * mine + local, 1, 0))
    seats_ref[...] = dot_nt(
        as_bf16(jnp.where(lines == place(1, count), 1, 0)), taken
    ).astype(jnp.bfloat16)


def serve(tokens_ref, incoming_ref, requester, start, served_ref):
    count = served_ref.shape[0]

    def copy(index, carry):
        served_ref[index] = tokens_ref[incoming_ref[requester, 0, start + index]]
        return carry

    lax.fori_loop(0, count, copy, 0, unroll=min(16, count))


def serve_all_kernel(plan, incoming_ref, tokens_ref, served_ref):
    for requester in range(plan.owners):
        serve(tokens_ref, incoming_ref, requester, 0, served_ref.at[requester])


def serve_far_kernel(plan, shard_ref, incoming_ref, tokens_ref, *served_refs):
    for distance, served_ref in enumerate(served_refs):
        relayed = distance < plan.half
        requester = shard_ref[0] ^ (distance + plan.half if relayed else distance)
        serve(tokens_ref, incoming_ref, requester, plan.base if relayed else 0, served_ref)


def serve_near_kernel(plan, shard_ref, incoming_ref, tokens_ref, *served_refs):
    for distance, served_ref in enumerate(served_refs):
        serve(tokens_ref, incoming_ref, shard_ref[0] ^ distance, 0, served_ref)


def relay_kernel(plan, shard_ref, incoming_ref, *refs):
    chunk_refs = refs[: plan.half]
    first_ref, second_ref, sem = refs[plan.half :]
    client = shard_ref[0] ^ plan.half
    position = 0
    for distance, chunk_ref in enumerate(chunk_refs):
        owner = (shard_ref[0] % plan.half) ^ distance
        at = 0
        for index in range(plan.half):
            amount = incoming_ref[client, 0, plan.capacity + index]
            at = at + jnp.where(index < owner, amount, 0)

        def begin(index, carry, chunk_ref=chunk_ref, at=at):
            source = chunk_ref.at[index]

            @pl.when(at + index < plan.part)
            def _():
                pltpu.make_async_copy(source, first_ref.at[at + index], sem).start()

            @pl.when(at + index >= plan.part)
            def _():
                target = second_ref.at[at + index - plan.part]
                pltpu.make_async_copy(source, target, sem).start()

            return carry

        amount = incoming_ref[client, 0, plan.capacity + owner]
        lax.fori_loop(0, amount, begin, 0)
        position = position + amount

    def finish(index, carry):
        pltpu.make_async_copy(chunk_refs[0].at[0], first_ref.at[0], sem).wait()
        return carry

    lax.fori_loop(0, position, finish, 0)


def fetch(plan, where, source_refs, target_ref, sem):
    def among(low, high):
        if high - low == 1:
            source = source_refs[low].at[where - plan.starts[low]]
            pltpu.make_async_copy(source, target_ref, sem).start()
            return
        middle = (low + high) // 2

        @pl.when(where < plan.starts[middle])
        def _():
            among(low, middle)

        @pl.when(where >= plan.starts[middle])
        def _():
            among(middle, high)

    among(0, len(source_refs))


def bounds(plan, phase, info_ref, blocks):
    full = info_ref[1, 0]
    return (0, full) if phase == 0 else (full, blocks)


def pick_kernel(plan, phase, core_ref, info_ref, *refs):
    source_refs = refs[:-2]
    picked_ref, sem = refs[-2:]
    count = picked_ref.shape[0]
    start = (1 - core_ref[0]) * count
    group = 2 * BLOCK
    low, high = bounds(plan, phase, info_ref, count // group)

    def begin(step, carry):
        for index in range(group):
            where = info_ref[0, start + step * group + index]
            fetch(plan, where, source_refs, picked_ref.at[step * group + index], sem)
        return carry

    def finish(step, carry):
        span = pl.ds(0, group)
        pltpu.make_async_copy(source_refs[0].at[span], picked_ref.at[span], sem).wait()
        return carry

    lax.fori_loop(low, high, begin, 0)
    lax.fori_loop(low, high, finish, 0)


def compare_kernel(
    plan,
    phase,
    length,
    head_dim,
    core_ref,
    scale_ref,
    info_ref,
    far_ref,
    gain_attn_ref,
    gain_mlp_ref,
    bias_a_ref,
    bias_b_ref,
    *refs,
):
    if phase:
        earlier_ref, *refs = refs
    held_refs, source_refs = refs[:10], refs[10:-17]
    result_ref = refs[-17]
    matrix_refs = refs[-16:-6]
    own_ref, normed_ref, pooled_ref, hidden_ref, sems, matrix_sems = refs[-6:]
    qk_a_ref, qk_b_ref, value_a_ref, value_b_ref, out_a_ref, out_b_ref = matrix_refs[:6]
    in_a_ref, in_b_ref, back_a_ref, back_b_ref = matrix_refs[6:]
    loads = [
        pltpu.make_async_copy(held, ref, matrix_sems.at[k])
        for k, (held, ref) in enumerate(zip(held_refs, matrix_refs))
    ]
    group = 2 * BLOCK
    half = BLOCK * length
    rows = 2 * half
    blocks = own_ref.shape[0] // group
    low, high = bounds(plan, phase, info_ref, blocks)
    count = result_ref.shape[0]
    pair_dim = 2 * head_dim
    first = core_ref[0] == 0
    start = core_ref[0] * own_ref.shape[0]
    even = lax.broadcasted_iota(jnp.int32, (half, pair_dim), 1) < head_dim
    same = (
        lax.broadcasted_iota(jnp.int32, (half, half), 0) // length
        == lax.broadcasted_iota(jnp.int32, (half, half), 1) // length
    )
    row_pair = lax.broadcasted_iota(jnp.int32, (group, rows), 1) % half // length
    pool = jnp.where(row_pair == lax.broadcasted_iota(jnp.int32, (group, rows), 0), 1.0, 0.0)
    pool = pool.astype(jnp.bfloat16)

    def begin(step, carry):
        for index in range(group):
            at = step * group + index
            fetch(plan, info_ref[0, start + at], source_refs, own_ref.at[at], sems.at[step])
        return carry

    def split(values):
        zero = jnp.zeros_like(values)
        return jnp.concatenate(
            [jnp.where(even, values, zero), jnp.where(even, zero, values)], axis=0
        )

    ones = split(jnp.ones((half, pair_dim), jnp.bfloat16))

    def weigh(scores, factor):
        scores = jnp.where(same, scores, -1e30)
        top = jnp.max(scores, axis=1, keepdims=True)
        return jnp.exp2((scores - top) * factor).astype(jnp.bfloat16)

    def mix(query, value, here, there, factors):
        scores = dot_nt(query[here], split(query[there]))
        weights = [weigh(scores[:, k * half : (k + 1) * half], factors[k]) for k in range(2)]
        mixed = dot(
            jnp.concatenate(weights, axis=1), jnp.concatenate([split(value[there]), ones], axis=1)
        )
        total = mixed[:, pair_dim:]
        inverse = pl.reciprocal(total, approx=True)
        inverse = inverse * (2.0 - total * inverse)
        return (mixed[:, :pair_dim] * inverse).astype(jnp.bfloat16)

    def pair_rows(step):
        return pl.ds(pl.multiple_of(step * BLOCK, BLOCK), BLOCK)

    def attend(step, between):
        span = pl.ds(step * group, group)
        pltpu.make_async_copy(
            source_refs[0].at[pl.ds(0, group)], own_ref.at[span], sems.at[step]
        ).wait()
        own = own_ref[span].reshape(rows, -1).astype(jnp.float32)
        far = far_ref[span].reshape(rows, -1).astype(jnp.float32)
        hidden = jnp.concatenate(
            [jnp.where(first, own, far), jnp.where(first, far, own)], axis=1
        )
        normed = norm_rows(hidden, gain_attn_ref[...]).astype(jnp.bfloat16)
        between()
        head = 0
        for qk_ref, value_ref, out_ref in (
            (qk_a_ref, value_a_ref, out_a_ref),
            (qk_b_ref, value_b_ref, out_b_ref),
        ):
            query = dot(normed, qk_ref[...]).astype(jnp.bfloat16)
            value = dot(normed, value_ref[...]).astype(jnp.bfloat16)
            between()
            mixed = []
            for at in range(0, query.shape[1], pair_dim):
                factors = [scale_ref[head + k] * (LOG2E / head_dim**0.5) for k in range(2)]
                head += 2
                q = query[:, at : at + pair_dim]
                v = value[:, at : at + pair_dim]
                sides = [slice(0, half), slice(half, rows)]
                mixed.append(
                    jnp.concatenate(
                        [mix(q, v, sides[k], sides[1 - k], factors) for k in range(2)], axis=0
                    )
                )
                between()
            hidden = hidden + dot(jnp.concatenate(mixed, axis=1), out_ref[...])
        hidden_ref[pair_rows(step), :] = jnp.sum(
            hidden.reshape(2, BLOCK, length, -1), axis=(0, 2)
        )
        normed_ref[step % 2] = norm_rows(hidden, gain_mlp_ref[...]).astype(jnp.bfloat16)
        between()

    def expand(step):
        offset = 0
        for in_ref, bias_ref in ((in_a_ref, bias_a_ref), (in_b_ref, bias_b_ref)):
            units = in_ref.shape[1]
            tile = units // 4
            for at in range(0, units, tile):
                cut = slice(at, at + tile)
                inner = dot(normed_ref[step % 2], in_ref[:, cut]) + bias_ref[:, cut]
                inner = inner.astype(jnp.bfloat16)
                cubic = inner * inner * jnp.bfloat16(0.0356774081) + jnp.bfloat16(0.7978845608)
                bent = (jnp.tanh(inner * cubic) + jnp.bfloat16(1.0)) * inner
                pooled = dot(pool, bent)
                pooled_ref[pair_rows(step), offset + at : offset + at + tile] = pooled[:BLOCK]
                yield
            offset += units

    def run(steps):
        for _ in steps:
            pass

    @pl.when(high > low)
    def _():
        for load in loads[:4]:
            load.start()
        begin(low, 0)
        for load in loads[4:]:
            load.start()
        lax.fori_loop(low + 1, high, begin, 0)
        for load in loads[:6]:
            load.wait()
        attend(low, lambda: None)
        for load in loads[6:8]:
            load.wait()

        def block(step, carry):
            tiles = expand(step - 1)
            attend(step, lambda: next(tiles, None))
            run(tiles)
            return carry

        lax.fori_loop(low + 1, high, block, 0)
        run(expand(high - 1))
        for load in loads[8:]:
            load.wait()
        pooled = pooled_ref[...] * (0.25 / length)
        coarse = pooled.astype(jnp.bfloat16)
        fine = (pooled - coarse.astype(jnp.float32)).astype(jnp.bfloat16)
        both = jnp.concatenate([coarse, fine], axis=0)
        units = back_a_ref.shape[0]
        back = dot(both[:, :units], back_a_ref[...]) + dot(both[:, units:], back_b_ref[...])
        mean = hidden_ref[...] * (0.5 / length)
        result = (mean + back[:count] + back[count:]).astype(jnp.bfloat16)
        if phase:
            line = lax.broadcasted_iota(jnp.int32, result.shape, 0)
            done = line < low * BLOCK
            result = jnp.where(done, earlier_ref[...].astype(jnp.float32), result.astype(jnp.float32))
        result_ref[...] = result.astype(jnp.bfloat16)

    if phase:

        @pl.when(high <= low)
        def _():
            result_ref[...] = earlier_ref[...]


def seat_kernel(core_ref, seats_ref, here_ref, there_ref, result_ref):
    first = core_ref[0] == 0
    here = here_ref[...].astype(jnp.float32)
    there = there_ref[...].astype(jnp.float32)
    both = jnp.concatenate([jnp.where(first, here, there), jnp.where(first, there, here)], axis=0)
    result_ref[...] = dot(seats_ref[...], both.astype(jnp.bfloat16)).astype(jnp.bfloat16)


def on_device(
    image_tokens,
    pair_owner,
    pair_slot,
    gain_attn,
    w_qk,
    w_value,
    logit_scale,
    w_out,
    gain_mlp,
    w_in,
    bias_in,
    w_back,
):
    owner_count = lax.axis_size("shard")
    groups = lax.axis_size("groups")
    core = lax.axis_index("mp").reshape(1)
    shard = lax.axis_index("shard").reshape(1)
    pair_count = pair_owner.shape[0]
    _, length, features = image_tokens.shape
    width = 2 * features
    head_dim = w_qk.shape[1] // logit_scale.shape[0]
    mine = pair_count // 2
    plan = Plan(pair_count, owner_count)

    def swap(values):
        return lax.ppermute(values, "mp", [(0, 1), (1, 0)])

    def across(values, distance):
        return lax.ppermute(values, "shard", [(k, k ^ distance) for k in range(owner_count)])

    def images(count):
        return jax.ShapeDtypeStruct((count, length, features), jnp.bfloat16)

    smem = pl.BlockSpec(memory_space=pltpu.SMEM)
    vmem = pl.BlockSpec(memory_space=pltpu.VMEM)
    hbm = pl.BlockSpec(memory_space=pltpu.HBM)

    wanted, info, seats = pl.pallas_call(
        functools.partial(place_kernel, plan, pair_count),
        out_shape=(
            jax.ShapeDtypeStruct((owner_count, 1, plan.row), jnp.int32),
            jax.ShapeDtypeStruct((8, 2 * pair_count), jnp.int32),
            jax.ShapeDtypeStruct((pair_count, pair_count), jnp.bfloat16),
        ),
        in_specs=[smem, vmem, vmem],
    )(shard, pair_owner.T, pair_slot.T)
    incoming = lax.all_to_all(wanted, "shard", split_axis=0, concat_axis=0, tiled=True)
    second = None
    if plan.extra:
        served = pl.pallas_call(
            functools.partial(serve_far_kernel, plan),
            out_shape=[images(plan.extra)] * plan.half + [images(plan.base)] * plan.half,
            in_specs=[smem, smem, vmem],
        )(shard, incoming, image_tokens)
        chunks = [served[0]] + [across(served[k], k) for k in range(1, plan.half)]
        direct = [across(served[k], k) for k in range(plan.half, owner_count)]
        incoming_again, _ = lax.optimization_barrier((incoming, served[0]))
        near = pl.pallas_call(
            functools.partial(serve_near_kernel, plan),
            out_shape=[images(plan.capacity)] * plan.half,
            in_specs=[smem, smem, vmem],
        )(shard, incoming_again, image_tokens)
        near = [near[0]] + [across(near[k], k) for k in range(1, plan.half)]
        first, second = pl.pallas_call(
            functools.partial(relay_kernel, plan),
            out_shape=[images(plan.part)] * 2,
            in_specs=[smem, smem] + [hbm] * plan.half,
            scratch_shapes=[pltpu.SemaphoreType.DMA],
        )(shard, incoming, *chunks)
        first = across(first, plan.half)
        crowded = jnp.max(jnp.sum(incoming[:, 0, plan.capacity :], axis=1)) > plan.part
        crowded = crowded.astype(jnp.int32)
        passed = crowded
        for _ in range(groups - 1):
            passed = lax.ppermute(passed, "groups", [(k, (k + 1) % groups) for k in range(groups)])
            crowded = jnp.maximum(crowded, passed)
        second = lax.cond(
            crowded > 0, lambda part: across(part, plan.half), lambda part: part, second
        )
        sources = near + direct
    else:
        served = pl.pallas_call(
            functools.partial(serve_all_kernel, plan),
            out_shape=jax.ShapeDtypeStruct(
                (owner_count, plan.base, length, features), jnp.bfloat16
            ),
            in_specs=[smem, vmem],
        )(incoming, image_tokens)
        returned = lax.all_to_all(served, "shard", split_axis=0, concat_axis=0, tiled=True)
        sources = [returned.reshape(-1, length, features)]
    weights = (w_qk, w_value, w_out, w_in, w_back, bias_in, logit_scale)
    swapped = [swap(w) for w in weights]
    sources, swapped = lax.optimization_barrier((sources, swapped))
    far_qk, far_value, far_out, far_in, far_back, far_bias, far_scale = swapped
    scale = jnp.concatenate([logit_scale, far_scale])
    vectors = [v.reshape(1, -1) for v in (gain_attn, gain_mlp, bias_in, far_bias)]
    matrices = [w_qk, far_qk, w_value, far_value, w_out, far_out, w_in, far_in, w_back, far_back]
    units = 2 * w_in.shape[1]

    def compare(phase, sources, earlier):
        picked = pl.pallas_call(
            functools.partial(pick_kernel, plan, phase),
            out_shape=images(pair_count),
            in_specs=[smem, smem] + [hbm] * len(sources),
            scratch_shapes=[pltpu.SemaphoreType.DMA],
        )(core, info, *sources)
        far = swap(picked)
        flops = 2 * mine * length * width * (3 * width + units)
        return pl.pallas_call(
            functools.partial(compare_kernel, plan, phase, length, head_dim),
            out_shape=jax.ShapeDtypeStruct((mine, width), jnp.bfloat16),
            in_specs=[smem] * 3 + [vmem] * (5 + len(earlier)) + [hbm] * (10 + len(sources)),
            out_specs=vmem,
            scratch_shapes=[pltpu.VMEM(m.shape, m.dtype) for m in matrices]
            + [
                pltpu.VMEM((pair_count, length, features), jnp.bfloat16),
                pltpu.VMEM((2, 2 * BLOCK * length, width), jnp.bfloat16),
                pltpu.VMEM((mine, units), jnp.float32),
                pltpu.VMEM((mine, width), jnp.float32),
                pltpu.SemaphoreType.DMA((mine // BLOCK,)),
                pltpu.SemaphoreType.DMA((10,)),
            ],
            compiler_params=pltpu.CompilerParams(vmem_limit_bytes=32 * 2**20),
            cost_estimate=pl.CostEstimate(
                flops=flops, bytes_accessed=8 * 2**20, transcendentals=mine * length * units
            ),
        )(core, scale, info, far, *vectors, *earlier, *matrices, *sources)

    if plan.extra:
        results = compare(0, sources, [])
        results = compare(1, sources + [first, second], [results])
    else:
        results = compare(1, sources, [jnp.zeros((mine, width), jnp.bfloat16)])
    return pl.pallas_call(
        seat_kernel,
        out_shape=jax.ShapeDtypeStruct((pair_count, width), jnp.bfloat16),
        in_specs=[smem, vmem, vmem, vmem],
    )(core, seats, results, swap(results))


def solution(mesh):
    in_specs = (
        P(("groups", "shard"), None, "mp"),
        P(("groups", "shard"), None),
        P(("groups", "shard"), None),
        P(),
        P(None, "mp"),
        P(None, "mp"),
        P("mp"),
        P("mp", None),
        P(),
        P(None, "mp"),
        P("mp"),
        P("mp", None),
    )
    out_specs = P(("groups", "shard"), None)
    return jax.shard_map(
        on_device, mesh=mesh, in_specs=in_specs, out_specs=out_specs, check_vma=False
    )
```

time: 196 us -> 127 us (0.65)
  blocking collectives: 65.1 us -> 13.7 us
  Pallas kernels: 0 us -> 41 us
  waiting for transfers between devices: 53.5 us -> 28.4 us
  starting transfers between devices: 0.27 us -> 24.2 us
  matrix products: 18.1 us -> 0 us
  other arithmetic: 18.3 us -> 3.8 us
  local copies, waits for them, and re-layouts: 26.6 us -> 13.3 us
  between operations: 13.4 us -> 1.58 us
    all_to_all x1 -> x0, blocking collectives: 51.5 us -> none  [on_device(): lax.all_to_all(served, 'shard', split_axis=0, concat_axis=0, tiled=True)]
    psum x2 -> x0, waiting for transfers between devices: 41.4 us -> none  [the longest x1 22.3 us: on_device(): lax.psum(partial_value.astype(jnp.bfloat16), 'mp').astype(jnp.float32)]
    pallas_call x0 -> x9, Pallas kernels: none -> 41 us  [the longest x2 23.4 us: compare(): pl.pallas_call(functools.partial(compare_kernel, plan, phase, length, hea...]
    ppermute x0 -> x22, waiting for transfers between devices: none -> 28.4 us  [the longest x11 24.8 us: across(): lax.ppermute(values, 'shard', [(k, k ^ distance) for k in range(owner_cou...]
    ppermute x0 -> x22, starting transfers between devices: none -> 24.2 us  [the longest x11 19.3 us: across(): lax.ppermute(values, 'shard', [(k, k ^ distance) for k in range(owner_cou...]
    dot_general x6 -> x0, matrix products: 18.1 us -> none  [the longest x1 7.24 us: expand(): jnp.einsum('pstf,fd->pstd', inner, w_back, preferred_element_type=jnp.flo...]
    all_gather x1 -> x0, waiting for transfers between devices: 12 us -> none  [on_device(): fetched = lax.all_gather(returned, 'mp', axis=3, tiled=True)]
    unnamed x30 -> x80, local copies, waits for them, and re-layouts: 1.81 us -> 13.3 us
  transfers between devices with their start and end apart: 3 -> 22, of which waited for: 3 -> 11; matrix products, arithmetic and copies ran while one was open for 0% -> 3% of each run, Pallas kernels for 0% -> 25%
where the time goes in v4:
time: 127 us; the launch traced here: 126 us
  Pallas kernels  41 us (32%)
  waiting for transfers between devices  28.4 us (22%)
  starting transfers between devices  24.2 us (19%)
  blocking collectives  13.7 us (11%)
  local copies, waits for them, and re-layouts  13.3 us (10%)
  other arithmetic  3.8 us (3%)
  between operations  1.58 us (1%)
    ppermute x11, waiting for transfers between devices, across(): lax.ppermute(values, 'shard', [(k, k ^ distance) for k in range(owner_cou...  24.8 us
    pallas_call x2, Pallas kernels, compare(): pl.pallas_call(functools.partial(compare_kernel, plan, phase, length, hea...  23.4 us
    ppermute x11, starting transfers between devices, across(): lax.ppermute(values, 'shard', [(k, k ^ distance) for k in range(owner_cou...  19.3 us
    all_to_all x1, blocking collectives, on_device(): lax.all_to_all(wanted, 'shard', split_axis=0, concat_axis=0, tiled=True)  13.7 us
    unnamed x80, local copies, waits for them, and re-layouts  13.3 us
    pallas_call x2, Pallas kernels, compare(): pl.pallas_call(functools.partial(pick_kernel, plan, phase), out_shape=ima...  6.01 us
    pallas_call x1, Pallas kernels, on_device(): pl.pallas_call(functools.partial(serve_near_kernel, plan), out_shape=[ima...  2.96 us
    ppermute x10, waiting for transfers between devices, swap(): return lax.ppermute(values, 'mp', [(0, 1), (1, 0)])  2.96 us
  transfers between devices with their start and end apart: 22, of which 11 were waited for; matrix products, arithmetic and copies ran while one was open for 3% of the time, Pallas kernels for 25%

profile of v4, /device:TPU:0, one launch (start us, length us, event | category | flops | bytes accessed | tf_op | source)
XLA Modules:
  0.0 126.1 jit_solution(15478819435650323235)
XLA Ops:
  0.6 1.9 %shard_map.118 = (s32[8,1,36]{2,1,0:T(1,128)}, s32[8,128]{1,0:T(8,128)}, bf16[64,64]{1,0:T(8,128)(2,1)}) custom-call(s32[1]{0:T(128)} %bitcast.1.shard_ref, s32[2,64]{1,0:T(2,128)} %bitcast.16, s32[2,64]{1,0:T(2,128)} %bitcast.17), custom_call_target="tpu_custom_call" | custom-call | tf_op jit(solution)/shard_map/pallas_call | solution.py:457
  2.5 13.7 %all_to_all.5.incoming_ref = s32[8,1,36]{2,1,0:T(1,128)} all-to-all(s32[8,1,36]{2,1,0:T(1,128)} %get-tuple-element.44), channel_id=1, replica_groups=mesh['groups'=2,'shard'=8,'mp'=2] {'shard'}, dimensions={0} | all-to-all | bytes 2304 | tf_op jit(solution)/shard_map/all_to_all | solution.py:466
  16.2 2.7 %shard_map.119 = (bf16[16,16,256]{2,1,0:T(8,128)(2,1)}, bf16[16,16,256]{2,1,0:T(8,128)(2,1)}, bf16[16,16,256]{2,1,0:T(8,128)(2,1)}, bf16[16,16,256]{2,1,0:T(8,12...) custom-call(s32[1]{0:T(128)} %bitcast.1.shard_ref, ...), custom_call_target="tpu_custom_call" | custom-call | tf_op jit(solution)/shard_map/pallas_call | solution.py:469
  19.5 2.4 %collective-permute-start.5 = (bf16[16,16,256]{2,1,0:T(8,128)(2,1)}, bf16[16,16,256]{2,1,0:T(8,128)(2,1)S(1)}, u32[]{:S(2)}, u32[]{:S(2)}) collective-permute-start(bf16[16,16,256]{2,1,0:T(8,128)(2,1)} %get-tuple-element.52), channel_id=1, source_target_pairs={{0,10},{2,8},{4,14},{6,12},{8,2},{10,0},{12,6},{14,4},{1,11},{3,9}... | collective-permute-start | bytes 393224 | tf_op jit(solution)/shard_map/ppermute | solution.py:448
  24.7 7.7 %collective-permute-done.4.refs_4_.refs_14_.refs_15_ = bf16[16,16,256]{2,1,0:T(8,128)(2,1)S(1)} collective-permute-done((bf16[16,16,256]{2,1,0:T(8,128)(2,1)}, bf16[16,16,256]{2,1,0:T(8,128)(2,1)S(1)}, u32[]{:S(2)}, u32[]{:S(2)}) %collective-permute-start.4) | collective-permute-done | bytes 131104 | tf_op jit(solution)/shard_map/ppermute | solution.py:448
  32.4 1.7 %collective-permute-start.7 = (bf16[16,16,256]{2,1,0:T(8,128)(2,1)}, bf16[16,16,256]{2,1,0:T(8,128)(2,1)S(1)}, u32[]{:S(2)}, u32[]{:S(2)}) collective-permute-start(bf16[16,16,256]{2,1,0:T(8,128)(2,1)} %get-tuple-element.54), channel_id=1, source_target_pairs={{0,14},{2,12},{4,10},{6,8},{8,6},{10,4},{12,2},{14,0},{1,15},{3,13... | collective-permute-start | bytes 393224 | tf_op jit(solution)/shard_map/ppermute | solution.py:448
  34.1 1.3 %collective-permute-done.5.refs_5_.refs_15_.refs_16_ = bf16[16,16,256]{2,1,0:T(8,128)(2,1)S(1)} collective-permute-done((bf16[16,16,256]{2,1,0:T(8,128)(2,1)}, bf16[16,16,256]{2,1,0:T(8,128)(2,1)S(1)}, u32[]{:S(2)}, u32[]{:S(2)}) %collective-permute-start.5) | collective-permute-done | bytes 131104 | tf_op jit(solution)/shard_map/ppermute | solution.py:448
  35.4 4.1 %collective-permute-start.15 = (bf16[16,16,256]{2,1,0:T(8,128)(2,1)}, bf16[16,16,256]{2,1,0:T(8,128)(2,1)S(1)}, u32[]{:S(2)}, u32[]{:S(2)}) collective-permute-start(bf16[16,16,256]{2,1,0:T(8,128)(2,1)} %get-tuple-element.65), channel_id=1, source_target_pairs={{0,2},{2,0},{4,6},{6,4},{8,10},{10,8},{12,14},{14,12},{1,3},{3,1},... | collective-permute-start | bytes 393224 | tf_op jit(solution)/shard_map/ppermute | solution.py:448
  39.5 1.9 %collective-permute-start.16 = (bf16[16,16,256]{2,1,0:T(8,128)(2,1)}, bf16[16,16,256]{2,1,0:T(8,128)(2,1)S(1)}, u32[]{:S(2)}, u32[]{:S(2)}) collective-permute-start(bf16[16,16,256]{2,1,0:T(8,128)(2,1)} %get-tuple-element.66), channel_id=1, source_target_pairs={{0,4},{2,6},{4,0},{6,2},{8,12},{10,14},{12,8},{14,10},{1,5},{3,7},... | collective-permute-start | bytes 393224 | tf_op jit(solution)/shard_map/ppermute | solution.py:448
  41.4 3.6 %collective-permute-start.17 = (bf16[16,16,256]{2,1,0:T(8,128)(2,1)}, bf16[16,16,256]{2,1,0:T(8,128)(2,1)S(1)}, u32[]{:S(2)}, u32[]{:S(2)}) collective-permute-start(bf16[16,16,256]{2,1,0:T(8,128)(2,1)} %get-tuple-element.67), channel_id=1, source_target_pairs={{0,6},{2,4},{4,2},{6,0},{8,14},{10,12},{12,10},{14,8},{1,7},{3,5},... | collective-permute-start | bytes 393224 | tf_op jit(solution)/shard_map/ppermute | solution.py:448
  45.7 3.2 %collective-permute-done.17.refs_3_ = bf16[16,16,256]{2,1,0:T(8,128)(2,1)S(1)} collective-permute-done((bf16[16,16,256]{2,1,0:T(8,128)(2,1)}, bf16[16,16,256]{2,1,0:T(8,128)(2,1)S(1)}, u32[]{:S(2)}, u32[]{:S(2)}) %collective-permute-start.17) | collective-permute-done | bytes 131104 | tf_op jit(solution)/shard_map/ppermute | solution.py:448
  49.6 3.0 %shard_map.120 = (bf16[32,16,256]{2,1,0:T(8,128)(2,1)}, bf16[32,16,256]{2,1,0:T(8,128)(2,1)}, bf16[32,16,256]{2,1,0:T(8,128)(2,1)}, bf16[32,16,256]{2,1,0:T(8,128)(2,1)}) custom-call(s32[1]{0:T(128)} %bitcast.1.shard_ref, s32[8,1,36]{2,1,0:T(1,128)} %all_to_all.5.incoming_ref, bf16[256,16,256]{2,1,0:T(8,128)(2,1)} %tokens_ref.3), custom_call_target="tpu_custom_call" | custom-call | tf_op jit(solution)/shard_map/pallas_call | solution.py:477
  53.3 2.5 %collective-permute-start.2 = (bf16[32,16,256]{2,1,0:T(8,128)(2,1)}, bf16[32,16,256]{2,1,0:T(8,128)(2,1)S(1)}, u32[]{:S(2)}, u32[]{:S(2)}) collective-permute-start(bf16[32,16,256]{2,1,0:T(8,128)(2,1)} %get-tuple-element.49), channel_id=1, source_target_pairs={{0,4},{2,6},{4,0},{6,2},{8,12},{10,14},{12,8},{14,10},{1,5},{3,7},... | collective-permute-start | bytes 786440 | tf_op jit(solution)/shard_map/ppermute | solution.py:448
  56.1 2.5 %shard_map.121 = (bf16[32,16,256]{2,1,0:T(8,128)(2,1)}, bf16[32,16,256]{2,1,0:T(8,128)(2,1)}) custom-call(s32[1]{0:T(128)} %bitcast.1.shard_ref, s32[8,1,36]{2,1,0:T(1,128)} %all_to_all.5.incoming_ref, bf16[16,16,256]{2,1,0:T(8,128)(2,1)} %get-tuple-element.45.refs_0_, bf16[16,16,256]{2,1,0:T(8,128)(2,1)} %copy-done.34, bf16[16,16,256]{2,1,0:T(8,128)(2,1)} %copy-done.35, ...), custom_call_target="tpu_custom_call" | custom-call | tf_op jit(solution)/shard_map/pallas_call | solution.py:483
  58.6 2.2 %collective-permute-done.1.refs_1_.refs_11_.refs_12_ = bf16[32,16,256]{2,1,0:T(8,128)(2,1)S(1)} collective-permute-done((bf16[32,16,256]{2,1,0:T(8,128)(2,1)}, bf16[32,16,256]{2,1,0:T(8,128)(2,1)S(1)}, u32[]{:S(2)}, u32[]{:S(2)}) %collective-permute-start.1) | collective-permute-done | bytes 262176 | tf_op jit(solution)/shard_map/ppermute | solution.py:448
  63.1 8.9 %collective-permute-done.3.refs_3_.refs_13_.refs_14_ = bf16[32,16,256]{2,1,0:T(8,128)(2,1)S(1)} collective-permute-done((bf16[32,16,256]{2,1,0:T(8,128)(2,1)}, bf16[32,16,256]{2,1,0:T(8,128)(2,1)S(1)}, u32[]{:S(2)}, u32[]{:S(2)}) %collective-permute-start.3) | collective-permute-done | bytes 262176 | tf_op jit(solution)/shard_map/ppermute | solution.py:448
  73.2 3.3 %shard_map.123 = bf16[64,16,256]{2,1,0:T(8,128)(2,1)} custom-call(s32[1]{0:T(128)} %bitcast.core_ref, s32[8,128]{1,0:T(8,128)} %get-tuple-element.56.info_ref, bf16[32,16,256]{2,1,0:T(8,128)(2,1)} %get-tuple-element.57.refs_0_.refs_10_.refs_11_, bf16[32,16,256]{2,1,0:T(8,128)(2,1)} %copy-done.5, bf16[32,16,256]{2,1,0:T(8,128)(2,1)} %copy-done.7, ...), custom_call_target="tpu_custom_call" | custom-call | tf_op jit(solution)/shard_map/pallas_call | solution.py:520
  76.7 1.7 %slice_reduce_fusion = s32[8]{0:T(128)} fusion(s32[8,1,36]{2,1,0:T(1,128)} %all_to_all.5.incoming_ref), kind=kLoop, calls=%fused_computation | loop fusion | flops 24 | bytes 160 | tf_op jit(solution)/shard_map/reduce_sum | solution.py:490
  78.4 1.4 %reduce_max.9 = s32[]{:T(128)} reduce(s32[8]{0:T(128)} %slice_reduce_fusion, s32[]{:T(128)} %constant.12.clone.1), dimensions={0}, to_apply=%region_1.0 | reduce | flops 7 | bytes 40 | tf_op jit(solution)/shard_map/reduce_max | solution.py:490
  80.3 2.9 %collective-permute-start.19 = (s32[]{:T(128)}, s32[]{:T(128)}, u32[]{:S(2)}, u32[]{:S(2)}) collective-permute-start(s32[]{:T(128)} %convert_element_type.6), channel_id=1, source_target_pairs={{0,16},{16,0},{1,17},{17,1},{2,18},{18,2},{3,19},{19,3},{4,20},{20... | collective-permute-start | bytes 20 | tf_op jit(solution)/shard_map/ppermute | solution.py:494
  84.5 2.7 %shard_map.122 = bf16[64,16,256]{2,1,0:T(8,128)(2,1)} custom-call(s32[1]{0:T(128)} %bitcast.core_ref, s32[8,128]{1,0:T(8,128)} %get-tuple-element.56.info_ref, bf16[32,16,256]{2,1,0:T(8,128)(2,1)} %get-tuple-element.57.refs_0_.refs_10_.refs_11_, bf16[32,16,256]{2,1,0:T(8,128)(2,1)} %copy-done.5, bf16[32,16,256]{2,1,0:T(8,128)(2,1)} %copy-done.7, ...), custom_call_target="tpu_custom_call" | custom-call | tf_op jit(solution)/shard_map/pallas_call | solution.py:520
  98.5 16.0 %shard_map.124.refs_0_ = bf16[32,512]{1,0:T(8,128)(2,1)S(1)} custom-call(s32[1]{0:T(128)} %bitcast.core_ref, f32[8]{0:T(128)S(1)} %pad_maximum_fusion.scale_ref, s32[8,128]{1,0:T(8,128)S(1)} %copy-done.29, bf16[64,16,256]{2,1,0:T(8,128)(2,1)} %collective-permute-done.21.far_ref, f32[1,512]{1,0:T(1,128)S(1)} %bitcast.12, f32[1,512]{1,0:T(1,128)S(1)} %bitcast.14, ...), custom_call_target="tpu_custom_call" | custom-call | flops 1879048192 | bytes 8388608 | tf_op jit(solution)/shard_map/pallas_call | solution.py:528
  114.5 7.4 %shard_map.125.here_ref = bf16[32,512]{1,0:T(8,128)(2,1)S(1)} custom-call(s32[1]{0:T(128)} %bitcast.core_ref, f32[8]{0:T(128)S(1)} %pad_maximum_fusion.scale_ref, s32[8,128]{1,0:T(8,128)S(1)} %copy-done.29, bf16[64,16,256]{2,1,0:T(8,128)(2,1)S(1)} %collective-permute-done.20.far_ref, f32[1,512]{1,0:T(1,128)S(1)} %bitcast.13, f32[1,512]{1,0:T(1,128)S(1)} %bitcast.15, ...), custom_call_target="tpu_custom_call" | custom-call | flops 1879048192 | bytes 8388608 | tf_op jit(solution)/shard_map/pallas_call | solution.py:528
  124.5 1.6 %shard_map.126 = bf16[64,512]{1,0:T(8,128)(2,1)} custom-call(s32[1]{0:T(128)} %bitcast.core_ref, bf16[64,64]{1,0:T(8,128)(2,1)} %get-tuple-element.43.seats_ref, bf16[32,512]{1,0:T(8,128)(2,1)} %copy-done.28, bf16[32,512]{1,0:T(8,128)(2,1)} %copy-done.37), custom_call_target="tpu_custom_call" | custom-call | tf_op jit(solution)/shard_map/pallas_call | solution.py:553
  (114 shorter events, 24.3 us)
Async XLA Ops:
  0.0 45.2 %copy-start.19 = (bf16[512,256]{1,0:T(8,128)(2,1)S(1)}, bf16[512,256]{1,0:T(8,128)(2,1)}, u32[]{:S(2)}) copy-start(bf16[512,256]{1,0:T(8,128)(2,1)} %refs_1_.1) | copy-start | bytes 786436
  0.0 48.9 %copy-start.22 = (bf16[512,256]{1,0:T(8,128)(2,1)S(1)}, bf16[512,256]{1,0:T(8,128)(2,1)}, u32[]{:S(2)}) copy-start(bf16[512,256]{1,0:T(8,128)(2,1)} %refs_3_.1) | copy-start | bytes 786436
  0.0 72.1 %collective-permute-start.11 = (bf16[512,1024]{1,0:T(8,128)(2,1)}, bf16[512,1024]{1,0:T(8,128)(2,1)S(1)}, u32[]{:S(2)}, u32[]{:S(2)}) collective-permute-start(bf16[512,1024]{1,0:T(8,128)(2,1)} %refs_7_.1), channel_id=1, source_target_pairs={{0,1},{1,0},{2,3},{3,2},{4,5},{5,4},{6,7},{7,6},{8,9},{9,8},{10,11... | collective-permute-start | bytes 3145736 | tf_op jit(solution)/shard_map/ppermute | solution.py:445
  0.6 71.5 %collective-permute-start.12 = (bf16[1024,512]{1,0:T(8,128)(2,1)}, bf16[1024,512]{1,0:T(8,128)(2,1)S(1)}, u32[]{:S(2)}, u32[]{:S(2)}) collective-permute-start(bf16[1024,512]{1,0:T(8,128)(2,1)} %refs_9_.1), channel_id=1, source_target_pairs={{0,1},{1,0},{2,3},{3,2},{4,5},{5,4},{6,7},{7,6},{8,9},{9,8},{10,11... | collective-permute-start | bytes 3145736 | tf_op jit(solution)/shard_map/ppermute | solution.py:445
  18.9 13.5 %collective-permute-start.4 = (bf16[16,16,256]{2,1,0:T(8,128)(2,1)}, bf16[16,16,256]{2,1,0:T(8,128)(2,1)S(1)}, u32[]{:S(2)}, u32[]{:S(2)}) collective-permute-start(bf16[16,16,256]{2,1,0:T(8,128)(2,1)} %get-tuple-element.51), channel_id=1, source_target_pairs={{0,8},{2,10},{4,12},{6,14},{8,0},{10,2},{12,4},{14,6},{1,9},{3,11}... | collective-permute-start | bytes 393224 | tf_op jit(solution)/shard_map/ppermute | solution.py:448
  19.5 15.9 %collective-permute-start.5 = (bf16[16,16,256]{2,1,0:T(8,128)(2,1)}, bf16[16,16,256]{2,1,0:T(8,128)(2,1)S(1)}, u32[]{:S(2)}, u32[]{:S(2)}) collective-permute-start(bf16[16,16,256]{2,1,0:T(8,128)(2,1)} %get-tuple-element.52), channel_id=1, source_target_pairs={{0,10},{2,8},{4,14},{6,12},{8,2},{10,0},{12,6},{14,4},{1,11},{3,9}... | collective-permute-start | bytes 393224 | tf_op jit(solution)/shard_map/ppermute | solution.py:448
  21.8 1.1 collective-permute-start.14
  23.0 1.2 collective-permute-start.13
  24.1 15.4 %collective-permute-start.6 = (bf16[16,16,256]{2,1,0:T(8,128)(2,1)}, bf16[16,16,256]{2,1,0:T(8,128)(2,1)S(1)}, u32[]{:S(2)}, u32[]{:S(2)}) collective-permute-start(bf16[16,16,256]{2,1,0:T(8,128)(2,1)} %get-tuple-element.53), channel_id=1, source_target_pairs={{0,12},{2,14},{4,8},{6,10},{8,4},{10,6},{12,0},{14,2},{1,13},{3,15... | collective-permute-start | bytes 393224 | tf_op jit(solution)/shard_map/ppermute | solution.py:448
  32.4 9.0 %collective-permute-start.7 = (bf16[16,16,256]{2,1,0:T(8,128)(2,1)}, bf16[16,16,256]{2,1,0:T(8,128)(2,1)S(1)}, u32[]{:S(2)}, u32[]{:S(2)}) collective-permute-start(bf16[16,16,256]{2,1,0:T(8,128)(2,1)} %get-tuple-element.54), channel_id=1, source_target_pairs={{0,14},{2,12},{4,10},{6,8},{8,6},{10,4},{12,2},{14,0},{1,15},{3,13... | collective-permute-start | bytes 393224 | tf_op jit(solution)/shard_map/ppermute | solution.py:448
  35.4 9.6 %collective-permute-start.15 = (bf16[16,16,256]{2,1,0:T(8,128)(2,1)}, bf16[16,16,256]{2,1,0:T(8,128)(2,1)S(1)}, u32[]{:S(2)}, u32[]{:S(2)}) collective-permute-start(bf16[16,16,256]{2,1,0:T(8,128)(2,1)} %get-tuple-element.65), channel_id=1, source_target_pairs={{0,2},{2,0},{4,6},{6,4},{8,10},{10,8},{12,14},{14,12},{1,3},{3,1},... | collective-permute-start | bytes 393224 | tf_op jit(solution)/shard_map/ppermute | solution.py:448
  39.5 5.7 %collective-permute-start.16 = (bf16[16,16,256]{2,1,0:T(8,128)(2,1)}, bf16[16,16,256]{2,1,0:T(8,128)(2,1)S(1)}, u32[]{:S(2)}, u32[]{:S(2)}) collective-permute-start(bf16[16,16,256]{2,1,0:T(8,128)(2,1)} %get-tuple-element.66), channel_id=1, source_target_pairs={{0,4},{2,6},{4,0},{6,2},{8,12},{10,14},{12,8},{14,10},{1,5},{3,7},... | collective-permute-start | bytes 393224 | tf_op jit(solution)/shard_map/ppermute | solution.py:448
  41.4 7.5 %collective-permute-start.17 = (bf16[16,16,256]{2,1,0:T(8,128)(2,1)}, bf16[16,16,256]{2,1,0:T(8,128)(2,1)S(1)}, u32[]{:S(2)}, u32[]{:S(2)}) collective-permute-start(bf16[16,16,256]{2,1,0:T(8,128)(2,1)} %get-tuple-element.67), channel_id=1, source_target_pairs={{0,6},{2,4},{4,2},{6,0},{8,14},{10,12},{12,10},{14,8},{1,7},{3,5},... | collective-permute-start | bytes 393224 | tf_op jit(solution)/shard_map/ppermute | solution.py:448
  45.0 7.5 %collective-permute-start.10 = (bf16[256,512]{1,0:T(8,128)(2,1)S(1)}, bf16[256,512]{1,0:T(8,128)(2,1)}, u32[]{:S(2)}, u32[]{:S(2)}) collective-permute-start(bf16[256,512]{1,0:T(8,128)(2,1)S(1)} %copy-done.25), channel_id=1, source_target_pairs={{0,1},{1,0},{2,3},{3,2},{4,5},{5,4},{6,7},{7,6},{8,9},{9,8},{10,11... | collective-permute-start | bytes 786440 | tf_op jit(solution)/shard_map/ppermute | solution.py:445
  45.2 8.0 %collective-permute-start.8 = (bf16[512,256]{1,0:T(8,128)(2,1)S(1)}, bf16[512,256]{1,0:T(8,128)(2,1)}, u32[]{:S(2)}, u32[]{:S(2)}) collective-permute-start(bf16[512,256]{1,0:T(8,128)(2,1)S(1)} %copy-done.19), channel_id=1, source_target_pairs={{0,1},{1,0},{2,3},{3,2},{4,5},{5,4},{6,7},{7,6},{8,9},{9,8},{10,11... | collective-permute-start | bytes 786440 | tf_op jit(solution)/shard_map/ppermute | solution.py:445
  48.9 6.8 %collective-permute-start.9 = (bf16[512,256]{1,0:T(8,128)(2,1)S(1)}, bf16[512,256]{1,0:T(8,128)(2,1)}, u32[]{:S(2)}, u32[]{:S(2)}) collective-permute-start(bf16[512,256]{1,0:T(8,128)(2,1)S(1)} %copy-done.22), channel_id=1, source_target_pairs={{0,1},{1,0},{2,3},{3,2},{4,5},{5,4},{6,7},{7,6},{8,9},{9,8},{10,11... | collective-permute-start | bytes 786440 | tf_op jit(solution)/shard_map/ppermute | solution.py:445
  52.6 8.3 %collective-permute-start.1 = (bf16[32,16,256]{2,1,0:T(8,128)(2,1)}, bf16[32,16,256]{2,1,0:T(8,128)(2,1)S(1)}, u32[]{:S(2)}, u32[]{:S(2)}) collective-permute-start(bf16[32,16,256]{2,1,0:T(8,128)(2,1)} %get-tuple-element.48), channel_id=1, source_target_pairs={{0,2},{2,0},{4,6},{6,4},{8,10},{10,8},{12,14},{14,12},{1,3},{3,1},... | collective-permute-start | bytes 786440 | tf_op jit(solution)/shard_map/ppermute | solution.py:448
  53.3 9.9 %collective-permute-start.2 = (bf16[32,16,256]{2,1,0:T(8,128)(2,1)}, bf16[32,16,256]{2,1,0:T(8,128)(2,1)S(1)}, u32[]{:S(2)}, u32[]{:S(2)}) collective-permute-start(bf16[32,16,256]{2,1,0:T(8,128)(2,1)} %get-tuple-element.49), channel_id=1, source_target_pairs={{0,4},{2,6},{4,0},{6,2},{8,12},{10,14},{12,8},{14,10},{1,5},{3,7},... | collective-permute-start | bytes 786440 | tf_op jit(solution)/shard_map/ppermute | solution.py:448
  55.8 16.3 %collective-permute-start.3 = (bf16[32,16,256]{2,1,0:T(8,128)(2,1)}, bf16[32,16,256]{2,1,0:T(8,128)(2,1)S(1)}, u32[]{:S(2)}, u32[]{:S(2)}) collective-permute-start(bf16[32,16,256]{2,1,0:T(8,128)(2,1)} %get-tuple-element.50), channel_id=1, source_target_pairs={{0,6},{2,4},{4,2},{6,0},{8,14},{10,12},{12,10},{14,8},{1,7},{3,5},... | collective-permute-start | bytes 786440 | tf_op jit(solution)/shard_map/ppermute | solution.py:448
  60.8 23.7 %collective-permute-start.18 = (bf16[32,16,256]{2,1,0:T(8,128)(2,1)}, bf16[32,16,256]{2,1,0:T(8,128)(2,1)}, u32[]{:S(2)}, u32[]{:S(2)}) collective-permute-start(bf16[32,16,256]{2,1,0:T(8,128)(2,1)} %get-tuple-element.68), channel_id=1, source_target_pairs={{0,8},{2,10},{4,12},{6,14},{8,0},{10,2},{12,4},{14,6},{1,9},{3,11}... | collective-permute-start | bytes 786440 | tf_op jit(solution)/shard_map/ppermute | solution.py:448
  76.6 11.5 %collective-permute-start.21 = (bf16[64,16,256]{2,1,0:T(8,128)(2,1)}, bf16[64,16,256]{2,1,0:T(8,128)(2,1)}, u32[]{:S(2)}, u32[]{:S(2)}) collective-permute-start(bf16[64,16,256]{2,1,0:T(8,128)(2,1)} %shard_map.123), channel_id=1, source_target_pairs={{0,1},{1,0},{2,3},{3,2},{4,5},{5,4},{6,7},{7,6},{8,9},{9,8},{10,11... | collective-permute-start | bytes 1572872 | tf_op jit(solution)/shard_map/ppermute | solution.py:445
  80.3 3.6 %collective-permute-start.19 = (s32[]{:T(128)}, s32[]{:T(128)}, u32[]{:S(2)}, u32[]{:S(2)}) collective-permute-start(s32[]{:T(128)} %convert_element_type.6), channel_id=1, source_target_pairs={{0,16},{16,0},{1,17},{17,1},{2,18},{18,2},{3,19},{19,3},{4,20},{20... | collective-permute-start | bytes 20 | tf_op jit(solution)/shard_map/ppermute | solution.py:494
  87.3 27.2 %collective-permute-start.20 = (bf16[64,16,256]{2,1,0:T(8,128)(2,1)}, bf16[64,16,256]{2,1,0:T(8,128)(2,1)S(1)}, u32[]{:S(2)}, u32[]{:S(2)}) collective-permute-start(bf16[64,16,256]{2,1,0:T(8,128)(2,1)} %shard_map.122), channel_id=1, source_target_pairs={{0,1},{1,0},{2,3},{3,2},{4,5},{5,4},{6,7},{7,6},{8,9},{9,8},{10,11... | collective-permute-start | bytes 1572872 | tf_op jit(solution)/shard_map/ppermute | solution.py:445
  122.5 1.4 %collective-permute-start.22 = (bf16[32,512]{1,0:T(8,128)(2,1)S(1)}, bf16[32,512]{1,0:T(8,128)(2,1)S(1)}, u32[]{:S(2)}, u32[]{:S(2)}) collective-permute-start(bf16[32,512]{1,0:T(8,128)(2,1)S(1)} %shard_map.125.here_ref), channel_id=1, source_target_pairs={{0,1},{1,0},{2,3},{3,2},{4,5},{5,4},{6,7},{7,6},{8,9},{9,8},{10,11... | collective-permute-start | bytes 98312 | tf_op jit(solution)/shard_map/ppermute | solution.py:445
  (38 other events, 435.1 us)

commit v5 on v0

v5 whole, which is shorter than its diff:
```python
import functools

import jax
import jax.numpy as jnp
from jax import lax
from jax.experimental import pallas as pl
from jax.experimental.pallas import tpu as pltpu
from jax.sharding import PartitionSpec as P

LOG2E = 1.4426950408889634
BLOCK = 8


def norm_rows(values, gain):
    center = values - jnp.mean(values, axis=-1, keepdims=True)
    spread = jnp.mean(center * center, axis=-1, keepdims=True)
    return center * lax.rsqrt(spread + 1e-05) * gain


def dot_nt(a, b):
    return lax.dot_general(a, b, (((1,), (1,)), ((), ())), preferred_element_type=jnp.float32)


def dot(a, b):
    return jnp.dot(a, b, preferred_element_type=jnp.float32)


class Plan:
    def __init__(self, pair_count, owner_count):
        self.owners = owner_count
        self.capacity = max(2, 4 * pair_count // owner_count)
        self.half = owner_count // 2
        split = self.capacity >= 32 and self.half & (self.half - 1) == 0 and self.half > 0
        self.base = self.capacity // 2 if split else self.capacity
        self.extra = self.capacity - self.base
        self.part = self.half * self.extra // 2
        self.near_at = owner_count * self.base
        self.rest_at = self.near_at + self.half * self.extra
        self.slots = self.rest_at + 2 * self.part
        self.row = self.capacity + (self.half if split else 0)


def place_kernel(plan, count, shard_ref, owner_ref, slot_ref, wanted_ref, list_ref):
    total = 2 * count
    owners = plan.owners
    owner = jnp.concatenate([owner_ref[0:1, :], owner_ref[1:2, :]], axis=1)
    slot = jnp.concatenate([slot_ref[0:1, :], slot_ref[1:2, :]], axis=1)

    def place(dim, size):
        return lax.broadcasted_iota(jnp.int32, (size, total), dim)

    def as_bf16(values):
        return values.astype(jnp.float32).astype(jnp.bfloat16)

    row = place(0, owners)
    named = row == owner
    until = as_bf16(jnp.where(place(0, total) <= place(1, total), 1, 0))
    tally = dot(as_bf16(jnp.where(named, 1, 0)), until).astype(jnp.int32)
    rank = jnp.sum(jnp.where(named, tally, 0), axis=0, keepdims=True) - 1
    ranked = as_bf16(jnp.where(place(0, total) == rank, 1, 0))
    wanted = dot_nt(as_bf16(jnp.where(named, slot, 0)), ranked).astype(jnp.int32)
    where = owner * plan.base + rank
    if plan.extra:
        me = shard_ref[0]
        half = plan.half
        over = jnp.maximum(jnp.max(tally, axis=1, keepdims=True) - plan.base, 0)
        far_over = jnp.where(row // half != me // half, over, 0)
        before = jnp.zeros((owners, total), jnp.int32)
        for index in range(owners - 1):
            before = before + jnp.where(row > index, far_over[index : index + 1], 0)
        before = jnp.sum(jnp.where(named, before, 0), axis=0, keepdims=True)
        rest = rank - plan.base
        near = plan.near_at + ((owner % half) ^ (me % half)) * plan.extra + rest
        late = jnp.where(owner // half == me // half, near, plan.rest_at + before + rest)
        where = jnp.where(rest < 0, where, late)
        told = place(1, owners) == plan.capacity + row % half
        wanted = wanted + jnp.sum(jnp.where(told, far_over, 0), axis=0, keepdims=True)
    for index in range(owners):
        wanted_ref[index] = wanted[index : index + 1, : plan.row]
    entry = place(1, 1)
    side = entry // count
    pair = entry % count
    mine = count // 2
    local = pair % mine
    position = pair // mine * count + local // BLOCK * (2 * BLOCK) + side * BLOCK + local % BLOCK
    seated = as_bf16(jnp.where(place(0, total) == position, 1, 0))
    parts = as_bf16(jnp.where(place(0, 8) == 0, where // 16, where % 16))
    listed = dot_nt(parts, seated).astype(jnp.int32)
    list_ref[...] = listed[0:1] * 16 + listed[1:2]


def serve(tokens_ref, incoming_ref, requester, start, served_ref):
    count = served_ref.shape[0]

    def copy(index, carry):
        served_ref[index] = tokens_ref[incoming_ref[requester, 0, start + index]]
        return carry

    lax.fori_loop(0, count, copy, 0, unroll=min(16, count))


def serve_relays_kernel(plan, shard_ref, incoming_ref, tokens_ref, *served_refs):
    for distance, served_ref in enumerate(served_refs):
        requester = shard_ref[0] ^ (distance + plan.half)
        serve(tokens_ref, incoming_ref, requester, plan.base, served_ref)


def serve_kernel(plan, shard_ref, incoming_ref, tokens_ref, served_ref, *near_refs):
    for requester in range(plan.owners):
        serve(tokens_ref, incoming_ref, requester, 0, served_ref.at[requester])
    for distance, near_ref in enumerate(near_refs):
        serve(tokens_ref, incoming_ref, shard_ref[0] ^ distance, plan.base, near_ref)


def relay_kernel(plan, shard_ref, incoming_ref, *refs):
    chunk_refs = refs[: plan.half]
    first_ref, second_ref = refs[plan.half :]
    client = shard_ref[0] ^ plan.half
    for distance, chunk_ref in enumerate(chunk_refs):
        owner = (shard_ref[0] % plan.half) ^ distance
        at = 0
        for index in range(plan.half):
            amount = incoming_ref[client, 0, plan.capacity + index]
            at = at + jnp.where(index < owner, amount, 0)
        amount = incoming_ref[client, 0, plan.capacity + owner]
        fit = jnp.clip(plan.part - at, 0, amount)

        def pack(index, carry, chunk_ref=chunk_ref, at=at):
            first_ref[at + index] = chunk_ref[index]
            return carry

        def pack_more(index, carry, chunk_ref=chunk_ref, at=at):
            second_ref[at + index - plan.part] = chunk_ref[index]
            return carry

        lax.fori_loop(0, fit, pack, 0)
        lax.fori_loop(fit, amount, pack_more, 0)


def pick_kernel(plan, core_ref, list_ref, *refs):
    source_refs = refs[:-4]
    own_ref, other_ref, held_ref, sems = refs[-4:]
    count = own_ref.shape[0]
    at = 0
    loads = []
    for index, source_ref in enumerate(source_refs):
        size = source_ref.shape[0]
        loads.append(
            pltpu.make_async_copy(source_ref, held_ref.at[pl.ds(at, size)], sems.at[index])
        )
        at += size
    for load in loads:
        load.start()
    for load in loads:
        load.wait()
    start = core_ref[0] * count

    def pick(index, carry):
        other_ref[index] = held_ref[list_ref[0, count - start + index]]
        own_ref[index] = held_ref[list_ref[0, start + index]]
        return carry

    lax.fori_loop(0, count, pick, 0, unroll=8)


def compare_kernel(
    length,
    head_dim,
    core_ref,
    scale_ref,
    own_ref,
    far_ref,
    gain_attn_ref,
    gain_mlp_ref,
    *refs,
):
    held_refs = refs[:12]
    result_ref, qkv_ref, out_ref, in_ref, back_ref, bias_ref = refs[12:18]
    normed_ref, heads_ref, mixed_ref, hidden_ref, pooled_ref, mean_ref, sems = refs[18:]
    depth, units = in_ref.shape
    width = depth
    wide = width // 2
    homes = [qkv_ref.at[:, pl.ds(k * wide, wide)] for k in range(4)]
    homes += [out_ref.at[pl.ds(k * wide, wide)] for k in range(2)]
    homes += [in_ref.at[:, pl.ds(k * units // 2, units // 2)] for k in range(2)]
    homes += [bias_ref.at[:, pl.ds(k * units // 2, units // 2)] for k in range(2)]
    homes += [back_ref.at[pl.ds(k * units // 2, units // 2)] for k in range(2)]
    loads = [
        pltpu.make_async_copy(held, home, sems.at[k])
        for k, (held, home) in enumerate(zip(held_refs, homes))
    ]
    for load in loads:
        load.start()
    half = BLOCK * length
    rows = 2 * half
    blocks = own_ref.shape[0] // (2 * BLOCK)
    count = result_ref.shape[0]
    long = 2 * rows
    tile = 256
    pair_dim = 2 * head_dim
    first = core_ref[0] == 0
    even = lax.broadcasted_iota(jnp.int32, (half, pair_dim), 1) < head_dim
    same = (
        lax.broadcasted_iota(jnp.int32, (half, half), 0) // length
        == lax.broadcasted_iota(jnp.int32, (half, half), 1) // length
    )
    row = lax.broadcasted_iota(jnp.int32, (2 * BLOCK, long), 1)
    row_pair = row // rows * BLOCK + row % half // length
    pool = jnp.where(row_pair == lax.broadcasted_iota(jnp.int32, row.shape, 0), 1.0, 0.0)
    pool = pool.astype(jnp.bfloat16)

    def span(step, size):
        return pl.ds(pl.multiple_of(step * size, size), size)

    def split(values):
        zero = jnp.zeros_like(values)
        return jnp.concatenate(
            [jnp.where(even, values, zero), jnp.where(even, zero, values)], axis=0
        )

    ones = split(jnp.ones((half, pair_dim), jnp.bfloat16))

    def start_block(step, carry):
        images = pl.ds(step * 2 * BLOCK, 2 * BLOCK)
        own = own_ref[images].reshape(rows, -1).astype(jnp.float32)
        far = far_ref[images].reshape(rows, -1).astype(jnp.float32)
        tokens = jnp.concatenate([jnp.where(first, own, far), jnp.where(first, far, own)], axis=1)
        hidden_ref[span(step, rows), :] = tokens
        normed_ref[span(step, rows), :] = norm_rows(tokens, gain_attn_ref[...]).astype(jnp.bfloat16)
        return carry

    def project(step, carry):
        here = span(step // 4, long)
        cut = span(step % 4, 2 * width // 4)
        heads_ref[here, cut] = dot(normed_ref[here, :], qkv_ref[:, cut]).astype(jnp.bfloat16)
        return carry

    def weigh(scores, factor):
        scores = jnp.where(same, scores, -1e30)
        top = jnp.max(scores, axis=1, keepdims=True)
        return jnp.exp2((scores - top) * factor).astype(jnp.bfloat16)

    def mix(query, key, value, factors):
        scores = dot_nt(query, split(key))
        weights = [weigh(scores[:, k * half : (k + 1) * half], factors[k]) for k in range(2)]
        mixed = dot(jnp.concatenate(weights, axis=1), jnp.concatenate([split(value), ones], axis=1))
        total = mixed[:, pair_dim:]
        inverse = pl.reciprocal(total, approx=True)
        inverse = inverse * (2.0 - total * inverse)
        return (mixed[:, :pair_dim] * inverse).astype(jnp.bfloat16)

    def attend(step, carry):
        for index in range(width // pair_dim):
            factors = [scale_ref[2 * index + k] * (LOG2E / head_dim**0.5) for k in range(2)]
            cut = slice(index * pair_dim, (index + 1) * pair_dim)
            beyond = slice(width + cut.start, width + cut.stop)
            sides = [span(2 * step + k, half) for k in range(2)]
            query = [heads_ref[side, cut] for side in sides]
            value = [heads_ref[side, beyond] for side in sides]
            for k in range(2):
                mixed_ref[sides[k], cut] = mix(query[k], query[1 - k], value[1 - k], factors)
        return carry

    def join(step, carry):
        here = span(step // 2, long)
        cut = span(step % 2, width // 2)
        hidden_ref[here, cut] += dot(mixed_ref[here, :], out_ref[:, cut])
        return carry

    def middle_block(step, carry):
        here = span(step, rows)
        hidden = hidden_ref[here, :]
        mean_ref[span(step, BLOCK), :] = jnp.sum(
            hidden.reshape(2, BLOCK, length, -1), axis=(0, 2)
        )
        normed_ref[here, :] = norm_rows(hidden, gain_mlp_ref[...]).astype(jnp.bfloat16)
        return carry

    def expand(step, carry):
        tiles = units // tile
        here = span(step // tiles, long)
        cut = span(step % tiles, tile)
        inner = dot(normed_ref[here, :], in_ref[:, cut]) + bias_ref[:, cut]
        inner = inner.astype(jnp.bfloat16)
        cubic = inner * inner * jnp.bfloat16(0.0356774081) + jnp.bfloat16(0.7978845608)
        bent = (jnp.tanh(inner * cubic) + jnp.bfloat16(1.0)) * inner
        pooled_ref[span(step // tiles, 2 * BLOCK), cut] = dot(pool, bent)
        return carry

    lax.fori_loop(0, blocks, start_block, 0)
    for load in loads[:4]:
        load.wait()
    lax.fori_loop(0, blocks // 2 * 4, project, 0)
    lax.fori_loop(0, blocks, attend, 0)
    for load in loads[4:6]:
        load.wait()
    lax.fori_loop(0, blocks // 2 * 2, join, 0)
    lax.fori_loop(0, blocks, middle_block, 0)
    for load in loads[6:10]:
        load.wait()
    lax.fori_loop(0, blocks // 2 * (units // tile), expand, 0)
    for load in loads[10:]:
        load.wait()
    pooled = pooled_ref[...] * (0.25 / length)
    coarse = pooled.astype(jnp.bfloat16)
    fine = (pooled - coarse.astype(jnp.float32)).astype(jnp.bfloat16)
    back = dot(jnp.concatenate([coarse, fine], axis=0), back_ref[...])
    mean = mean_ref[...] * (0.5 / length)
    result_ref[...] = (mean + back[:count] + back[count:]).astype(jnp.bfloat16)


def on_device(
    image_tokens,
    pair_owner,
    pair_slot,
    gain_attn,
    w_qk,
    w_value,
    logit_scale,
    w_out,
    gain_mlp,
    w_in,
    bias_in,
    w_back,
):
    owner_count = lax.axis_size("shard")
    groups = lax.axis_size("groups")
    core = lax.axis_index("mp").reshape(1)
    shard = lax.axis_index("shard").reshape(1)
    pair_count = pair_owner.shape[0]
    _, length, features = image_tokens.shape
    width = 2 * features
    head_dim = w_qk.shape[1] // logit_scale.shape[0]
    mine = pair_count // 2
    units = 2 * w_in.shape[1]
    plan = Plan(pair_count, owner_count)

    def swap(values):
        return lax.ppermute(values, "mp", [(0, 1), (1, 0)])

    def across(values, distance):
        return lax.ppermute(values, "shard", [(k, k ^ distance) for k in range(owner_count)])

    def images(*counts):
        return jax.ShapeDtypeStruct((*counts, length, features), jnp.bfloat16)

    smem = pl.BlockSpec(memory_space=pltpu.SMEM)
    vmem = pl.BlockSpec(memory_space=pltpu.VMEM)
    hbm = pl.BlockSpec(memory_space=pl.ANY)
    roomy = pltpu.CompilerParams(vmem_limit_bytes=56 * 2**20)

    wanted, order = pl.pallas_call(
        functools.partial(place_kernel, plan, pair_count),
        out_shape=(
            jax.ShapeDtypeStruct((owner_count, 1, plan.row), jnp.int32),
            jax.ShapeDtypeStruct((1, 2 * pair_count), jnp.int32),
        ),
        in_specs=[smem, vmem, vmem],
    )(shard, pair_owner.T, pair_slot.T)
    incoming = lax.all_to_all(wanted, "shard", split_axis=0, concat_axis=0, tiled=True)
    if plan.extra:
        chunks = pl.pallas_call(
            functools.partial(serve_relays_kernel, plan),
            out_shape=[images(plan.extra)] * plan.half,
            in_specs=[smem, smem, vmem],
        )(shard, incoming, image_tokens)
        incoming, chunks = lax.optimization_barrier((incoming, chunks))
        chunks = [chunks[0]] + [across(chunks[k], k) for k in range(1, plan.half)]
    served, *near = pl.pallas_call(
        functools.partial(serve_kernel, plan),
        out_shape=[images(owner_count, plan.base)]
        + [images(plan.extra)] * (plan.half if plan.extra else 0),
        in_specs=[smem, smem, vmem],
    )(shard, incoming, image_tokens)
    if plan.extra:
        served, near, chunks = lax.optimization_barrier((served, near, chunks))
    returned = lax.all_to_all(served, "shard", split_axis=0, concat_axis=0, tiled=True)
    sources = [returned.reshape(-1, length, features)]
    if plan.extra:
        first, second = pl.pallas_call(
            functools.partial(relay_kernel, plan),
            out_shape=[images(plan.part)] * 2,
            in_specs=[smem, smem] + [vmem] * plan.half,
        )(shard, incoming, *chunks)
        first = across(first, plan.half)
        near = [near[0]] + [across(near[k], k) for k in range(1, plan.half)]
        crowded = jnp.max(jnp.sum(incoming[:, 0, plan.capacity :], axis=1)) > plan.part
        crowded = crowded.astype(jnp.int32)
        passed = crowded
        for _ in range(groups - 1):
            passed = lax.ppermute(passed, "groups", [(k, (k + 1) % groups) for k in range(groups)])
            crowded = jnp.maximum(crowded, passed)
        second = lax.cond(
            crowded > 0, lambda part: across(part, plan.half), lambda part: part, second
        )
        sources += [*near, first, second]
    weights = (w_qk, w_value, w_out, w_in, w_back, bias_in, logit_scale)
    swapped = [swap(w) for w in weights]
    sources, swapped = lax.optimization_barrier((sources, swapped))
    far_qk, far_value, far_out, far_in, far_back, far_bias, far_scale = swapped
    own, other = pl.pallas_call(
        functools.partial(pick_kernel, plan),
        out_shape=[images(pair_count)] * 2,
        in_specs=[smem, smem] + [hbm] * len(sources),
        scratch_shapes=[
            pltpu.VMEM((plan.slots, length, features), jnp.bfloat16),
            pltpu.SemaphoreType.DMA((len(sources),)),
        ],
        compiler_params=roomy,
    )(core, order, *sources)
    far = swap(other)

    matrices = [w_qk, far_qk, w_value, far_value, w_out, far_out, w_in, far_in]
    matrices += [bias_in.reshape(1, -1), far_bias.reshape(1, -1), w_back, far_back]
    token_count = pair_count * length
    flops = 2 * token_count * width * (3 * width + units)
    here = pl.pallas_call(
        functools.partial(compare_kernel, length, head_dim),
        out_shape=jax.ShapeDtypeStruct((mine, width), jnp.bfloat16),
        in_specs=[smem] * 2 + [vmem] * 4 + [hbm] * 12,
        out_specs=vmem,
        scratch_shapes=[
            pltpu.VMEM((width, 2 * width), jnp.bfloat16),
            pltpu.VMEM((width, width), jnp.bfloat16),
            pltpu.VMEM((width, units), jnp.bfloat16),
            pltpu.VMEM((units, width), jnp.bfloat16),
            pltpu.VMEM((1, units), jnp.float32),
            pltpu.VMEM((token_count, width), jnp.bfloat16),
            pltpu.VMEM((token_count, 2 * width), jnp.bfloat16),
            pltpu.VMEM((token_count, width), jnp.bfloat16),
            pltpu.VMEM((token_count, width), jnp.float32),
            pltpu.VMEM((mine, units), jnp.float32),
            pltpu.VMEM((mine, width), jnp.float32),
            pltpu.SemaphoreType.DMA((12,)),
        ],
        compiler_params=roomy,
        cost_estimate=pl.CostEstimate(
            flops=flops, bytes_accessed=8 * 2**20, transcendentals=token_count * units
        ),
    )(
        core,
        jnp.concatenate([logit_scale, far_scale]),
        own,
        far,
        gain_attn.reshape(1, -1),
        gain_mlp.reshape(1, -1),
        *matrices,
    )
    there = swap(here)
    low = jnp.where(core == 0, here, there)
    high = jnp.where(core == 0, there, here)
    return jnp.concatenate([low, high], axis=0)


def solution(mesh):
    in_specs = (
        P(("groups", "shard"), None, "mp"),
        P(("groups", "shard"), None),
        P(("groups", "shard"), None),
        P(),
        P(None, "mp"),
        P(None, "mp"),
        P("mp"),
        P("mp", None),
        P(),
        P(None, "mp"),
        P("mp"),
        P("mp", None),
    )
    out_specs = P(("groups", "shard"), None)
    return jax.shard_map(
        on_device, mesh=mesh, in_specs=in_specs, out_specs=out_specs, check_vma=False
    )
```

time: 196 us -> 94.3 us (0.48)
  blocking collectives: 65.1 us -> 13.6 us
  Pallas kernels: 0 us -> 31.6 us
  waiting for transfers between devices: 53.5 us -> 22.2 us
  local copies, waits for them, and re-layouts: 26.6 us -> 1.9 us
  starting transfers between devices: 0.27 us -> 20.2 us
  matrix products: 18.1 us -> 0 us
  other arithmetic: 18.3 us -> 2.94 us
  between operations: 13.4 us -> 1.45 us
    all_to_all x1 -> x0, blocking collectives: 51.5 us -> none  [on_device(): lax.all_to_all(served, 'shard', split_axis=0, concat_axis=0, tiled=True)]
    psum x2 -> x0, waiting for transfers between devices: 41.4 us -> none  [the longest x1 22.3 us: on_device(): lax.psum(partial_value.astype(jnp.bfloat16), 'mp').astype(jnp.float32)]
    pallas_call x0 -> x6, Pallas kernels: none -> 31.6 us  [the longest x1 19.2 us: on_device(): pl.pallas_call(functools.partial(compare_kernel, length, head_dim), out_s...]
    ppermute x0 -> x17, waiting for transfers between devices: none -> 22.2 us  [the longest x7 16.6 us: across(): lax.ppermute(values, 'shard', [(k, k ^ distance) for k in range(owner_cou...]
    dot_general x6 -> x0, matrix products: 18.1 us -> none  [the longest x1 7.24 us: expand(): jnp.einsum('pstf,fd->pstd', inner, w_back, preferred_element_type=jnp.flo...]
    ppermute x0 -> x17, starting transfers between devices: none -> 16.6 us  [the longest x7 12 us: across(): lax.ppermute(values, 'shard', [(k, k ^ distance) for k in range(owner_cou...]
    all_gather x1 -> x0, waiting for transfers between devices: 12 us -> none  [on_device(): fetched = lax.all_gather(returned, 'mp', axis=3, tiled=True)]
    reshape x5 -> x0, local copies, waits for them, and re-layouts: 10.9 us -> none  [the longest x2 5.43 us: attend(): value = value.reshape(count, sides, length, heads, head_dim)]
  transfers between devices with their start and end apart: 3 -> 18, of which waited for: 3 -> 11; matrix products, arithmetic and copies ran while one was open for 0% -> 2% of each run, Pallas kernels for 0% -> 5%
where the time goes in v5:
time: 94.3 us; the launch traced here: 93.8 us
  Pallas kernels  31.6 us (34%)
  waiting for transfers between devices  22.2 us (24%)
  starting transfers between devices  20.2 us (21%)
  blocking collectives  13.6 us (14%)
  other arithmetic  2.94 us (3%)
  local copies, waits for them, and re-layouts  1.9 us (2%)
  between operations  1.45 us (2%)
    pallas_call x1, Pallas kernels, on_device(): pl.pallas_call(functools.partial(compare_kernel, length, head_dim), out_s...  19.2 us
    ppermute x7, waiting for transfers between devices, across(): lax.ppermute(values, 'shard', [(k, k ^ distance) for k in range(owner_cou...  16.6 us
    all_to_all x1, blocking collectives, on_device(): lax.all_to_all(wanted, 'shard', split_axis=0, concat_axis=0, tiled=True)  13.6 us
    ppermute x7, starting transfers between devices, across(): lax.ppermute(values, 'shard', [(k, k ^ distance) for k in range(owner_cou...  12 us
    ppermute x9, waiting for transfers between devices, swap(): return lax.ppermute(values, 'mp', [(0, 1), (1, 0)])  4.89 us
    all_to_all x1, starting transfers between devices, on_device(): lax.all_to_all(served, 'shard', split_axis=0, concat_axis=0, tiled=True)  3.56 us
    pallas_call x1, Pallas kernels, on_device(): pl.pallas_call(functools.partial(pick_kernel, plan), out_shape=[images(pa...  3.32 us
    pallas_call x1, Pallas kernels, on_device(): pl.pallas_call(functools.partial(serve_kernel, plan), out_shape=[images(o...  2.91 us
  transfers between devices with their start and end apart: 18, of which 11 were waited for; matrix products, arithmetic and copies ran while one was open for 2% of the time, Pallas kernels for 5%

profile of v5, /device:TPU:0, one launch (start us, length us, event | category | flops | bytes accessed | tf_op | source)
XLA Modules:
  0.0 93.8 jit_solution(9048871894263935978)
XLA Ops:
  0.0 1.8 %shard_map.118 = (s32[8,1,36]{2,1,0:T(1,128)}, s32[1,128]{1,0:T(1,128)}) custom-call(s32[1]{0:T(128)} %bitcast.2.shard_ref, s32[2,64]{1,0:T(2,128)} %bitcast.11, s32[2,64]{1,0:T(2,128)} %bitcast.12), custom_call_target="tpu_custom_call" | custom-call | tf_op jit(solution)/shard_map/pallas_call | solution.py:352
  1.8 13.6 %all_to_all.10.incoming_ref = s32[8,1,36]{2,1,0:T(1,128)} all-to-all(s32[8,1,36]{2,1,0:T(1,128)} %get-tuple-element.53), channel_id=1, replica_groups=mesh['groups'=2,'shard'=8,'mp'=2] {'shard'}, dimensions={0} | all-to-all | bytes 2304 | tf_op jit(solution)/shard_map/all_to_all | solution.py:360
  15.4 2.5 %shard_map.119 = (bf16[16,16,256]{2,1,0:T(8,128)(2,1)}, bf16[16,16,256]{2,1,0:T(8,128)(2,1)}, bf16[16,16,256]{2,1,0:T(8,128)(2,1)}, bf16[16,16,256]{2,1,0:T(8,128)(2,1)}) custom-call(s32[1]{0:T(128)} %bitcast.2.shard_ref, s32[8,1,36]{2,1,0:T(1,128)} %all_to_all.10.incoming_ref, bf16[256,16,256]{2,1,0:T(8,128)(2,1)} %tokens_ref.3), custom_call_target="tpu_custom_call" | custom-call | tf_op jit(solution)/shard_map/pallas_call | solution.py:362
  19.2 2.2 %collective-permute-start.3 = (bf16[16,16,256]{2,1,0:T(8,128)(2,1)}, bf16[16,16,256]{2,1,0:T(8,128)(2,1)S(1)}, u32[]{:S(2)}, u32[]{:S(2)}) collective-permute-start(bf16[16,16,256]{2,1,0:T(8,128)(2,1)} %get-tuple-element.67), channel_id=1, source_target_pairs={{0,6},{2,4},{4,2},{6,0},{8,14},{10,12},{12,10},{14,8},{1,7},{3,5},... | collective-permute-start | bytes 393224 | tf_op jit(solution)/shard_map/ppermute | solution.py:342
  21.4 2.9 %shard_map.120 = (bf16[8,16,16,256]{3,2,1,0:T(8,128)(2,1)}, bf16[16,16,256]{2,1,0:T(8,128)(2,1)}, bf16[16,16,256]{2,1,0:T(8,128)(2,1)}, bf16[16,16,256]{2,1,0:T(8,128)(2,1)}, bf16[16,16,256]{2,1,0:T(8,128)(2,1)}) custom-call(s32[1]{0:T(128)} %bitcast.2.shard_ref, s32[8,1,36]{2,1,0:T(1,128)} %all_to_all.10.incoming_ref, bf16[256,16,256]{2,1,0:T(8,128)(2,1)} %tokens_ref.3), custom_call_target="tpu_custom_call" | custom-call | tf_op jit(solution)/shard_map/pallas_call | solution.py:369
  24.5 1.6 %collective-permute-done.3.refs_3_ = bf16[16,16,256]{2,1,0:T(8,128)(2,1)S(1)} collective-permute-done((bf16[16,16,256]{2,1,0:T(8,128)(2,1)}, bf16[16,16,256]{2,1,0:T(8,128)(2,1)S(1)}, u32[]{:S(2)}, u32[]{:S(2)}) %collective-permute-start.3) | collective-permute-done | bytes 131104 | tf_op jit(solution)/shard_map/ppermute | solution.py:342
  26.1 3.6 %all-to-all-start.1 = ((bf16[8,16,16,256]{3,2,1,0:T(8,128)(2,1)}), bf16[8,16,16,256]{3,2,1,0:T(8,128)(2,1)S(1)}, u32[]{:S(2)}, u32[]{:S(2)}) async-start(bf16[8,16,16,256]{3,2,1,0:T(8,128)(2,1)} %get-tuple-element.68), calls=%async_computation.1 | async-start | bytes 2097152 | tf_op jit(solution)/shard_map/all_to_all | solution.py:377
  32.4 2.9 %collective-permute-start.8 = (s32[]{:T(128)}, s32[]{:T(128)}, u32[]{:S(2)}, u32[]{:S(2)}) collective-permute-start(s32[]{:T(128)} %convert_element_type.6), channel_id=1, source_target_pairs={{0,16},{16,0},{1,17},{17,1},{2,18},{18,2},{3,19},{19,3},{4,20},{20... | collective-permute-start | bytes 20 | tf_op jit(solution)/shard_map/ppermute | solution.py:391
  36.6 2.0 %shard_map.121 = (bf16[32,16,256]{2,1,0:T(8,128)(2,1)}, bf16[32,16,256]{2,1,0:T(8,128)(2,1)S(1)}) custom-call(s32[1]{0:T(128)} %bitcast.2.shard_ref, s32[8,1,36]{2,1,0:T(1,128)} %all_to_all.10.incoming_ref, bf16[16,16,256]{2,1,0:T(8,128)(2,1)} %get-tuple-element.73.refs_0_, bf16[16,16,256]{2,1,0:T(8,128)(2,1)} %copy-done.2, bf16[16,16,256]{2,1,0:T(8,128)(2,1)} %copy-done.3, ...), custom_call_target="tpu_custom_call" | custom-call | tf_op jit(solution)/shard_map/pallas_call | solution.py:380
  38.6 1.1 %collective-permute-done.15 = f32[4]{0:T(128)S(1)} collective-permute-done((f32[4]{0:T(128)S(1)}, f32[4]{0:T(128)S(1)}, u32[]{:S(2)}, u32[]{:S(2)}) %collective-permute-start.15) | collective-permute-done | bytes 48 | tf_op jit(solution)/shard_map/ppermute | solution.py:339
  40.0 1.0 %collective-permute-done.14 = f32[1024]{0:T(1024)S(1)} collective-permute-done((f32[1024]{0:T(1024)S(1)}, f32[1024]{0:T(1024)S(1)}, u32[]{:S(2)}, u32[]{:S(2)}) %collective-permute-start.14) | collective-permute-done | bytes 4128 | tf_op jit(solution)/shard_map/ppermute | solution.py:339
  41.1 1.8 %collective-permute-start.4 = (bf16[16,16,256]{2,1,0:T(8,128)(2,1)}, bf16[16,16,256]{2,1,0:T(8,128)(2,1)S(1)}, u32[]{:S(2)}, u32[]{:S(2)}) collective-permute-start(bf16[16,16,256]{2,1,0:T(8,128)(2,1)} %get-tuple-element.70), channel_id=1, source_target_pairs={{0,2},{2,0},{4,6},{6,4},{8,10},{10,8},{12,14},{14,12},{1,3},{3,1},... | collective-permute-start | bytes 393224 | tf_op jit(solution)/shard_map/ppermute | solution.py:342
  42.9 2.5 %collective-permute-start.7 = (bf16[32,16,256]{2,1,0:T(8,128)(2,1)}, bf16[32,16,256]{2,1,0:T(8,128)(2,1)S(1)}, u32[]{:S(2)}, u32[]{:S(2)}) collective-permute-start(bf16[32,16,256]{2,1,0:T(8,128)(2,1)} %get-tuple-element.77), channel_id=1, source_target_pairs={{0,8},{2,10},{4,12},{6,14},{8,0},{10,2},{12,4},{14,6},{1,9},{3,11}... | collective-permute-start | bytes 786440 | tf_op jit(solution)/shard_map/ppermute | solution.py:342
  45.4 1.5 %collective-permute-start.5 = (bf16[16,16,256]{2,1,0:T(8,128)(2,1)}, bf16[16,16,256]{2,1,0:T(8,128)(2,1)S(1)}, u32[]{:S(2)}, u32[]{:S(2)}) collective-permute-start(bf16[16,16,256]{2,1,0:T(8,128)(2,1)} %get-tuple-element.71), channel_id=1, source_target_pairs={{0,4},{2,6},{4,0},{6,2},{8,12},{10,14},{12,8},{14,10},{1,5},{3,7},... | collective-permute-start | bytes 393224 | tf_op jit(solution)/shard_map/ppermute | solution.py:342
  46.9 1.6 %collective-permute-done.4.refs_2_ = bf16[16,16,256]{2,1,0:T(8,128)(2,1)S(1)} collective-permute-done((bf16[16,16,256]{2,1,0:T(8,128)(2,1)}, bf16[16,16,256]{2,1,0:T(8,128)(2,1)S(1)}, u32[]{:S(2)}, u32[]{:S(2)}) %collective-permute-start.4) | collective-permute-done | bytes 131104 | tf_op jit(solution)/shard_map/ppermute | solution.py:342
  48.5 2.7 %collective-permute-start.6 = (bf16[16,16,256]{2,1,0:T(8,128)(2,1)}, bf16[16,16,256]{2,1,0:T(8,128)(2,1)S(1)}, u32[]{:S(2)}, u32[]{:S(2)}) collective-permute-start(bf16[16,16,256]{2,1,0:T(8,128)(2,1)} %get-tuple-element.72), channel_id=1, source_target_pairs={{0,6},{2,4},{4,2},{6,0},{8,14},{10,12},{12,10},{14,8},{1,7},{3,5},... | collective-permute-start | bytes 393224 | tf_op jit(solution)/shard_map/ppermute | solution.py:342
  51.2 4.0 %collective-permute-done.5.refs_3_ = bf16[16,16,256]{2,1,0:T(8,128)(2,1)S(1)} collective-permute-done((bf16[16,16,256]{2,1,0:T(8,128)(2,1)}, bf16[16,16,256]{2,1,0:T(8,128)(2,1)S(1)}, u32[]{:S(2)}, u32[]{:S(2)}) %collective-permute-start.5) | collective-permute-done | bytes 131104 | tf_op jit(solution)/shard_map/ppermute | solution.py:342
  55.3 1.9 %collective-permute-done.6.refs_4_ = bf16[16,16,256]{2,1,0:T(8,128)(2,1)S(1)} collective-permute-done((bf16[16,16,256]{2,1,0:T(8,128)(2,1)}, bf16[16,16,256]{2,1,0:T(8,128)(2,1)S(1)}, u32[]{:S(2)}, u32[]{:S(2)}) %collective-permute-start.6) | collective-permute-done | bytes 131104 | tf_op jit(solution)/shard_map/ppermute | solution.py:342
  57.1 7.2 %collective-permute-done.7.refs_5_ = bf16[32,16,256]{2,1,0:T(8,128)(2,1)S(1)} collective-permute-done((bf16[32,16,256]{2,1,0:T(8,128)(2,1)}, bf16[32,16,256]{2,1,0:T(8,128)(2,1)S(1)}, u32[]{:S(2)}, u32[]{:S(2)}) %collective-permute-start.7) | collective-permute-done | bytes 262176 | tf_op jit(solution)/shard_map/ppermute | solution.py:342
  65.5 3.3 %shard_map.122 = (bf16[64,16,256]{2,1,0:T(8,128)(2,1)}, bf16[64,16,256]{2,1,0:T(8,128)(2,1)}) custom-call(s32[1]{0:T(128)} %bitcast.core_ref, s32[1,128]{1,0:T(1,128)} %get-tuple-element.80.list_ref, bf16[128,16,256]{2,1,0:T(8,128)(2,1)} %bitcast.10, bf16[16,16,256]{2,1,0:T(8,128)(2,1)} %get-tuple-element.82.refs_1_, bf16[16,16,256]{2,1,0:T(8,128)(2,1)} %copy-done.5, ...), custom_call_target="tpu_custom_call" | custom-call | tf_op jit(solution)/shard_map/pallas_call | solution.py:401
  69.5 1.5 %collective-permute-done.16.far_ref = bf16[64,16,256]{2,1,0:T(8,128)(2,1)S(1)} collective-permute-done((bf16[64,16,256]{2,1,0:T(8,128)(2,1)}, bf16[64,16,256]{2,1,0:T(8,128)(2,1)S(1)}, u32[]{:S(2)}, u32[]{:S(2)}) %collective-permute-start.16) | collective-permute-done | bytes 524320 | tf_op jit(solution)/shard_map/ppermute | solution.py:339
  71.0 0.8 copy-done.10
  71.8 19.2 %shard_map.123 = bf16[32,512]{1,0:T(8,128)(2,1)} custom-call(s32[1]{0:T(128)} %bitcast.core_ref, f32[8]{0:T(128)} %pad_maximum_fusion.1.scale_ref, bf16[64,16,256]{2,1,0:T(8,128)(2,1)} %get-tuple-element.88.own_ref, bf16[64,16,256]{2,1,0:T(8,128)(2,1)} %copy-done.10, f32[1,512]{1,0:T(1,128)} %bitcast.15, f32[1,512]{1,0:T(1,128)} %bitcast.16, ...), custom_call_target="tpu_custom_call" | custom-call | flops 3758096384 | bytes 8388608 | tf_op jit(solution)/shard_map/pallas_call | solution.py:417
  91.2 1.3 %collective-permute-done.17 = bf16[32,512]{1,0:T(8,128)(2,1)S(1)} collective-permute-done((bf16[32,512]{1,0:T(8,128)(2,1)}, bf16[32,512]{1,0:T(8,128)(2,1)S(1)}, u32[]{:S(2)}, u32[]{:S(2)}) %collective-permute-start.17) | collective-permute-done | bytes 32800 | tf_op jit(solution)/shard_map/ppermute | solution.py:339
  (61 shorter events, 8.0 us)
Async XLA Ops:
  17.9 13.0 %copy-start.8 = (s32[8,1,36]{2,1,0:T(1,128)S(1)}, s32[8,1,36]{2,1,0:T(1,128)}, u32[]{:S(2)}) copy-start(s32[8,1,36]{2,1,0:T(1,128)} %all_to_all.10.incoming_ref) | copy-start | bytes 3460
  17.9 6.6 %collective-permute-start.1 = (bf16[16,16,256]{2,1,0:T(8,128)(2,1)}, bf16[16,16,256]{2,1,0:T(8,128)(2,1)S(1)}, u32[]{:S(2)}, u32[]{:S(2)}) collective-permute-start(bf16[16,16,256]{2,1,0:T(8,128)(2,1)} %get-tuple-element.65), channel_id=1, source_target_pairs={{0,2},{2,0},{4,6},{6,4},{8,10},{10,8},{12,14},{14,12},{1,3},{3,1},... | collective-permute-start | bytes 393224 | tf_op jit(solution)/shard_map/ppermute | solution.py:342
  18.6 5.9 %collective-permute-start.2 = (bf16[16,16,256]{2,1,0:T(8,128)(2,1)}, bf16[16,16,256]{2,1,0:T(8,128)(2,1)S(1)}, u32[]{:S(2)}, u32[]{:S(2)}) collective-permute-start(bf16[16,16,256]{2,1,0:T(8,128)(2,1)} %get-tuple-element.66), channel_id=1, source_target_pairs={{0,4},{2,6},{4,0},{6,2},{8,12},{10,14},{12,8},{14,10},{1,5},{3,7},... | collective-permute-start | bytes 393224 | tf_op jit(solution)/shard_map/ppermute | solution.py:342
  19.2 6.9 %collective-permute-start.3 = (bf16[16,16,256]{2,1,0:T(8,128)(2,1)}, bf16[16,16,256]{2,1,0:T(8,128)(2,1)S(1)}, u32[]{:S(2)}, u32[]{:S(2)}) collective-permute-start(bf16[16,16,256]{2,1,0:T(8,128)(2,1)} %get-tuple-element.67), channel_id=1, source_target_pairs={{0,6},{2,4},{4,2},{6,0},{8,14},{10,12},{12,10},{14,8},{1,7},{3,5},... | collective-permute-start | bytes 393224 | tf_op jit(solution)/shard_map/ppermute | solution.py:342
  24.3 14.3 %copy-start.17 = (f32[4]{0:T(128)S(1)}, f32[4]{0:T(128)}, u32[]{:S(2)}) copy-start(f32[4]{0:T(128)} %param.20) | copy-start | bytes 52
  24.3 15.4 %copy-start.15 = (f32[1024]{0:T(1024)S(1)}, f32[1024]{0:T(1024)}, u32[]{:S(2)}) copy-start(f32[1024]{0:T(1024)} %param.24) | copy-start | bytes 12292
  24.3 16.6 %copy-start.11 = (bf16[512,256]{1,0:T(8,128)(2,1)S(1)}, bf16[512,256]{1,0:T(8,128)(2,1)}, u32[]{:S(2)}) copy-start(bf16[512,256]{1,0:T(8,128)(2,1)} %refs_0_.1) | copy-start | bytes 786436
  26.1 38.2 %all-to-all-start.1 = ((bf16[8,16,16,256]{3,2,1,0:T(8,128)(2,1)}), bf16[8,16,16,256]{3,2,1,0:T(8,128)(2,1)S(1)}, u32[]{:S(2)}, u32[]{:S(2)}) async-start(bf16[8,16,16,256]{3,2,1,0:T(8,128)(2,1)} %get-tuple-element.68), calls=%async_computation.1 | async-start | bytes 2097152 | tf_op jit(solution)/shard_map/all_to_all | solution.py:377
  29.7 34.7 %collective-permute-start.12 = (bf16[512,1024]{1,0:T(8,128)(2,1)S(1)}, bf16[512,1024]{1,0:T(8,128)(2,1)}, u32[]{:S(2)}, u32[]{:S(2)}) collective-permute-start(bf16[512,1024]{1,0:T(8,128)(2,1)S(1)} %copy-done.9), channel_id=1, source_target_pairs={{0,1},{1,0},{2,3},{3,2},{4,5},{5,4},{6,7},{7,6},{8,9},{9,8},{10,11... | collective-permute-start | bytes 3145736 | tf_op jit(solution)/shard_map/ppermute | solution.py:339
  29.8 34.6 %collective-permute-start.13 = (bf16[1024,512]{1,0:T(8,128)(2,1)}, bf16[1024,512]{1,0:T(8,128)(2,1)}, u32[]{:S(2)}, u32[]{:S(2)}) collective-permute-start(bf16[1024,512]{1,0:T(8,128)(2,1)} %refs_10_.1), channel_id=1, source_target_pairs={{0,1},{1,0},{2,3},{3,2},{4,5},{5,4},{6,7},{7,6},{8,9},{9,8},{10,11... | collective-permute-start | bytes 3145736 | tf_op jit(solution)/shard_map/ppermute | solution.py:339
  30.3 10.8 %collective-permute-start.10 = (bf16[512,256]{1,0:T(8,128)(2,1)S(1)}, bf16[512,256]{1,0:T(8,128)(2,1)}, u32[]{:S(2)}, u32[]{:S(2)}) collective-permute-start(bf16[512,256]{1,0:T(8,128)(2,1)S(1)} %copy-done.12), channel_id=1, source_target_pairs={{0,1},{1,0},{2,3},{3,2},{4,5},{5,4},{6,7},{7,6},{8,9},{9,8},{10,11... | collective-permute-start | bytes 786440 | tf_op jit(solution)/shard_map/ppermute | solution.py:339
  30.4 12.6 %collective-permute-start.11 = (bf16[256,512]{1,0:T(8,128)(2,1)S(1)}, bf16[256,512]{1,0:T(8,128)(2,1)}, u32[]{:S(2)}, u32[]{:S(2)}) collective-permute-start(bf16[256,512]{1,0:T(8,128)(2,1)S(1)} %copy-done.13), channel_id=1, source_target_pairs={{0,1},{1,0},{2,3},{3,2},{4,5},{5,4},{6,7},{7,6},{8,9},{9,8},{10,11... | collective-permute-start | bytes 786440 | tf_op jit(solution)/shard_map/ppermute | solution.py:339
  32.4 3.6 %collective-permute-start.8 = (s32[]{:T(128)}, s32[]{:T(128)}, u32[]{:S(2)}, u32[]{:S(2)}) collective-permute-start(s32[]{:T(128)} %convert_element_type.6), channel_id=1, source_target_pairs={{0,16},{16,0},{1,17},{17,1},{2,18},{18,2},{3,19},{19,3},{4,20},{20... | collective-permute-start | bytes 20 | tf_op jit(solution)/shard_map/ppermute | solution.py:391
  38.6 1.1 %collective-permute-start.15 = (f32[4]{0:T(128)S(1)}, f32[4]{0:T(128)S(1)}, u32[]{:S(2)}, u32[]{:S(2)}) collective-permute-start(f32[4]{0:T(128)S(1)} %copy-done.17), channel_id=1, source_target_pairs={{0,1},{1,0},{2,3},{3,2},{4,5},{5,4},{6,7},{7,6},{8,9},{9,8},{10,11... | collective-permute-start | bytes 56 | tf_op jit(solution)/shard_map/ppermute | solution.py:339
  39.7 1.2 %collective-permute-start.14 = (f32[1024]{0:T(1024)S(1)}, f32[1024]{0:T(1024)S(1)}, u32[]{:S(2)}, u32[]{:S(2)}) collective-permute-start(f32[1024]{0:T(1024)S(1)} %copy-done.15), channel_id=1, source_target_pairs={{0,1},{1,0},{2,3},{3,2},{4,5},{5,4},{6,7},{7,6},{8,9},{9,8},{10,11... | collective-permute-start | bytes 12296 | tf_op jit(solution)/shard_map/ppermute | solution.py:339
  40.9 30.1 %copy-start.16 = (f32[1024]{0:T(1024)}, f32[1024]{0:T(1024)S(1)}, u32[]{:S(2)}) copy-start(f32[1024]{0:T(1024)S(1)} %collective-permute-done.14) | copy-start | bytes 12292
  40.9 4.5 %collective-permute-start.9 = (bf16[512,256]{1,0:T(8,128)(2,1)S(1)}, bf16[512,256]{1,0:T(8,128)(2,1)S(1)}, u32[]{:S(2)}, u32[]{:S(2)}) collective-permute-start(bf16[512,256]{1,0:T(8,128)(2,1)S(1)} %copy-done.11), channel_id=1, source_target_pairs={{0,1},{1,0},{2,3},{3,2},{4,5},{5,4},{6,7},{7,6},{8,9},{9,8},{10,11... | collective-permute-start | bytes 786440 | tf_op jit(solution)/shard_map/ppermute | solution.py:339
  41.1 7.4 %collective-permute-start.4 = (bf16[16,16,256]{2,1,0:T(8,128)(2,1)}, bf16[16,16,256]{2,1,0:T(8,128)(2,1)S(1)}, u32[]{:S(2)}, u32[]{:S(2)}) collective-permute-start(bf16[16,16,256]{2,1,0:T(8,128)(2,1)} %get-tuple-element.70), channel_id=1, source_target_pairs={{0,2},{2,0},{4,6},{6,4},{8,10},{10,8},{12,14},{14,12},{1,3},{3,1},... | collective-permute-start | bytes 393224 | tf_op jit(solution)/shard_map/ppermute | solution.py:342
  42.9 21.4 %collective-permute-start.7 = (bf16[32,16,256]{2,1,0:T(8,128)(2,1)}, bf16[32,16,256]{2,1,0:T(8,128)(2,1)S(1)}, u32[]{:S(2)}, u32[]{:S(2)}) collective-permute-start(bf16[32,16,256]{2,1,0:T(8,128)(2,1)} %get-tuple-element.77), channel_id=1, source_target_pairs={{0,8},{2,10},{4,12},{6,14},{8,0},{10,2},{12,4},{14,6},{1,9},{3,11}... | collective-permute-start | bytes 786440 | tf_op jit(solution)/shard_map/ppermute | solution.py:342
  45.4 9.9 %collective-permute-start.5 = (bf16[16,16,256]{2,1,0:T(8,128)(2,1)}, bf16[16,16,256]{2,1,0:T(8,128)(2,1)S(1)}, u32[]{:S(2)}, u32[]{:S(2)}) collective-permute-start(bf16[16,16,256]{2,1,0:T(8,128)(2,1)} %get-tuple-element.71), channel_id=1, source_target_pairs={{0,4},{2,6},{4,0},{6,2},{8,12},{10,14},{12,8},{14,10},{1,5},{3,7},... | collective-permute-start | bytes 393224 | tf_op jit(solution)/shard_map/ppermute | solution.py:342
  48.5 15.9 %copy-start.5 = (bf16[16,16,256]{2,1,0:T(8,128)(2,1)}, bf16[16,16,256]{2,1,0:T(8,128)(2,1)S(1)}, u32[]{:S(2)}) copy-start(bf16[16,16,256]{2,1,0:T(8,128)(2,1)S(1)} %collective-permute-done.4.refs_2_) | copy-start | bytes 393220
  48.5 8.6 %collective-permute-start.6 = (bf16[16,16,256]{2,1,0:T(8,128)(2,1)}, bf16[16,16,256]{2,1,0:T(8,128)(2,1)S(1)}, u32[]{:S(2)}, u32[]{:S(2)}) collective-permute-start(bf16[16,16,256]{2,1,0:T(8,128)(2,1)} %get-tuple-element.72), channel_id=1, source_target_pairs={{0,6},{2,4},{4,2},{6,0},{8,14},{10,12},{12,10},{14,8},{1,7},{3,5},... | collective-permute-start | bytes 393224 | tf_op jit(solution)/shard_map/ppermute | solution.py:342
  68.8 2.2 %collective-permute-start.16 = (bf16[64,16,256]{2,1,0:T(8,128)(2,1)}, bf16[64,16,256]{2,1,0:T(8,128)(2,1)S(1)}, u32[]{:S(2)}, u32[]{:S(2)}) collective-permute-start(bf16[64,16,256]{2,1,0:T(8,128)(2,1)} %get-tuple-element.89), channel_id=1, source_target_pairs={{0,1},{1,0},{2,3},{3,2},{4,5},{5,4},{6,7},{7,6},{8,9},{9,8},{10,11... | collective-permute-start | bytes 1572872 | tf_op jit(solution)/shard_map/ppermute | solution.py:339
  91.0 1.5 %collective-permute-start.17 = (bf16[32,512]{1,0:T(8,128)(2,1)}, bf16[32,512]{1,0:T(8,128)(2,1)S(1)}, u32[]{:S(2)}, u32[]{:S(2)}) collective-permute-start(bf16[32,512]{1,0:T(8,128)(2,1)} %shard_map.123), channel_id=1, source_target_pairs={{0,1},{1,0},{2,3},{3,2},{4,5},{5,4},{6,7},{7,6},{8,9},{9,8},{10,11... | collective-permute-start | bytes 98312 | tf_op jit(solution)/shard_map/ppermute | solution.py:339
  (12 other events, 93.6 us)

commit v6 on v5

--- a/solution.py
+++ b/solution.py
@@ -137,10 +137,10 @@
         lax.fori_loop(fit, amount, pack_more, 0)
 
 
-def pick_kernel(plan, core_ref, list_ref, *refs):
-    source_refs = refs[:-4]
-    own_ref, other_ref, held_ref, sems = refs[-4:]
-    count = own_ref.shape[0]
+def pick_kernel(core_ref, list_ref, *refs):
+    source_refs = refs[:-3]
+    picked_ref, held_ref, sems = refs[-3:]
+    count = picked_ref.shape[0]
     at = 0
     loads = []
     for index, source_ref in enumerate(source_refs):
@@ -156,11 +156,10 @@
     start = core_ref[0] * count
 
     def pick(index, carry):
-        other_ref[index] = held_ref[list_ref[0, count - start + index]]
-        own_ref[index] = held_ref[list_ref[0, start + index]]
-        return carry
-
-    lax.fori_loop(0, count, pick, 0, unroll=8)
+        picked_ref[index] = held_ref[list_ref[0, start + index]]
+        return carry
+
+    lax.fori_loop(0, count, pick, 0, unroll=16)
 
 
 def compare_kernel(
@@ -168,17 +167,15 @@
     head_dim,
     core_ref,
     scale_ref,
-    own_ref,
-    far_ref,
     gain_attn_ref,
     gain_mlp_ref,
     *refs,
 ):
-    held_refs = refs[:12]
-    result_ref, qkv_ref, out_ref, in_ref, back_ref, bias_ref = refs[12:18]
-    normed_ref, heads_ref, mixed_ref, hidden_ref, pooled_ref, mean_ref, sems = refs[18:]
-    depth, units = in_ref.shape
-    width = depth
+    own_held_ref, far_held_ref, *held_refs = refs[:14]
+    result_ref, qkv_ref, out_ref, in_ref, back_ref, bias_ref = refs[14:20]
+    tokens_ref, normed_ref, heads_ref, mixed_ref, hidden_ref = refs[20:25]
+    inner_ref, bent_ref, pooled_ref, mean_ref, sems, token_sems = refs[25:]
+    width, units = in_ref.shape
     wide = width // 2
     homes = [qkv_ref.at[:, pl.ds(k * wide, wide)] for k in range(4)]
     homes += [out_ref.at[pl.ds(k * wide, wide)] for k in range(2)]
@@ -189,25 +186,24 @@
         pltpu.make_async_copy(held, home, sems.at[k])
         for k, (held, home) in enumerate(zip(held_refs, homes))
     ]
-    for load in loads:
+    core = core_ref[0]
+    token_loads = [
+        pltpu.make_async_copy(own_held_ref, tokens_ref.at[core], token_sems.at[0]),
+        pltpu.make_async_copy(far_held_ref, tokens_ref.at[1 - core], token_sems.at[1]),
+    ]
+    for load in token_loads + loads:
         load.start()
     half = BLOCK * length
     rows = 2 * half
-    blocks = own_ref.shape[0] // (2 * BLOCK)
     count = result_ref.shape[0]
-    long = 2 * rows
+    blocks = count // BLOCK
     tile = 256
     pair_dim = 2 * head_dim
-    first = core_ref[0] == 0
     even = lax.broadcasted_iota(jnp.int32, (half, pair_dim), 1) < head_dim
     same = (
         lax.broadcasted_iota(jnp.int32, (half, half), 0) // length
         == lax.broadcasted_iota(jnp.int32, (half, half), 1) // length
     )
-    row = lax.broadcasted_iota(jnp.int32, (2 * BLOCK, long), 1)
-    row_pair = row // rows * BLOCK + row % half // length
-    pool = jnp.where(row_pair == lax.broadcasted_iota(jnp.int32, row.shape, 0), 1.0, 0.0)
-    pool = pool.astype(jnp.bfloat16)
 
     def span(step, size):
         return pl.ds(pl.multiple_of(step * size, size), size)
@@ -220,17 +216,19 @@
 
     ones = split(jnp.ones((half, pair_dim), jnp.bfloat16))
 
-    def start_block(step, carry):
-        images = pl.ds(step * 2 * BLOCK, 2 * BLOCK)
-        own = own_ref[images].reshape(rows, -1).astype(jnp.float32)
-        far = far_ref[images].reshape(rows, -1).astype(jnp.float32)
-        tokens = jnp.concatenate([jnp.where(first, own, far), jnp.where(first, far, own)], axis=1)
-        hidden_ref[span(step, rows), :] = tokens
-        normed_ref[span(step, rows), :] = norm_rows(tokens, gain_attn_ref[...]).astype(jnp.bfloat16)
+    def begin(step, carry):
+        images = pl.ds(step * 2, 2)
+        here = span(step, 2 * length)
+        tokens = [
+            tokens_ref[k, images].reshape(2 * length, -1).astype(jnp.float32) for k in range(2)
+        ]
+        tokens = jnp.concatenate(tokens, axis=1)
+        hidden_ref[here, :] = tokens
+        normed_ref[here, :] = norm_rows(tokens, gain_attn_ref[...]).astype(jnp.bfloat16)
         return carry
 
     def project(step, carry):
-        here = span(step // 4, long)
+        here = span(step // 4, rows)
         cut = span(step % 4, 2 * width // 4)
         heads_ref[here, cut] = dot(normed_ref[here, :], qkv_ref[:, cut]).astype(jnp.bfloat16)
         return carry
@@ -262,43 +260,64 @@
         return carry
 
     def join(step, carry):
-        here = span(step // 2, long)
+        here = span(step // 2, rows)
         cut = span(step % 2, width // 2)
         hidden_ref[here, cut] += dot(mixed_ref[here, :], out_ref[:, cut])
         return carry
 
-    def middle_block(step, carry):
-        here = span(step, rows)
-        hidden = hidden_ref[here, :]
-        mean_ref[span(step, BLOCK), :] = jnp.sum(
-            hidden.reshape(2, BLOCK, length, -1), axis=(0, 2)
-        )
-        normed_ref[here, :] = norm_rows(hidden, gain_mlp_ref[...]).astype(jnp.bfloat16)
-        return carry
+    def middle(step, carry):
+        total = 0.0
+        for side in range(2):
+            at = (step // BLOCK * 2 + side) * BLOCK + step % BLOCK
+            here = span(at, length)
+            hidden = hidden_ref[here, :]
+            total = total + jnp.sum(hidden, axis=0, keepdims=True)
+            normed_ref[here, :] = norm_rows(hidden, gain_mlp_ref[...]).astype(jnp.bfloat16)
+        mean_ref[pl.ds(step, 1), :] = total
+        return carry
+
+    long = inner_ref.shape[1]
+    pairs = long // (2 * length)
+    row = lax.broadcasted_iota(jnp.int32, (pairs, long), 1)
+    row_pair = row // rows * BLOCK + row % half // length
+    pool = jnp.where(row_pair == lax.broadcasted_iota(jnp.int32, row.shape, 0), 1.0, 0.0)
+    pool = pool.astype(jnp.bfloat16)
+    tiles = units // tile
+    steps = count // pairs * tiles
+    piece = 32
 
     def expand(step, carry):
-        tiles = units // tile
-        here = span(step // tiles, long)
-        cut = span(step % tiles, tile)
-        inner = dot(normed_ref[here, :], in_ref[:, cut]) + bias_ref[:, cut]
-        inner = inner.astype(jnp.bfloat16)
-        cubic = inner * inner * jnp.bfloat16(0.0356774081) + jnp.bfloat16(0.7978845608)
-        bent = (jnp.tanh(inner * cubic) + jnp.bfloat16(1.0)) * inner
-        pooled_ref[span(step // tiles, 2 * BLOCK), cut] = dot(pool, bent)
-        return carry
-
-    lax.fori_loop(0, blocks, start_block, 0)
+        new = lax.rem(step, steps)
+        here = span(new // tiles, long)
+        cut = span(lax.rem(new, tiles), tile)
+        inner_ref[lax.rem(step, 2)] = dot(normed_ref[here, :], in_ref[:, cut])
+        pooled = dot(pool, bent_ref[lax.rem(step, 2)])
+        last = lax.rem(step + steps - 1, steps)
+        bias = bias_ref[:, span(lax.rem(last, tiles), tile)]
+        for at in range(0, long, piece):
+            inner = inner_ref[lax.rem(step + 1, 2), at : at + piece, :] + bias
+            inner = inner.astype(jnp.bfloat16)
+            cubic = inner * inner * jnp.bfloat16(0.0356774081) + jnp.bfloat16(0.7978845608)
+            bent = (jnp.tanh(inner * cubic) + jnp.bfloat16(1.0)) * inner
+            bent_ref[lax.rem(step + 1, 2), at : at + piece, :] = bent
+        old = lax.rem(step + steps - 2, steps)
+        pooled_ref[span(old // tiles, pairs), span(lax.rem(old, tiles), tile)] = pooled
+        return carry
+
+    for load in token_loads:
+        load.wait()
+    lax.fori_loop(0, count, begin, 0, unroll=8)
     for load in loads[:4]:
         load.wait()
-    lax.fori_loop(0, blocks // 2 * 4, project, 0)
+    lax.fori_loop(0, blocks * 4, project, 0, unroll=2)
     lax.fori_loop(0, blocks, attend, 0)
     for load in loads[4:6]:
         load.wait()
-    lax.fori_loop(0, blocks // 2 * 2, join, 0)
-    lax.fori_loop(0, blocks, middle_block, 0)
+    lax.fori_loop(0, blocks * 2, join, 0, unroll=2)
+    lax.fori_loop(0, count, middle, 0, unroll=8)
     for load in loads[6:10]:
         load.wait()
-    lax.fori_loop(0, blocks // 2 * (units // tile), expand, 0)
+    lax.fori_loop(0, steps + 2, expand, 0)
     for load in loads[10:]:
         load.wait()
     pooled = pooled_ref[...] * (0.25 / length)
@@ -347,7 +366,6 @@
     smem = pl.BlockSpec(memory_space=pltpu.SMEM)
     vmem = pl.BlockSpec(memory_space=pltpu.VMEM)
     hbm = pl.BlockSpec(memory_space=pl.ANY)
-    roomy = pltpu.CompilerParams(vmem_limit_bytes=56 * 2**20)
 
     wanted, order = pl.pallas_call(
         functools.partial(place_kernel, plan, pair_count),
@@ -372,16 +390,19 @@
         + [images(plan.extra)] * (plan.half if plan.extra else 0),
         in_specs=[smem, smem, vmem],
     )(shard, incoming, image_tokens)
-    if plan.extra:
-        served, near, chunks = lax.optimization_barrier((served, near, chunks))
-    returned = lax.all_to_all(served, "shard", split_axis=0, concat_axis=0, tiled=True)
-    sources = [returned.reshape(-1, length, features)]
+    weights = (w_qk, w_value, w_out, w_in, w_back, bias_in, logit_scale)
     if plan.extra:
         first, second = pl.pallas_call(
             functools.partial(relay_kernel, plan),
             out_shape=[images(plan.part)] * 2,
             in_specs=[smem, smem] + [vmem] * plan.half,
         )(shard, incoming, *chunks)
+        served, near, first, second, incoming, weights = lax.optimization_barrier(
+            (served, near, first, second, incoming, weights)
+        )
+    returned = lax.all_to_all(served, "shard", split_axis=0, concat_axis=0, tiled=True)
+    sources = [returned.reshape(-1, length, features)]
+    if plan.extra:
         first = across(first, plan.half)
         near = [near[0]] + [across(near[k], k) for k in range(1, plan.half)]
         crowded = jnp.max(jnp.sum(incoming[:, 0, plan.capacity :], axis=1)) > plan.part
@@ -394,30 +415,31 @@
             crowded > 0, lambda part: across(part, plan.half), lambda part: part, second
         )
         sources += [*near, first, second]
-    weights = (w_qk, w_value, w_out, w_in, w_back, bias_in, logit_scale)
     swapped = [swap(w) for w in weights]
     sources, swapped = lax.optimization_barrier((sources, swapped))
     far_qk, far_value, far_out, far_in, far_back, far_bias, far_scale = swapped
-    own, other = pl.pallas_call(
-        functools.partial(pick_kernel, plan),
-        out_shape=[images(pair_count)] * 2,
-        in_specs=[smem, smem] + [hbm] * len(sources),
-        scratch_shapes=[
-            pltpu.VMEM((plan.slots, length, features), jnp.bfloat16),
-            pltpu.SemaphoreType.DMA((len(sources),)),
-        ],
-        compiler_params=roomy,
-    )(core, order, *sources)
-    far = swap(other)
-
+
+    def pick(core):
+        return pl.pallas_call(
+            pick_kernel,
+            out_shape=images(pair_count),
+            in_specs=[smem, smem] + [hbm] * len(sources),
+            scratch_shapes=[
+                pltpu.VMEM((plan.slots, length, features), jnp.bfloat16),
+                pltpu.SemaphoreType.DMA((len(sources),)),
+            ],
+        )(core, order, *sources)
+
+    far = swap(pick(1 - core))
+    own = pick(core)
     matrices = [w_qk, far_qk, w_value, far_value, w_out, far_out, w_in, far_in]
     matrices += [bias_in.reshape(1, -1), far_bias.reshape(1, -1), w_back, far_back]
     token_count = pair_count * length
-    flops = 2 * token_count * width * (3 * width + units)
+    long = token_count // 2
     here = pl.pallas_call(
         functools.partial(compare_kernel, length, head_dim),
         out_shape=jax.ShapeDtypeStruct((mine, width), jnp.bfloat16),
-        in_specs=[smem] * 2 + [vmem] * 4 + [hbm] * 12,
+        in_specs=[smem] * 2 + [vmem] * 2 + [hbm] * 14,
         out_specs=vmem,
         scratch_shapes=[
             pltpu.VMEM((width, 2 * width), jnp.bfloat16),
@@ -425,25 +447,31 @@
             pltpu.VMEM((width, units), jnp.bfloat16),
             pltpu.VMEM((units, width), jnp.bfloat16),
             pltpu.VMEM((1, units), jnp.float32),
+            pltpu.VMEM((2, pair_count, length, features), jnp.bfloat16),
             pltpu.VMEM((token_count, width), jnp.bfloat16),
             pltpu.VMEM((token_count, 2 * width), jnp.bfloat16),
             pltpu.VMEM((token_count, width), jnp.bfloat16),
             pltpu.VMEM((token_count, width), jnp.float32),
+            pltpu.VMEM((2, long, 256), jnp.float32),
+            pltpu.VMEM((2, long, 256), jnp.bfloat16),
             pltpu.VMEM((mine, units), jnp.float32),
             pltpu.VMEM((mine, width), jnp.float32),
             pltpu.SemaphoreType.DMA((12,)),
+            pltpu.SemaphoreType.DMA((2,)),
         ],
-        compiler_params=roomy,
+        compiler_params=pltpu.CompilerParams(vmem_limit_bytes=56 * 2**20),
         cost_estimate=pl.CostEstimate(
-            flops=flops, bytes_accessed=8 * 2**20, transcendentals=token_count * units
+            flops=2 * token_count * width * (3 * width + units),
+            bytes_accessed=8 * 2**20,
+            transcendentals=token_count * units,
         ),
     )(
         core,
         jnp.concatenate([logit_scale, far_scale]),
+        gain_attn.reshape(1, -1),
+        gain_mlp.reshape(1, -1),
         own,
         far,
-        gain_attn.reshape(1, -1),
-        gain_mlp.reshape(1, -1),
         *matrices,
     )
     there = swap(here)

time: 94.3 us -> 104 us (1.10)
  Pallas kernels: 31.6 us -> 37.9 us
  waiting for transfers between devices: 22.2 us -> 27.1 us
  starting transfers between devices: 20.2 us -> 17.6 us
    ppermute x7, waiting for transfers between devices: 16.6 us -> 21.2 us  [across(): lax.ppermute(values, 'shard', [(k, k ^ distance) for k in range(owner_cou...]
    pallas_call x1, Pallas kernels: 19.2 us -> 22.7 us  [on_device(): pl.pallas_call(functools.partial(compare_kernel, length, head_dim), out_s...]
    pallas_call x1 -> x2, Pallas kernels: 3.32 us -> 6.08 us  [pick(): pl.pallas_call(pick_kernel, out_shape=images(pair_count), in_specs=[smem,...]
    ppermute x7, starting transfers between devices: 12 us -> 9.76 us  [across(): lax.ppermute(values, 'shard', [(k, k ^ distance) for k in range(owner_cou...]
    unnamed x36 -> x34, local copies, waits for them, and re-layouts: 1.9 us -> 2.42 us
  transfers between devices with their start and end apart: 18 -> 18, of which waited for: 11 -> 10; matrix products, arithmetic and copies ran while one was open for 2% -> 2% of each run, Pallas kernels for 5% -> 6%
where the time goes in v6:
time: 104 us; the launch traced here: 103 us
  Pallas kernels  37.9 us (36%)
  waiting for transfers between devices  27.1 us (26%)
  starting transfers between devices  17.6 us (17%)
  blocking collectives  13.6 us (13%)
  other arithmetic  2.95 us (3%)
  local copies, waits for them, and re-layouts  2.42 us (2%)
  between operations  1.47 us (1%)
    pallas_call x1, Pallas kernels, on_device(): pl.pallas_call(functools.partial(compare_kernel, length, head_dim), out_s...  22.7 us
    ppermute x7, waiting for transfers between devices, across(): lax.ppermute(values, 'shard', [(k, k ^ distance) for k in range(owner_cou...  21.2 us
    all_to_all x1, blocking collectives, on_device(): lax.all_to_all(wanted, 'shard', split_axis=0, concat_axis=0, tiled=True)  13.6 us
    ppermute x7, starting transfers between devices, across(): lax.ppermute(values, 'shard', [(k, k ^ distance) for k in range(owner_cou...  9.76 us
    pallas_call x2, Pallas kernels, pick(): pl.pallas_call(pick_kernel, out_shape=images(pair_count), in_specs=[smem,...  6.08 us
    ppermute x9, waiting for transfers between devices, swap(): return lax.ppermute(values, 'mp', [(0, 1), (1, 0)])  5.01 us
    all_to_all x1, starting transfers between devices, on_device(): lax.all_to_all(served, 'shard', split_axis=0, concat_axis=0, tiled=True)  3.56 us
    pallas_call x1, Pallas kernels, on_device(): pl.pallas_call(functools.partial(serve_kernel, plan), out_shape=[images(o...  2.93 us
  transfers between devices with their start and end apart: 18, of which 10 were waited for; matrix products, arithmetic and copies ran while one was open for 2% of the time, Pallas kernels for 6%

profile of v6, /device:TPU:0, one launch (start us, length us, event | category | flops | bytes accessed | tf_op | source)
XLA Modules:
  0.0 103.1 jit_solution(15235271265858810961)
XLA Ops:
  0.0 1.8 %shard_map.118 = (s32[8,1,36]{2,1,0:T(1,128)}, s32[1,128]{1,0:T(1,128)}) custom-call(s32[1]{0:T(128)} %bitcast.2.shard_ref, s32[2,64]{1,0:T(2,128)} %bitcast.12, s32[2,64]{1,0:T(2,128)} %bitcast.13), custom_call_target="tpu_custom_call" | custom-call | tf_op jit(solution)/shard_map/pallas_call | solution.py:370
  1.8 13.6 %all_to_all.10.incoming_ref = s32[8,1,36]{2,1,0:T(1,128)} all-to-all(s32[8,1,36]{2,1,0:T(1,128)} %get-tuple-element.57), channel_id=1, replica_groups=mesh['groups'=2,'shard'=8,'mp'=2] {'shard'}, dimensions={0} | all-to-all | bytes 2304 | tf_op jit(solution)/shard_map/all_to_all | solution.py:378
  15.4 2.5 %shard_map.119 = (bf16[16,16,256]{2,1,0:T(8,128)(2,1)}, bf16[16,16,256]{2,1,0:T(8,128)(2,1)}, bf16[16,16,256]{2,1,0:T(8,128)(2,1)}, bf16[16,16,256]{2,1,0:T(8,128)(2,1)}) custom-call(s32[1]{0:T(128)} %bitcast.2.shard_ref, s32[8,1,36]{2,1,0:T(1,128)} %all_to_all.10.incoming_ref, bf16[256,16,256]{2,1,0:T(8,128)(2,1)} %tokens_ref.3), custom_call_target="tpu_custom_call" | custom-call | tf_op jit(solution)/shard_map/pallas_call | solution.py:380
  19.1 2.2 %collective-permute-start.3 = (bf16[16,16,256]{2,1,0:T(8,128)(2,1)}, bf16[16,16,256]{2,1,0:T(8,128)(2,1)S(1)}, u32[]{:S(2)}, u32[]{:S(2)}) collective-permute-start(bf16[16,16,256]{2,1,0:T(8,128)(2,1)} %get-tuple-element.71), channel_id=1, source_target_pairs={{0,6},{2,4},{4,2},{6,0},{8,14},{10,12},{12,10},{14,8},{1,7},{3,5},... | collective-permute-start | bytes 393224 | tf_op jit(solution)/shard_map/ppermute | solution.py:361
  21.3 2.9 %shard_map.120 = (bf16[8,16,16,256]{3,2,1,0:T(8,128)(2,1)}, bf16[16,16,256]{2,1,0:T(8,128)(2,1)}, bf16[16,16,256]{2,1,0:T(8,128)(2,1)}, bf16[16,16,256]{2,1,0:T(8,128)(2,1)}, bf16[16,16,256]{2,1,0:T(8,128)(2,1)}) custom-call(s32[1]{0:T(128)} %bitcast.2.shard_ref, s32[8,1,36]{2,1,0:T(1,128)} %all_to_all.10.incoming_ref, bf16[256,16,256]{2,1,0:T(8,128)(2,1)} %tokens_ref.3), custom_call_target="tpu_custom_call" | custom-call | tf_op jit(solution)/shard_map/pallas_call | solution.py:387
  24.4 1.6 %collective-permute-done.3.refs_3_ = bf16[16,16,256]{2,1,0:T(8,128)(2,1)S(1)} collective-permute-done((bf16[16,16,256]{2,1,0:T(8,128)(2,1)}, bf16[16,16,256]{2,1,0:T(8,128)(2,1)S(1)}, u32[]{:S(2)}, u32[]{:S(2)}) %collective-permute-start.3) | collective-permute-done | bytes 131104 | tf_op jit(solution)/shard_map/ppermute | solution.py:361
  26.7 1.9 %shard_map.121 = (bf16[32,16,256]{2,1,0:T(8,128)(2,1)}, bf16[32,16,256]{2,1,0:T(8,128)(2,1)S(1)}) custom-call(s32[1]{0:T(128)} %bitcast.2.shard_ref, s32[8,1,36]{2,1,0:T(1,128)} %all_to_all.10.incoming_ref, bf16[16,16,256]{2,1,0:T(8,128)(2,1)} %get-tuple-element.68.refs_0_, bf16[16,16,256]{2,1,0:T(8,128)(2,1)} %copy-done.5, bf16[16,16,256]{2,1,0:T(8,128)(2,1)} %copy-done.6, ...), custom_call_target="tpu_custom_call" | custom-call | tf_op jit(solution)/shard_map/pallas_call | solution.py:395
  28.7 3.6 %all-to-all-start.1 = ((bf16[8,16,16,256]{3,2,1,0:T(8,128)(2,1)}), bf16[8,16,16,256]{3,2,1,0:T(8,128)(2,1)S(1)}, u32[]{:S(2)}, u32[]{:S(2)}) async-start(bf16[8,16,16,256]{3,2,1,0:T(8,128)(2,1)} %get-tuple-element.74), calls=%async_computation.1 | async-start | bytes 2097152 | tf_op jit(solution)/shard_map/all_to_all | solution.py:403
  32.8 1.8 %collective-permute-start.4 = (bf16[16,16,256]{2,1,0:T(8,128)(2,1)S(1)}, bf16[16,16,256]{2,1,0:T(8,128)(2,1)S(1)}, u32[]{:S(2)}, u32[]{:S(2)}) collective-permute-start(bf16[16,16,256]{2,1,0:T(8,128)(2,1)S(1)} %copy-done.13), channel_id=1, source_target_pairs={{0,2},{2,0},{4,6},{6,4},{8,10},{10,8},{12,14},{14,12},{1,3},{3,1},... | collective-permute-start | bytes 393224 | tf_op jit(solution)/shard_map/ppermute | solution.py:361
  34.7 2.4 %collective-permute-start.7 = (bf16[32,16,256]{2,1,0:T(8,128)(2,1)}, bf16[32,16,256]{2,1,0:T(8,128)(2,1)S(1)}, u32[]{:S(2)}, u32[]{:S(2)}) collective-permute-start(bf16[32,16,256]{2,1,0:T(8,128)(2,1)} %get-tuple-element.79), channel_id=1, source_target_pairs={{0,8},{2,10},{4,12},{6,14},{8,0},{10,2},{12,4},{14,6},{1,9},{3,11}... | collective-permute-start | bytes 786440 | tf_op jit(solution)/shard_map/ppermute | solution.py:361
  38.7 2.8 %collective-permute-start.8 = (s32[]{:T(128)}, s32[]{:T(128)}, u32[]{:S(2)}, u32[]{:S(2)}) collective-permute-start(s32[]{:T(128)} %convert_element_type.6), channel_id=1, source_target_pairs={{0,16},{16,0},{1,17},{17,1},{2,18},{18,2},{3,19},{19,3},{4,20},{20... | collective-permute-start | bytes 20 | tf_op jit(solution)/shard_map/ppermute | solution.py:412
  41.5 0.9 collective-permute-done.8
  43.1 1.1 %collective-permute-done.15 = f32[4]{0:T(128)S(1)} collective-permute-done((f32[4]{0:T(128)S(1)}, f32[4]{0:T(128)S(1)}, u32[]{:S(2)}, u32[]{:S(2)}) %collective-permute-start.15) | collective-permute-done | bytes 48 | tf_op jit(solution)/shard_map/ppermute | solution.py:358
  44.4 1.0 collective-permute-done.14
  45.4 1.5 %collective-permute-start.5 = (bf16[16,16,256]{2,1,0:T(8,128)(2,1)}, bf16[16,16,256]{2,1,0:T(8,128)(2,1)S(1)}, u32[]{:S(2)}, u32[]{:S(2)}) collective-permute-start(bf16[16,16,256]{2,1,0:T(8,128)(2,1)} %get-tuple-element.77), channel_id=1, source_target_pairs={{0,4},{2,6},{4,0},{6,2},{8,12},{10,14},{12,8},{14,10},{1,5},{3,7},... | collective-permute-start | bytes 393224 | tf_op jit(solution)/shard_map/ppermute | solution.py:361
  47.4 9.8 %collective-permute-done.5.refs_3_ = bf16[16,16,256]{2,1,0:T(8,128)(2,1)S(1)} collective-permute-done((bf16[16,16,256]{2,1,0:T(8,128)(2,1)}, bf16[16,16,256]{2,1,0:T(8,128)(2,1)S(1)}, u32[]{:S(2)}, u32[]{:S(2)}) %collective-permute-start.5) | collective-permute-done | bytes 131104 | tf_op jit(solution)/shard_map/ppermute | solution.py:361
  57.3 1.4 %collective-permute-done.6.refs_4_ = bf16[16,16,256]{2,1,0:T(8,128)(2,1)S(1)} collective-permute-done((bf16[16,16,256]{2,1,0:T(8,128)(2,1)}, bf16[16,16,256]{2,1,0:T(8,128)(2,1)S(1)}, u32[]{:S(2)}, u32[]{:S(2)}) %collective-permute-start.6) | collective-permute-done | bytes 131104 | tf_op jit(solution)/shard_map/ppermute | solution.py:361
  58.7 8.2 %collective-permute-done.7.refs_5_ = bf16[32,16,256]{2,1,0:T(8,128)(2,1)S(1)} collective-permute-done((bf16[32,16,256]{2,1,0:T(8,128)(2,1)}, bf16[32,16,256]{2,1,0:T(8,128)(2,1)S(1)}, u32[]{:S(2)}, u32[]{:S(2)}) %collective-permute-start.7) | collective-permute-done | bytes 262176 | tf_op jit(solution)/shard_map/ppermute | solution.py:361
  66.9 1.9 %collective-permute-done.11.refs_7_ = bf16[256,512]{1,0:T(8,128)(2,1)} collective-permute-done((bf16[256,512]{1,0:T(8,128)(2,1)}, bf16[256,512]{1,0:T(8,128)(2,1)}, u32[]{:S(2)}, u32[]{:S(2)}) %collective-permute-start.11) | collective-permute-done | bytes 262176 | tf_op jit(solution)/shard_map/ppermute | solution.py:358
  68.8 0.9 copy-done
  69.8 3.0 %shard_map.123 = bf16[64,16,256]{2,1,0:T(8,128)(2,1)} custom-call(s32[1]{0:T(128)S(6)} %sub.3.core_ref, s32[1,128]{1,0:T(1,128)} %get-tuple-element.90.list_ref, bf16[128,16,256]{2,1,0:T(8,128)(2,1)} %bitcast.10, bf16[16,16,256]{2,1,0:T(8,128)(2,1)} %get-tuple-element.92.refs_1_, bf16[16,16,256]{2,1,0:T(8,128)(2,1)} %copy-done.2, ...), custom_call_target="tpu_custom_call" | custom-call | tf_op jit(solution)/shard_map/pallas_call | solution.py:423
  73.0 3.0 %shard_map.122.refs_0_ = bf16[64,16,256]{2,1,0:T(8,128)(2,1)} custom-call(s32[1]{0:T(128)} %bitcast.core_ref, s32[1,128]{1,0:T(1,128)} %get-tuple-element.90.list_ref, bf16[128,16,256]{2,1,0:T(8,128)(2,1)} %bitcast.11, bf16[16,16,256]{2,1,0:T(8,128)(2,1)} %get-tuple-element.92.refs_1_, bf16[16,16,256]{2,1,0:T(8,128)(2,1)} %copy-done.2, ...), custom_call_target="tpu_custom_call" | custom-call | tf_op jit(solution)/shard_map/pallas_call | solution.py:423
  77.5 22.7 %shard_map.124 = bf16[32,512]{1,0:T(8,128)(2,1)} custom-call(s32[1]{0:T(128)} %bitcast.core_ref, f32[8]{0:T(128)} %pad_maximum_fusion.1.scale_ref, f32[1,512]{1,0:T(1,128)} %bitcast.16, f32[1,512]{1,0:T(1,128)} %bitcast.17, bf16[64,16,256]{2,1,0:T(8,128)(2,1)} %shard_map.122.refs_0_, bf16[64,16,256]{2,1,0:T(8,128)(2,1)} %copy-done.10, ...), custom_call_target="tpu_custom_call" | custom-call | flops 3758096384 | bytes 8388608 | tf_op jit(solution)/shard_map/pallas_call | solution.py:439
  100.6 1.1 %collective-permute-done.17 = bf16[32,512]{1,0:T(8,128)(2,1)S(1)} collective-permute-done((bf16[32,512]{1,0:T(8,128)(2,1)}, bf16[32,512]{1,0:T(8,128)(2,1)S(1)}, u32[]{:S(2)}, u32[]{:S(2)}) %collective-permute-start.17) | collective-permute-done | bytes 32800 | tf_op jit(solution)/shard_map/ppermute | solution.py:358
  (60 shorter events, 7.9 us)
Async XLA Ops:
  17.8 19.2 %copy-start.8 = (s32[8,1,36]{2,1,0:T(1,128)S(1)}, s32[8,1,36]{2,1,0:T(1,128)}, u32[]{:S(2)}) copy-start(s32[8,1,36]{2,1,0:T(1,128)} %all_to_all.10.incoming_ref) | copy-start | bytes 3460
  17.8 6.6 %collective-permute-start.1 = (bf16[16,16,256]{2,1,0:T(8,128)(2,1)}, bf16[16,16,256]{2,1,0:T(8,128)(2,1)S(1)}, u32[]{:S(2)}, u32[]{:S(2)}) collective-permute-start(bf16[16,16,256]{2,1,0:T(8,128)(2,1)} %get-tuple-element.69), channel_id=1, source_target_pairs={{0,2},{2,0},{4,6},{6,4},{8,10},{10,8},{12,14},{14,12},{1,3},{3,1},... | collective-permute-start | bytes 393224 | tf_op jit(solution)/shard_map/ppermute | solution.py:361
  18.6 5.9 %collective-permute-start.2 = (bf16[16,16,256]{2,1,0:T(8,128)(2,1)}, bf16[16,16,256]{2,1,0:T(8,128)(2,1)S(1)}, u32[]{:S(2)}, u32[]{:S(2)}) collective-permute-start(bf16[16,16,256]{2,1,0:T(8,128)(2,1)} %get-tuple-element.70), channel_id=1, source_target_pairs={{0,4},{2,6},{4,0},{6,2},{8,12},{10,14},{12,8},{14,10},{1,5},{3,7},... | collective-permute-start | bytes 393224 | tf_op jit(solution)/shard_map/ppermute | solution.py:361
  19.1 6.9 %collective-permute-start.3 = (bf16[16,16,256]{2,1,0:T(8,128)(2,1)}, bf16[16,16,256]{2,1,0:T(8,128)(2,1)S(1)}, u32[]{:S(2)}, u32[]{:S(2)}) collective-permute-start(bf16[16,16,256]{2,1,0:T(8,128)(2,1)} %get-tuple-element.71), channel_id=1, source_target_pairs={{0,6},{2,4},{4,2},{6,0},{8,14},{10,12},{12,10},{14,8},{1,7},{3,5},... | collective-permute-start | bytes 393224 | tf_op jit(solution)/shard_map/ppermute | solution.py:361
  24.3 19.9 %copy-start.14 = (f32[1024]{0:T(1024)S(1)}, f32[1024]{0:T(1024)}, u32[]{:S(2)}) copy-start(f32[1024]{0:T(1024)} %param.24) | copy-start | bytes 12292
  24.3 33.0 %copy-start.11 = (bf16[512,256]{1,0:T(8,128)(2,1)S(1)}, bf16[512,256]{1,0:T(8,128)(2,1)}, u32[]{:S(2)}) copy-start(bf16[512,256]{1,0:T(8,128)(2,1)} %refs_2_.1) | copy-start | bytes 786436
  24.3 34.4 %copy-start.12 = (bf16[512,256]{1,0:T(8,128)(2,1)S(1)}, bf16[512,256]{1,0:T(8,128)(2,1)}, u32[]{:S(2)}) copy-start(bf16[512,256]{1,0:T(8,128)(2,1)} %refs_4_.1) | copy-start | bytes 786436
  28.7 40.1 %all-to-all-start.1 = ((bf16[8,16,16,256]{3,2,1,0:T(8,128)(2,1)}), bf16[8,16,16,256]{3,2,1,0:T(8,128)(2,1)S(1)}, u32[]{:S(2)}, u32[]{:S(2)}) async-start(bf16[8,16,16,256]{3,2,1,0:T(8,128)(2,1)} %get-tuple-element.74), calls=%async_computation.1 | async-start | bytes 2097152 | tf_op jit(solution)/shard_map/all_to_all | solution.py:403
  32.2 36.5 %collective-permute-start.12 = (bf16[512,1024]{1,0:T(8,128)(2,1)S(1)}, bf16[512,1024]{1,0:T(8,128)(2,1)}, u32[]{:S(2)}, u32[]{:S(2)}) collective-permute-start(bf16[512,1024]{1,0:T(8,128)(2,1)S(1)} %copy-done.9), channel_id=1, source_target_pairs={{0,1},{1,0},{2,3},{3,2},{4,5},{5,4},{6,7},{7,6},{8,9},{9,8},{10,11... | collective-permute-start | bytes 3145736 | tf_op jit(solution)/shard_map/ppermute | solution.py:358
  32.3 36.5 %collective-permute-start.13 = (bf16[1024,512]{1,0:T(8,128)(2,1)}, bf16[1024,512]{1,0:T(8,128)(2,1)}, u32[]{:S(2)}, u32[]{:S(2)}) collective-permute-start(bf16[1024,512]{1,0:T(8,128)(2,1)} %refs_12_.1), channel_id=1, source_target_pairs={{0,1},{1,0},{2,3},{3,2},{4,5},{5,4},{6,7},{7,6},{8,9},{9,8},{10,11... | collective-permute-start | bytes 3145736 | tf_op jit(solution)/shard_map/ppermute | solution.py:358
  32.8 14.0 %collective-permute-start.4 = (bf16[16,16,256]{2,1,0:T(8,128)(2,1)S(1)}, bf16[16,16,256]{2,1,0:T(8,128)(2,1)S(1)}, u32[]{:S(2)}, u32[]{:S(2)}) collective-permute-start(bf16[16,16,256]{2,1,0:T(8,128)(2,1)S(1)} %copy-done.13), channel_id=1, source_target_pairs={{0,2},{2,0},{4,6},{6,4},{8,10},{10,8},{12,14},{14,12},{1,3},{3,1},... | collective-permute-start | bytes 393224 | tf_op jit(solution)/shard_map/ppermute | solution.py:361
  34.7 32.2 %collective-permute-start.7 = (bf16[32,16,256]{2,1,0:T(8,128)(2,1)}, bf16[32,16,256]{2,1,0:T(8,128)(2,1)S(1)}, u32[]{:S(2)}, u32[]{:S(2)}) collective-permute-start(bf16[32,16,256]{2,1,0:T(8,128)(2,1)} %get-tuple-element.79), channel_id=1, source_target_pairs={{0,8},{2,10},{4,12},{6,14},{8,0},{10,2},{12,4},{14,6},{1,9},{3,11}... | collective-permute-start | bytes 786440 | tf_op jit(solution)/shard_map/ppermute | solution.py:361
  38.7 3.7 %collective-permute-start.8 = (s32[]{:T(128)}, s32[]{:T(128)}, u32[]{:S(2)}, u32[]{:S(2)}) collective-permute-start(s32[]{:T(128)} %convert_element_type.6), channel_id=1, source_target_pairs={{0,16},{16,0},{1,17},{17,1},{2,18},{18,2},{3,19},{19,3},{4,20},{20... | collective-permute-start | bytes 20 | tf_op jit(solution)/shard_map/ppermute | solution.py:412
  43.0 1.2 %collective-permute-start.15 = (f32[4]{0:T(128)S(1)}, f32[4]{0:T(128)S(1)}, u32[]{:S(2)}, u32[]{:S(2)}) collective-permute-start(f32[4]{0:T(128)S(1)} %copy-done.16), channel_id=1, source_target_pairs={{0,1},{1,0},{2,3},{3,2},{4,5},{5,4},{6,7},{7,6},{8,9},{9,8},{10,11... | collective-permute-start | bytes 56 | tf_op jit(solution)/shard_map/ppermute | solution.py:358
  44.2 1.2 %collective-permute-start.14 = (f32[1024]{0:T(1024)S(1)}, f32[1024]{0:T(1024)S(1)}, u32[]{:S(2)}, u32[]{:S(2)}) collective-permute-start(f32[1024]{0:T(1024)S(1)} %copy-done.14), channel_id=1, source_target_pairs={{0,1},{1,0},{2,3},{3,2},{4,5},{5,4},{6,7},{7,6},{8,9},{9,8},{10,11... | collective-permute-start | bytes 12296 | tf_op jit(solution)/shard_map/ppermute | solution.py:358
  45.4 30.7 %copy-start.15 = (f32[1024]{0:T(1024)}, f32[1024]{0:T(1024)S(1)}, u32[]{:S(2)}) copy-start(f32[1024]{0:T(1024)S(1)} %collective-permute-done.14) | copy-start | bytes 12292
  45.4 11.9 %collective-permute-start.5 = (bf16[16,16,256]{2,1,0:T(8,128)(2,1)}, bf16[16,16,256]{2,1,0:T(8,128)(2,1)S(1)}, u32[]{:S(2)}, u32[]{:S(2)}) collective-permute-start(bf16[16,16,256]{2,1,0:T(8,128)(2,1)} %get-tuple-element.77), channel_id=1, source_target_pairs={{0,4},{2,6},{4,0},{6,2},{8,12},{10,14},{12,8},{14,10},{1,5},{3,7},... | collective-permute-start | bytes 393224 | tf_op jit(solution)/shard_map/ppermute | solution.py:361
  46.9 21.9 %copy-start.2 = (bf16[16,16,256]{2,1,0:T(8,128)(2,1)}, bf16[16,16,256]{2,1,0:T(8,128)(2,1)S(1)}, u32[]{:S(2)}) copy-start(bf16[16,16,256]{2,1,0:T(8,128)(2,1)S(1)} %collective-permute-done.4.refs_2_) | copy-start | bytes 393220
  46.9 11.8 %collective-permute-start.6 = (bf16[16,16,256]{2,1,0:T(8,128)(2,1)}, bf16[16,16,256]{2,1,0:T(8,128)(2,1)S(1)}, u32[]{:S(2)}, u32[]{:S(2)}) collective-permute-start(bf16[16,16,256]{2,1,0:T(8,128)(2,1)} %get-tuple-element.78), channel_id=1, source_target_pairs={{0,6},{2,4},{4,2},{6,0},{8,14},{10,12},{12,10},{14,8},{1,7},{3,5},... | collective-permute-start | bytes 393224 | tf_op jit(solution)/shard_map/ppermute | solution.py:361
  57.3 9.6 %collective-permute-start.9 = (bf16[512,256]{1,0:T(8,128)(2,1)S(1)}, bf16[512,256]{1,0:T(8,128)(2,1)}, u32[]{:S(2)}, u32[]{:S(2)}) collective-permute-start(bf16[512,256]{1,0:T(8,128)(2,1)S(1)} %copy-done.11), channel_id=1, source_target_pairs={{0,1},{1,0},{2,3},{3,2},{4,5},{5,4},{6,7},{7,6},{8,9},{9,8},{10,11... | collective-permute-start | bytes 786440 | tf_op jit(solution)/shard_map/ppermute | solution.py:358
  58.7 8.2 %collective-permute-start.10 = (bf16[512,256]{1,0:T(8,128)(2,1)S(1)}, bf16[512,256]{1,0:T(8,128)(2,1)}, u32[]{:S(2)}, u32[]{:S(2)}) collective-permute-start(bf16[512,256]{1,0:T(8,128)(2,1)S(1)} %copy-done.12), channel_id=1, source_target_pairs={{0,1},{1,0},{2,3},{3,2},{4,5},{5,4},{6,7},{7,6},{8,9},{9,8},{10,11... | collective-permute-start | bytes 786440 | tf_op jit(solution)/shard_map/ppermute | solution.py:358
  66.9 1.9 %collective-permute-start.11 = (bf16[256,512]{1,0:T(8,128)(2,1)}, bf16[256,512]{1,0:T(8,128)(2,1)}, u32[]{:S(2)}, u32[]{:S(2)}) collective-permute-start(bf16[256,512]{1,0:T(8,128)(2,1)} %refs_6_.1), channel_id=1, source_target_pairs={{0,1},{1,0},{2,3},{3,2},{4,5},{5,4},{6,7},{7,6},{8,9},{9,8},{10,11... | collective-permute-start | bytes 786440 | tf_op jit(solution)/shard_map/ppermute | solution.py:358
  72.8 3.9 %collective-permute-start.16 = (bf16[64,16,256]{2,1,0:T(8,128)(2,1)}, bf16[64,16,256]{2,1,0:T(8,128)(2,1)S(1)}, u32[]{:S(2)}, u32[]{:S(2)}) collective-permute-start(bf16[64,16,256]{2,1,0:T(8,128)(2,1)} %shard_map.123), channel_id=1, source_target_pairs={{0,1},{1,0},{2,3},{3,2},{4,5},{5,4},{6,7},{7,6},{8,9},{9,8},{10,11... | collective-permute-start | bytes 1572872 | tf_op jit(solution)/shard_map/ppermute | solution.py:358
  100.2 1.5 %collective-permute-start.17 = (bf16[32,512]{1,0:T(8,128)(2,1)}, bf16[32,512]{1,0:T(8,128)(2,1)S(1)}, u32[]{:S(2)}, u32[]{:S(2)}) collective-permute-start(bf16[32,512]{1,0:T(8,128)(2,1)} %shard_map.124), channel_id=1, source_target_pairs={{0,1},{1,0},{2,3},{3,2},{4,5},{5,4},{6,7},{7,6},{8,9},{9,8},{10,11... | collective-permute-start | bytes 98312 | tf_op jit(solution)/shard_map/ppermute | solution.py:358
  (11 other events, 71.0 us)

commit v7 on v6

--- a/solution.py
+++ b/solution.py
@@ -99,17 +99,14 @@
     lax.fori_loop(0, count, copy, 0, unroll=min(16, count))
 
 
-def serve_relays_kernel(plan, shard_ref, incoming_ref, tokens_ref, *served_refs):
-    for distance, served_ref in enumerate(served_refs):
-        requester = shard_ref[0] ^ (distance + plan.half)
-        serve(tokens_ref, incoming_ref, requester, plan.base, served_ref)
-
-
-def serve_kernel(plan, shard_ref, incoming_ref, tokens_ref, served_ref, *near_refs):
+def serve_kernel(plan, incoming_ref, tokens_ref, served_ref):
     for requester in range(plan.owners):
         serve(tokens_ref, incoming_ref, requester, 0, served_ref.at[requester])
-    for distance, near_ref in enumerate(near_refs):
-        serve(tokens_ref, incoming_ref, shard_ref[0] ^ distance, plan.base, near_ref)
+
+
+def serve_rest_kernel(plan, shift, shard_ref, incoming_ref, tokens_ref, *served_refs):
+    for distance, served_ref in enumerate(served_refs):
+        serve(tokens_ref, incoming_ref, shard_ref[0] ^ (distance + shift), plan.base, served_ref)
 
 
 def relay_kernel(plan, shard_ref, incoming_ref, *refs):
@@ -166,15 +163,15 @@
     length,
     head_dim,
     core_ref,
-    scale_ref,
+    scale_a_ref,
+    scale_b_ref,
     gain_attn_ref,
     gain_mlp_ref,
     *refs,
 ):
     own_held_ref, far_held_ref, *held_refs = refs[:14]
     result_ref, qkv_ref, out_ref, in_ref, back_ref, bias_ref = refs[14:20]
-    tokens_ref, normed_ref, heads_ref, mixed_ref, hidden_ref = refs[20:25]
-    inner_ref, bent_ref, pooled_ref, mean_ref, sems, token_sems = refs[25:]
+    tokens_ref, pooled_ref, mean_ref, sems, token_sems = refs[20:]
     width, units = in_ref.shape
     wide = width // 2
     homes = [qkv_ref.at[:, pl.ds(k * wide, wide)] for k in range(4)]
@@ -199,6 +196,8 @@
     blocks = count // BLOCK
     tile = 256
     pair_dim = 2 * head_dim
+    scale_refs = (scale_a_ref, scale_b_ref)
+    per_core = width // head_dim // 2
     even = lax.broadcasted_iota(jnp.int32, (half, pair_dim), 1) < head_dim
     same = (
         lax.broadcasted_iota(jnp.int32, (half, half), 0) // length
@@ -215,23 +214,6 @@
         )
 
     ones = split(jnp.ones((half, pair_dim), jnp.bfloat16))
-
-    def begin(step, carry):
-        images = pl.ds(step * 2, 2)
-        here = span(step, 2 * length)
-        tokens = [
-            tokens_ref[k, images].reshape(2 * length, -1).astype(jnp.float32) for k in range(2)
-        ]
-        tokens = jnp.concatenate(tokens, axis=1)
-        hidden_ref[here, :] = tokens
-        normed_ref[here, :] = norm_rows(tokens, gain_attn_ref[...]).astype(jnp.bfloat16)
-        return carry
-
-    def project(step, carry):
-        here = span(step // 4, rows)
-        cut = span(step % 4, 2 * width // 4)
-        heads_ref[here, cut] = dot(normed_ref[here, :], qkv_ref[:, cut]).astype(jnp.bfloat16)
-        return carry
 
     def weigh(scores, factor):
         scores = jnp.where(same, scores, -1e30)
@@ -247,77 +229,53 @@
         inverse = inverse * (2.0 - total * inverse)
         return (mixed[:, :pair_dim] * inverse).astype(jnp.bfloat16)
 
-    def attend(step, carry):
+    row_pair = lax.broadcasted_iota(jnp.int32, (2 * BLOCK, rows), 1) % half // length
+    pool = jnp.where(row_pair == lax.broadcasted_iota(jnp.int32, row_pair.shape, 0), 1.0, 0.0)
+    pool = pool.astype(jnp.bfloat16)
+
+    def arrive(step, copies):
+        @pl.when(step == 0)
+        def _():
+            for copy in copies:
+                copy.wait()
+
+    def block(step, carry):
+        images = pl.ds(step * 2 * BLOCK, 2 * BLOCK)
+        hidden = jnp.concatenate(
+            [tokens_ref[k, images].reshape(rows, -1).astype(jnp.float32) for k in range(2)], axis=1
+        )
+        normed = norm_rows(hidden, gain_attn_ref[...]).astype(jnp.bfloat16)
+        arrive(step, loads[:4])
+        query = dot(normed, qkv_ref[:, :width]).astype(jnp.bfloat16)
+        value = dot(normed, qkv_ref[:, width:]).astype(jnp.bfloat16)
+        mixed = []
         for index in range(width // pair_dim):
-            factors = [scale_ref[2 * index + k] * (LOG2E / head_dim**0.5) for k in range(2)]
+            factors = [scale_refs[k // per_core][k % per_core] for k in (2 * index, 2 * index + 1)]
+            factors = [factor * (LOG2E / head_dim**0.5) for factor in factors]
             cut = slice(index * pair_dim, (index + 1) * pair_dim)
-            beyond = slice(width + cut.start, width + cut.stop)
-            sides = [span(2 * step + k, half) for k in range(2)]
-            query = [heads_ref[side, cut] for side in sides]
-            value = [heads_ref[side, beyond] for side in sides]
-            for k in range(2):
-                mixed_ref[sides[k], cut] = mix(query[k], query[1 - k], value[1 - k], factors)
-        return carry
-
-    def join(step, carry):
-        here = span(step // 2, rows)
-        cut = span(step % 2, width // 2)
-        hidden_ref[here, cut] += dot(mixed_ref[here, :], out_ref[:, cut])
-        return carry
-
-    def middle(step, carry):
-        total = 0.0
-        for side in range(2):
-            at = (step // BLOCK * 2 + side) * BLOCK + step % BLOCK
-            here = span(at, length)
-            hidden = hidden_ref[here, :]
-            total = total + jnp.sum(hidden, axis=0, keepdims=True)
-            normed_ref[here, :] = norm_rows(hidden, gain_mlp_ref[...]).astype(jnp.bfloat16)
-        mean_ref[pl.ds(step, 1), :] = total
-        return carry
-
-    long = inner_ref.shape[1]
-    pairs = long // (2 * length)
-    row = lax.broadcasted_iota(jnp.int32, (pairs, long), 1)
-    row_pair = row // rows * BLOCK + row % half // length
-    pool = jnp.where(row_pair == lax.broadcasted_iota(jnp.int32, row.shape, 0), 1.0, 0.0)
-    pool = pool.astype(jnp.bfloat16)
-    tiles = units // tile
-    steps = count // pairs * tiles
-    piece = 32
-
-    def expand(step, carry):
-        new = lax.rem(step, steps)
-        here = span(new // tiles, long)
-        cut = span(lax.rem(new, tiles), tile)
-        inner_ref[lax.rem(step, 2)] = dot(normed_ref[here, :], in_ref[:, cut])
-        pooled = dot(pool, bent_ref[lax.rem(step, 2)])
-        last = lax.rem(step + steps - 1, steps)
-        bias = bias_ref[:, span(lax.rem(last, tiles), tile)]
-        for at in range(0, long, piece):
-            inner = inner_ref[lax.rem(step + 1, 2), at : at + piece, :] + bias
-            inner = inner.astype(jnp.bfloat16)
-            cubic = inner * inner * jnp.bfloat16(0.0356774081) + jnp.bfloat16(0.7978845608)
-            bent = (jnp.tanh(inner * cubic) + jnp.bfloat16(1.0)) * inner
-            bent_ref[lax.rem(step + 1, 2), at : at + piece, :] = bent
-        old = lax.rem(step + steps - 2, steps)
-        pooled_ref[span(old // tiles, pairs), span(lax.rem(old, tiles), tile)] = pooled
+            sides = [slice(0, half), slice(half, rows)]
+            both = [
+                mix(query[sides[k], cut], query[sides[1 - k], cut], value[sides[1 - k], cut], factors)
+                for k in range(2)
+            ]
+            mixed.append(jnp.concatenate(both, axis=0))
+        arrive(step, loads[4:6])
+        hidden = hidden + dot(jnp.concatenate(mixed, axis=1), out_ref[...])
+        here = span(step, BLOCK)
+        mean_ref[here, :] = jnp.sum(hidden.reshape(2, BLOCK, length, -1), axis=(0, 2))
+        normed = norm_rows(hidden, gain_mlp_ref[...]).astype(jnp.bfloat16)
+        arrive(step, loads[6:10])
+        for at in range(0, units, tile):
+            cut = slice(at, at + tile)
+            inner = dot(normed, in_ref[:, cut]) + bias_ref[:, cut]
+            bent = jnp.tanh(inner * (0.7978845608028654 + 0.035677408136300125 * (inner * inner)))
+            bent = (inner * bent + inner).astype(jnp.bfloat16)
+            pooled_ref[here, cut] = dot(pool, bent)[:BLOCK]
         return carry
 
     for load in token_loads:
         load.wait()
-    lax.fori_loop(0, count, begin, 0, unroll=8)
-    for load in loads[:4]:
-        load.wait()
-    lax.fori_loop(0, blocks * 4, project, 0, unroll=2)
-    lax.fori_loop(0, blocks, attend, 0)
-    for load in loads[4:6]:
-        load.wait()
-    lax.fori_loop(0, blocks * 2, join, 0, unroll=2)
-    lax.fori_loop(0, count, middle, 0, unroll=8)
-    for load in loads[6:10]:
-        load.wait()
-    lax.fori_loop(0, steps + 2, expand, 0)
+    lax.fori_loop(0, blocks, block, 0)
     for load in loads[10:]:
         load.wait()
     pooled = pooled_ref[...] * (0.25 / length)
@@ -326,6 +284,13 @@
     back = dot(jnp.concatenate([coarse, fine], axis=0), back_ref[...])
     mean = mean_ref[...] * (0.5 / length)
     result_ref[...] = (mean + back[:count] + back[count:]).astype(jnp.bfloat16)
+
+
+def join_kernel(core_ref, here_ref, there_ref, result_ref):
+    count = here_ref.shape[0]
+    start = pl.multiple_of(core_ref[0] * count, count)
+    result_ref[pl.ds(start, count), :] = here_ref[...]
+    result_ref[pl.ds(pl.multiple_of(count - start, count), count), :] = there_ref[...]
 
 
 def on_device(
@@ -376,34 +341,35 @@
         in_specs=[smem, vmem, vmem],
     )(shard, pair_owner.T, pair_slot.T)
     incoming = lax.all_to_all(wanted, "shard", split_axis=0, concat_axis=0, tiled=True)
-    if plan.extra:
-        chunks = pl.pallas_call(
-            functools.partial(serve_relays_kernel, plan),
-            out_shape=[images(plan.extra)] * plan.half,
-            in_specs=[smem, smem, vmem],
-        )(shard, incoming, image_tokens)
-        incoming, chunks = lax.optimization_barrier((incoming, chunks))
-        chunks = [chunks[0]] + [across(chunks[k], k) for k in range(1, plan.half)]
-    served, *near = pl.pallas_call(
+    served = pl.pallas_call(
         functools.partial(serve_kernel, plan),
-        out_shape=[images(owner_count, plan.base)]
-        + [images(plan.extra)] * (plan.half if plan.extra else 0),
-        in_specs=[smem, smem, vmem],
-    )(shard, incoming, image_tokens)
+        out_shape=images(owner_count, plan.base),
+        in_specs=[smem, vmem],
+    )(incoming, image_tokens)
+    returned = lax.all_to_all(served, "shard", split_axis=0, concat_axis=0, tiled=True)
+    sources = [returned.reshape(-1, length, features)]
     weights = (w_qk, w_value, w_out, w_in, w_back, bias_in, logit_scale)
     if plan.extra:
+
+        def serve_rest(shift, incoming):
+            return pl.pallas_call(
+                functools.partial(serve_rest_kernel, plan, shift),
+                out_shape=[images(plan.extra)] * plan.half,
+                in_specs=[smem, smem, vmem],
+            )(shard, incoming, image_tokens)
+
+        incoming, served = lax.optimization_barrier((incoming, served))
+        chunks = serve_rest(plan.half, incoming)
+        chunks, weights = lax.optimization_barrier((chunks, weights))
+        chunks = [chunks[0]] + [across(chunks[k], k) for k in range(1, plan.half)]
         first, second = pl.pallas_call(
             functools.partial(relay_kernel, plan),
             out_shape=[images(plan.part)] * 2,
             in_specs=[smem, smem] + [vmem] * plan.half,
         )(shard, incoming, *chunks)
-        served, near, first, second, incoming, weights = lax.optimization_barrier(
-            (served, near, first, second, incoming, weights)
-        )
-    returned = lax.all_to_all(served, "shard", split_axis=0, concat_axis=0, tiled=True)
-    sources = [returned.reshape(-1, length, features)]
-    if plan.extra:
+        first, second, incoming = lax.optimization_barrier((first, second, incoming))
         first = across(first, plan.half)
+        near = serve_rest(0, incoming)
         near = [near[0]] + [across(near[k], k) for k in range(1, plan.half)]
         crowded = jnp.max(jnp.sum(incoming[:, 0, plan.capacity :], axis=1)) > plan.part
         crowded = crowded.astype(jnp.int32)
@@ -411,12 +377,15 @@
         for _ in range(groups - 1):
             passed = lax.ppermute(passed, "groups", [(k, (k + 1) % groups) for k in range(groups)])
             crowded = jnp.maximum(crowded, passed)
+        sources += [*near, first]
+    swapped = [swap(w) for w in weights]
+    sources, swapped = lax.optimization_barrier((sources, swapped))
+    if plan.extra:
+        second, sources = lax.optimization_barrier((second, sources))
         second = lax.cond(
             crowded > 0, lambda part: across(part, plan.half), lambda part: part, second
         )
-        sources += [*near, first, second]
-    swapped = [swap(w) for w in weights]
-    sources, swapped = lax.optimization_barrier((sources, swapped))
+        sources = [*sources, second]
     far_qk, far_value, far_out, far_in, far_back, far_bias, far_scale = swapped
 
     def pick(core):
@@ -435,11 +404,10 @@
     matrices = [w_qk, far_qk, w_value, far_value, w_out, far_out, w_in, far_in]
     matrices += [bias_in.reshape(1, -1), far_bias.reshape(1, -1), w_back, far_back]
     token_count = pair_count * length
-    long = token_count // 2
     here = pl.pallas_call(
         functools.partial(compare_kernel, length, head_dim),
         out_shape=jax.ShapeDtypeStruct((mine, width), jnp.bfloat16),
-        in_specs=[smem] * 2 + [vmem] * 2 + [hbm] * 14,
+        in_specs=[smem] * 3 + [vmem] * 2 + [hbm] * 14,
         out_specs=vmem,
         scratch_shapes=[
             pltpu.VMEM((width, 2 * width), jnp.bfloat16),
@@ -448,12 +416,6 @@
             pltpu.VMEM((units, width), jnp.bfloat16),
             pltpu.VMEM((1, units), jnp.float32),
             pltpu.VMEM((2, pair_count, length, features), jnp.bfloat16),
-            pltpu.VMEM((token_count, width), jnp.bfloat16),
-            pltpu.VMEM((token_count, 2 * width), jnp.bfloat16),
-            pltpu.VMEM((token_count, width), jnp.bfloat16),
-            pltpu.VMEM((token_count, width), jnp.float32),
-            pltpu.VMEM((2, long, 256), jnp.float32),
-            pltpu.VMEM((2, long, 256), jnp.bfloat16),
             pltpu.VMEM((mine, units), jnp.float32),
             pltpu.VMEM((mine, width), jnp.float32),
             pltpu.SemaphoreType.DMA((12,)),
@@ -467,7 +429,8 @@
         ),
     )(
         core,
-        jnp.concatenate([logit_scale, far_scale]),
+        logit_scale,
+        far_scale,
         gain_attn.reshape(1, -1),
         gain_mlp.reshape(1, -1),
         own,
@@ -475,9 +438,11 @@
         *matrices,
     )
     there = swap(here)
-    low = jnp.where(core == 0, here, there)
-    high = jnp.where(core == 0, there, here)
-    return jnp.concatenate([low, high], axis=0)
+    return pl.pallas_call(
+        join_kernel,
+        out_shape=jax.ShapeDtypeStruct((pair_count, width), jnp.bfloat16),
+        in_specs=[smem, vmem, vmem],
+    )(core, here, there)
 
 
 def solution(mesh):

time: 104 us -> 109 us (1.048)
  Pallas kernels: 37.9 us -> 40.4 us
  other arithmetic: 2.95 us -> 0.95 us
  starting transfers between devices: 17.6 us -> 19.3 us
  waiting for transfers between devices: 27.1 us -> 28.7 us
  local copies, waits for them, and re-layouts: 2.42 us -> 3.85 us
    ppermute x7, waiting for transfers between devices: 21.2 us -> 26.7 us  [across(): lax.ppermute(values, 'shard', [(k, k ^ distance) for k in range(owner_cou...]
    ppermute x9, waiting for transfers between devices: 5.01 us -> 1.09 us  [swap(): return lax.ppermute(values, 'mp', [(0, 1), (1, 0)])]
    pallas_call x2 -> x4, Pallas kernels: 5.4 us -> 9.06 us  [the longest x2 4.97 us: serve_rest(): pl.pallas_call(functools.partial(serve_rest_kernel, plan, shift), out_sha...]
    ppermute x7, starting transfers between devices: 9.76 us -> 11.6 us  [across(): lax.ppermute(values, 'shard', [(k, k ^ distance) for k in range(owner_cou...]
    unnamed x34 -> x38, local copies, waits for them, and re-layouts: 2.42 us -> 3.85 us
    concatenate x2 -> x0, other arithmetic: 1.24 us -> none  [the longest x1 0.64 us: on_device(): return jnp.concatenate([low, high], axis=0)]
    pallas_call x1, Pallas kernels: 22.7 us -> 21.5 us  [on_device(): pl.pallas_call(functools.partial(compare_kernel, length, head_dim), out_s...]
  transfers between devices with their start and end apart: 18 -> 18, of which waited for: 10 -> 8; matrix products, arithmetic and copies ran while one was open for 2% -> 1% of each run, Pallas kernels for 6% -> 9%
where the time goes in v7:
time: 109 us; the launch traced here: 108 us
  Pallas kernels  40.4 us (37%)
  waiting for transfers between devices  28.7 us (26%)
  starting transfers between devices  19.3 us (18%)
  blocking collectives  13.6 us (12%)
  local copies, waits for them, and re-layouts  3.85 us (4%)
  between operations  1.52 us (1%)
    ppermute x7, waiting for transfers between devices, across(): lax.ppermute(values, 'shard', [(k, k ^ distance) for k in range(owner_cou...  26.7 us
    pallas_call x1, Pallas kernels, on_device(): pl.pallas_call(functools.partial(compare_kernel, length, head_dim), out_s...  21.5 us
    all_to_all x1, blocking collectives, on_device(): lax.all_to_all(wanted, 'shard', split_axis=0, concat_axis=0, tiled=True)  13.6 us
    ppermute x7, starting transfers between devices, across(): lax.ppermute(values, 'shard', [(k, k ^ distance) for k in range(owner_cou...  11.6 us
    pallas_call x2, Pallas kernels, pick(): pl.pallas_call(pick_kernel, out_shape=images(pair_count), in_specs=[smem,...  6.08 us
    pallas_call x2, Pallas kernels, serve_rest(): pl.pallas_call(functools.partial(serve_rest_kernel, plan, shift), out_sha...  4.97 us
    unnamed x38, local copies, waits for them, and re-layouts  3.85 us
    all_to_all x1, starting transfers between devices, on_device(): lax.all_to_all(served, 'shard', split_axis=0, concat_axis=0, tiled=True)  3.7 us
  transfers between devices with their start and end apart: 18, of which 8 were waited for; matrix products, arithmetic and copies ran while one was open for 1% of the time, Pallas kernels for 9%

profile of v7, /device:TPU:0, one launch (start us, length us, event | category | flops | bytes accessed | tf_op | source)
XLA Modules:
  0.0 108.4 jit_solution(3232785409213658478)
XLA Ops:
  0.0 1.8 %shard_map.118 = (s32[8,1,36]{2,1,0:T(1,128)}, s32[1,128]{1,0:T(1,128)}) custom-call(s32[1]{0:T(128)} %bitcast.1.shard_ref, s32[2,64]{1,0:T(2,128)} %bitcast.11, s32[2,64]{1,0:T(2,128)} %bitcast.12), custom_call_target="tpu_custom_call" | custom-call | tf_op jit(solution)/shard_map/pallas_call | solution.py:335
  1.8 13.6 %all_to_all.10.incoming_ref = s32[8,1,36]{2,1,0:T(1,128)} all-to-all(s32[8,1,36]{2,1,0:T(1,128)} %get-tuple-element.57), channel_id=1, replica_groups=mesh['groups'=2,'shard'=8,'mp'=2] {'shard'}, dimensions={0} | all-to-all | bytes 2304 | tf_op jit(solution)/shard_map/all_to_all | solution.py:343
  15.4 2.7 %shard_map.119 = bf16[8,16,16,256]{3,2,1,0:T(8,128)(2,1)} custom-call(s32[8,1,36]{2,1,0:T(1,128)} %all_to_all.10.incoming_ref, bf16[256,16,256]{2,1,0:T(8,128)(2,1)} %tokens_ref.5), custom_call_target="tpu_custom_call" | custom-call | tf_op jit(solution)/shard_map/pallas_call | solution.py:344
  18.1 3.7 %all-to-all-start.1 = ((bf16[8,16,16,256]{3,2,1,0:T(8,128)(2,1)}), bf16[8,16,16,256]{3,2,1,0:T(8,128)(2,1)S(1)}, u32[]{:S(2)}, u32[]{:S(2)}) async-start(bf16[8,16,16,256]{3,2,1,0:T(8,128)(2,1)} %shard_map.119), calls=%async_computation.1 | async-start | bytes 2097152 | tf_op jit(solution)/shard_map/all_to_all | solution.py:349
  21.8 2.5 %shard_map.120 = (bf16[16,16,256]{2,1,0:T(8,128)(2,1)}, bf16[16,16,256]{2,1,0:T(8,128)(2,1)}, bf16[16,16,256]{2,1,0:T(8,128)(2,1)}, bf16[16,16,256]{2,1,0:T(8,128)(2,1)}) custom-call(s32[1]{0:T(128)} %bitcast.1.shard_ref, s32[8,1,36]{2,1,0:T(1,128)} %all_to_all.10.incoming_ref, bf16[256,16,256]{2,1,0:T(8,128)(2,1)} %tokens_ref.5), custom_call_target="tpu_custom_call" | custom-call | tf_op jit(solution)/shard_map/pallas_call | solution.py:355
  24.8 1.9 %collective-permute-start.1 = (bf16[16,16,256]{2,1,0:T(8,128)(2,1)}, bf16[16,16,256]{2,1,0:T(8,128)(2,1)S(1)}, u32[]{:S(2)}, u32[]{:S(2)}) collective-permute-start(bf16[16,16,256]{2,1,0:T(8,128)(2,1)} %get-tuple-element.64), channel_id=1, source_target_pairs={{0,2},{2,0},{4,6},{6,4},{8,10},{10,8},{12,14},{14,12},{1,3},{3,1},... | collective-permute-start | bytes 393224 | tf_op jit(solution)/shard_map/ppermute | solution.py:326
  26.7 1.5 %collective-permute-start.2 = (bf16[16,16,256]{2,1,0:T(8,128)(2,1)}, bf16[16,16,256]{2,1,0:T(8,128)(2,1)S(1)}, u32[]{:S(2)}, u32[]{:S(2)}) collective-permute-start(bf16[16,16,256]{2,1,0:T(8,128)(2,1)} %get-tuple-element.65), channel_id=1, source_target_pairs={{0,4},{2,6},{4,0},{6,2},{8,12},{10,14},{12,8},{14,10},{1,5},{3,7},... | collective-permute-start | bytes 393224 | tf_op jit(solution)/shard_map/ppermute | solution.py:326
  28.3 5.9 %collective-permute-done.1.refs_1_ = bf16[16,16,256]{2,1,0:T(8,128)(2,1)S(1)} collective-permute-done((bf16[16,16,256]{2,1,0:T(8,128)(2,1)}, bf16[16,16,256]{2,1,0:T(8,128)(2,1)S(1)}, u32[]{:S(2)}, u32[]{:S(2)}) %collective-permute-start.1) | collective-permute-done | bytes 131104 | tf_op jit(solution)/shard_map/ppermute | solution.py:326
  34.2 7.9 %collective-permute-done.2.refs_2_ = bf16[16,16,256]{2,1,0:T(8,128)(2,1)S(1)} collective-permute-done((bf16[16,16,256]{2,1,0:T(8,128)(2,1)}, bf16[16,16,256]{2,1,0:T(8,128)(2,1)S(1)}, u32[]{:S(2)}, u32[]{:S(2)}) %collective-permute-start.2) | collective-permute-done | bytes 131104 | tf_op jit(solution)/shard_map/ppermute | solution.py:326
  42.2 2.1 %collective-permute-done.3.refs_3_ = bf16[16,16,256]{2,1,0:T(8,128)(2,1)S(1)} collective-permute-done((bf16[16,16,256]{2,1,0:T(8,128)(2,1)}, bf16[16,16,256]{2,1,0:T(8,128)(2,1)S(1)}, u32[]{:S(2)}, u32[]{:S(2)}) %collective-permute-start.3) | collective-permute-done | bytes 131104 | tf_op jit(solution)/shard_map/ppermute | solution.py:326
  44.9 2.0 %shard_map.121 = (bf16[32,16,256]{2,1,0:T(8,128)(2,1)}, bf16[32,16,256]{2,1,0:T(8,128)(2,1)S(1)}) custom-call(s32[1]{0:T(128)} %bitcast.1.shard_ref, s32[8,1,36]{2,1,0:T(1,128)} %all_to_all.10.incoming_ref, bf16[16,16,256]{2,1,0:T(8,128)(2,1)} %get-tuple-element.63.refs_0_, bf16[16,16,256]{2,1,0:T(8,128)(2,1)} %copy-done.6, bf16[16,16,256]{2,1,0:T(8,128)(2,1)} %copy-done.7, ...), custom_call_target="tpu_custom_call" | custom-call | tf_op jit(solution)/shard_map/pallas_call | solution.py:365
  48.7 2.9 %collective-permute-start.15 = (s32[]{:T(128)}, s32[]{:T(128)}, u32[]{:S(2)}, u32[]{:S(2)}) collective-permute-start(s32[]{:T(128)} %convert_element_type.6), channel_id=1, source_target_pairs={{0,16},{16,0},{1,17},{17,1},{2,18},{18,2},{3,19},{19,3},{4,20},{20... | collective-permute-start | bytes 20 | tf_op jit(solution)/shard_map/ppermute | solution.py:378
  51.5 0.9 collective-permute-done.15
  52.4 2.5 %shard_map.122 = (bf16[16,16,256]{2,1,0:T(8,128)(2,1)}, bf16[16,16,256]{2,1,0:T(8,128)(2,1)}, bf16[16,16,256]{2,1,0:T(8,128)(2,1)}, bf16[16,16,256]{2,1,0:T(8,128)(2,1)}) custom-call(s32[1]{0:T(128)} %bitcast.1.shard_ref, s32[8,1,36]{2,1,0:T(1,128)} %all_to_all.10.incoming_ref, bf16[256,16,256]{2,1,0:T(8,128)(2,1)} %tokens_ref.5), custom_call_target="tpu_custom_call" | custom-call | tf_op jit(solution)/shard_map/pallas_call | solution.py:355
  54.9 1.1 %collective-permute-start.4 = (bf16[16,16,256]{2,1,0:T(8,128)(2,1)}, bf16[16,16,256]{2,1,0:T(8,128)(2,1)S(1)}, u32[]{:S(2)}, u32[]{:S(2)}) collective-permute-start(bf16[16,16,256]{2,1,0:T(8,128)(2,1)} %get-tuple-element.71), channel_id=1, source_target_pairs={{0,2},{2,0},{4,6},{6,4},{8,10},{10,8},{12,14},{14,12},{1,3},{3,1},... | collective-permute-start | bytes 393224 | tf_op jit(solution)/shard_map/ppermute | solution.py:326
  56.0 4.2 %collective-permute-start.7 = (bf16[32,16,256]{2,1,0:T(8,128)(2,1)}, bf16[32,16,256]{2,1,0:T(8,128)(2,1)S(1)}, u32[]{:S(2)}, u32[]{:S(2)}) collective-permute-start(bf16[32,16,256]{2,1,0:T(8,128)(2,1)} %get-tuple-element.74), channel_id=1, source_target_pairs={{0,8},{2,10},{4,12},{6,14},{8,0},{10,2},{12,4},{14,6},{1,9},{3,11}... | collective-permute-start | bytes 786440 | tf_op jit(solution)/shard_map/ppermute | solution.py:326
  61.0 2.8 %collective-permute-start.6 = (bf16[16,16,256]{2,1,0:T(8,128)(2,1)}, bf16[16,16,256]{2,1,0:T(8,128)(2,1)S(1)}, u32[]{:S(2)}, u32[]{:S(2)}) collective-permute-start(bf16[16,16,256]{2,1,0:T(8,128)(2,1)} %get-tuple-element.73), channel_id=1, source_target_pairs={{0,6},{2,4},{4,2},{6,0},{8,14},{10,12},{12,10},{14,8},{1,7},{3,5},... | collective-permute-start | bytes 393224 | tf_op jit(solution)/shard_map/ppermute | solution.py:326
  64.4 5.6 %collective-permute-done.5.refs_3_ = bf16[16,16,256]{2,1,0:T(8,128)(2,1)S(1)} collective-permute-done((bf16[16,16,256]{2,1,0:T(8,128)(2,1)}, bf16[16,16,256]{2,1,0:T(8,128)(2,1)S(1)}, u32[]{:S(2)}, u32[]{:S(2)}) %collective-permute-start.5) | collective-permute-done | bytes 131104 | tf_op jit(solution)/shard_map/ppermute | solution.py:326
  70.0 5.1 %collective-permute-done.6.refs_4_ = bf16[16,16,256]{2,1,0:T(8,128)(2,1)S(1)} collective-permute-done((bf16[16,16,256]{2,1,0:T(8,128)(2,1)}, bf16[16,16,256]{2,1,0:T(8,128)(2,1)S(1)}, u32[]{:S(2)}, u32[]{:S(2)}) %collective-permute-start.6) | collective-permute-done | bytes 131104 | tf_op jit(solution)/shard_map/ppermute | solution.py:326
  76.2 3.0 %shard_map.124 = bf16[64,16,256]{2,1,0:T(8,128)(2,1)} custom-call(s32[1]{0:T(128)S(6)} %sub.3.core_ref, s32[1,128]{1,0:T(1,128)} %get-tuple-element.83.list_ref, bf16[128,16,256]{2,1,0:T(8,128)(2,1)} %bitcast.9, bf16[16,16,256]{2,1,0:T(8,128)(2,1)} %get-tuple-element.92.refs_1_, bf16[16,16,256]{2,1,0:T(8,128)(2,1)} %copy-done.2, ...), custom_call_target="tpu_custom_call" | custom-call | tf_op jit(solution)/shard_map/pallas_call | solution.py:392
  79.3 3.0 %shard_map.123.refs_0_ = bf16[64,16,256]{2,1,0:T(8,128)(2,1)} custom-call(s32[1]{0:T(128)} %bitcast.core_ref, s32[1,128]{1,0:T(1,128)} %get-tuple-element.83.list_ref, bf16[128,16,256]{2,1,0:T(8,128)(2,1)} %bitcast.10, bf16[16,16,256]{2,1,0:T(8,128)(2,1)} %get-tuple-element.92.refs_1_, bf16[16,16,256]{2,1,0:T(8,128)(2,1)} %copy-done.2, ...), custom_call_target="tpu_custom_call" | custom-call | tf_op jit(solution)/shard_map/pallas_call | solution.py:392
  83.2 21.5 %shard_map.125.here_ref = bf16[32,512]{1,0:T(8,128)(2,1)} custom-call(s32[1]{0:T(128)} %bitcast.core_ref, f32[4]{0:T(128)} %scale_a_ref.1, f32[4]{0:T(128)} %copy-done.18, f32[1,512]{1,0:T(1,128)} %bitcast.15, f32[1,512]{1,0:T(1,128)} %bitcast.16, bf16[64,16,256]{2,1,0:T(8,128)(2,1)} %shard_map.123.refs_0_, bf16[64,16,256]{2,1,0:T(8,128)(2,1)} %copy-done.11, ...), custom_call_target="tpu_custom_call" | custom-call | flops 3758096384 | bytes 8388608 | tf_op jit(solution)/shard_map/pallas_call | solution.py:407
  105.3 1.1 collective-permute-done.17.there_ref
  107.0 1.4 %shard_map.126 = bf16[64,512]{1,0:T(8,128)(2,1)} custom-call(s32[1]{0:T(128)} %bitcast.core_ref, bf16[32,512]{1,0:T(8,128)(2,1)} %shard_map.125.here_ref, bf16[32,512]{1,0:T(8,128)(2,1)} %copy-done.9), custom_call_target="tpu_custom_call" | custom-call | tf_op jit(solution)/shard_map/pallas_call | solution.py:441
  (63 shorter events, 6.3 us)
Async XLA Ops:
  18.1 24.1 %copy-start.13 = (bf16[512,256]{1,0:T(8,128)(2,1)S(1)}, bf16[512,256]{1,0:T(8,128)(2,1)}, u32[]{:S(2)}) copy-start(bf16[512,256]{1,0:T(8,128)(2,1)} %refs_4_.1) | copy-start | bytes 786436
  18.1 26.2 %copy-start.17 = (f32[4]{0:T(128)S(1)}, f32[4]{0:T(128)}, u32[]{:S(2)}) copy-start(f32[4]{0:T(128)} %scale_a_ref.1) | copy-start | bytes 52
  18.1 28.9 %copy-start.15 = (f32[1024]{0:T(1024)S(1)}, f32[1024]{0:T(1024)}, u32[]{:S(2)}) copy-start(f32[1024]{0:T(1024)} %param.24) | copy-start | bytes 12292
  18.1 29.0 %copy-start.5 = (s32[8,1,36]{2,1,0:T(1,128)S(1)}, s32[8,1,36]{2,1,0:T(1,128)}, u32[]{:S(2)}) copy-start(s32[8,1,36]{2,1,0:T(1,128)} %all_to_all.10.incoming_ref) | copy-start | bytes 3460
  18.1 57.0 %all-to-all-start.1 = ((bf16[8,16,16,256]{3,2,1,0:T(8,128)(2,1)}), bf16[8,16,16,256]{3,2,1,0:T(8,128)(2,1)S(1)}, u32[]{:S(2)}, u32[]{:S(2)}) async-start(bf16[8,16,16,256]{3,2,1,0:T(8,128)(2,1)} %shard_map.119), calls=%async_computation.1 | async-start | bytes 2097152 | tf_op jit(solution)/shard_map/all_to_all | solution.py:349
  24.3 50.8 %collective-permute-start.11 = (bf16[512,1024]{1,0:T(8,128)(2,1)S(1)}, bf16[512,1024]{1,0:T(8,128)(2,1)}, u32[]{:S(2)}, u32[]{:S(2)}) collective-permute-start(bf16[512,1024]{1,0:T(8,128)(2,1)S(1)} %copy-done.10), channel_id=1, source_target_pairs={{0,1},{1,0},{2,3},{3,2},{4,5},{5,4},{6,7},{7,6},{8,9},{9,8},{10,11... | collective-permute-start | bytes 3145736 | tf_op jit(solution)/shard_map/ppermute | solution.py:323
  24.3 50.8 %collective-permute-start.12 = (bf16[1024,512]{1,0:T(8,128)(2,1)}, bf16[1024,512]{1,0:T(8,128)(2,1)}, u32[]{:S(2)}, u32[]{:S(2)}) collective-permute-start(bf16[1024,512]{1,0:T(8,128)(2,1)} %refs_12_.1), channel_id=1, source_target_pairs={{0,1},{1,0},{2,3},{3,2},{4,5},{5,4},{6,7},{7,6},{8,9},{9,8},{10,11... | collective-permute-start | bytes 3145736 | tf_op jit(solution)/shard_map/ppermute | solution.py:323
  24.8 9.4 %collective-permute-start.1 = (bf16[16,16,256]{2,1,0:T(8,128)(2,1)}, bf16[16,16,256]{2,1,0:T(8,128)(2,1)S(1)}, u32[]{:S(2)}, u32[]{:S(2)}) collective-permute-start(bf16[16,16,256]{2,1,0:T(8,128)(2,1)} %get-tuple-element.64), channel_id=1, source_target_pairs={{0,2},{2,0},{4,6},{6,4},{8,10},{10,8},{12,14},{14,12},{1,3},{3,1},... | collective-permute-start | bytes 393224 | tf_op jit(solution)/shard_map/ppermute | solution.py:326
  26.7 15.5 %collective-permute-start.2 = (bf16[16,16,256]{2,1,0:T(8,128)(2,1)}, bf16[16,16,256]{2,1,0:T(8,128)(2,1)S(1)}, u32[]{:S(2)}, u32[]{:S(2)}) collective-permute-start(bf16[16,16,256]{2,1,0:T(8,128)(2,1)} %get-tuple-element.65), channel_id=1, source_target_pairs={{0,4},{2,6},{4,0},{6,2},{8,12},{10,14},{12,8},{14,10},{1,5},{3,7},... | collective-permute-start | bytes 393224 | tf_op jit(solution)/shard_map/ppermute | solution.py:326
  28.2 16.1 %collective-permute-start.3 = (bf16[16,16,256]{2,1,0:T(8,128)(2,1)}, bf16[16,16,256]{2,1,0:T(8,128)(2,1)S(1)}, u32[]{:S(2)}, u32[]{:S(2)}) collective-permute-start(bf16[16,16,256]{2,1,0:T(8,128)(2,1)} %get-tuple-element.66), channel_id=1, source_target_pairs={{0,6},{2,4},{4,2},{6,0},{8,14},{10,12},{12,10},{14,8},{1,7},{3,5},... | collective-permute-start | bytes 393224 | tf_op jit(solution)/shard_map/ppermute | solution.py:326
  34.2 20.6 %collective-permute-start.8 = (bf16[512,256]{1,0:T(8,128)(2,1)S(1)}, bf16[512,256]{1,0:T(8,128)(2,1)}, u32[]{:S(2)}, u32[]{:S(2)}) collective-permute-start(bf16[512,256]{1,0:T(8,128)(2,1)S(1)} %copy-done.12), channel_id=1, source_target_pairs={{0,1},{1,0},{2,3},{3,2},{4,5},{5,4},{6,7},{7,6},{8,9},{9,8},{10,11... | collective-permute-start | bytes 786440 | tf_op jit(solution)/shard_map/ppermute | solution.py:323
  42.2 13.8 %collective-permute-start.9 = (bf16[512,256]{1,0:T(8,128)(2,1)S(1)}, bf16[512,256]{1,0:T(8,128)(2,1)}, u32[]{:S(2)}, u32[]{:S(2)}) collective-permute-start(bf16[512,256]{1,0:T(8,128)(2,1)S(1)} %copy-done.13), channel_id=1, source_target_pairs={{0,1},{1,0},{2,3},{3,2},{4,5},{5,4},{6,7},{7,6},{8,9},{9,8},{10,11... | collective-permute-start | bytes 786440 | tf_op jit(solution)/shard_map/ppermute | solution.py:323
  44.3 2.7 %collective-permute-start.14 = (f32[4]{0:T(128)S(1)}, f32[4]{0:T(128)S(1)}, u32[]{:S(2)}, u32[]{:S(2)}) collective-permute-start(f32[4]{0:T(128)S(1)} %copy-done.17), channel_id=1, source_target_pairs={{0,1},{1,0},{2,3},{3,2},{4,5},{5,4},{6,7},{7,6},{8,9},{9,8},{10,11... | collective-permute-start | bytes 56 | tf_op jit(solution)/shard_map/ppermute | solution.py:323
  47.0 32.3 %copy-start.18 = (f32[4]{0:T(128)}, f32[4]{0:T(128)S(1)}, u32[]{:S(2)}) copy-start(f32[4]{0:T(128)S(1)} %collective-permute-done.14.scale_b_ref) | copy-start | bytes 52
  47.0 1.7 %collective-permute-start.13 = (f32[1024]{0:T(1024)S(1)}, f32[1024]{0:T(1024)S(1)}, u32[]{:S(2)}, u32[]{:S(2)}) collective-permute-start(f32[1024]{0:T(1024)S(1)} %copy-done.15), channel_id=1, source_target_pairs={{0,1},{1,0},{2,3},{3,2},{4,5},{5,4},{6,7},{7,6},{8,9},{9,8},{10,11... | collective-permute-start | bytes 12296 | tf_op jit(solution)/shard_map/ppermute | solution.py:323
  48.7 30.6 %copy-start.16 = (f32[1024]{0:T(1024)}, f32[1024]{0:T(1024)S(1)}, u32[]{:S(2)}) copy-start(f32[1024]{0:T(1024)S(1)} %collective-permute-done.13) | copy-start | bytes 12292
  48.7 3.7 %collective-permute-start.15 = (s32[]{:T(128)}, s32[]{:T(128)}, u32[]{:S(2)}, u32[]{:S(2)}) collective-permute-start(s32[]{:T(128)} %convert_element_type.6), channel_id=1, source_target_pairs={{0,16},{16,0},{1,17},{17,1},{2,18},{18,2},{3,19},{19,3},{4,20},{20... | collective-permute-start | bytes 20 | tf_op jit(solution)/shard_map/ppermute | solution.py:378
  52.4 7.8 %collective-permute-start.10 = (bf16[256,512]{1,0:T(8,128)(2,1)}, bf16[256,512]{1,0:T(8,128)(2,1)S(1)}, u32[]{:S(2)}, u32[]{:S(2)}) collective-permute-start(bf16[256,512]{1,0:T(8,128)(2,1)} %refs_6_.1), channel_id=1, source_target_pairs={{0,1},{1,0},{2,3},{3,2},{4,5},{5,4},{6,7},{7,6},{8,9},{9,8},{10,11... | collective-permute-start | bytes 786440 | tf_op jit(solution)/shard_map/ppermute | solution.py:323
  54.9 6.1 %collective-permute-start.4 = (bf16[16,16,256]{2,1,0:T(8,128)(2,1)}, bf16[16,16,256]{2,1,0:T(8,128)(2,1)S(1)}, u32[]{:S(2)}, u32[]{:S(2)}) collective-permute-start(bf16[16,16,256]{2,1,0:T(8,128)(2,1)} %get-tuple-element.71), channel_id=1, source_target_pairs={{0,2},{2,0},{4,6},{6,4},{8,10},{10,8},{12,14},{14,12},{1,3},{3,1},... | collective-permute-start | bytes 393224 | tf_op jit(solution)/shard_map/ppermute | solution.py:326
  56.0 19.1 %collective-permute-start.7 = (bf16[32,16,256]{2,1,0:T(8,128)(2,1)}, bf16[32,16,256]{2,1,0:T(8,128)(2,1)S(1)}, u32[]{:S(2)}, u32[]{:S(2)}) collective-permute-start(bf16[32,16,256]{2,1,0:T(8,128)(2,1)} %get-tuple-element.74), channel_id=1, source_target_pairs={{0,8},{2,10},{4,12},{6,14},{8,0},{10,2},{12,4},{14,6},{1,9},{3,11}... | collective-permute-start | bytes 786440 | tf_op jit(solution)/shard_map/ppermute | solution.py:326
  60.9 9.1 %collective-permute-start.5 = (bf16[16,16,256]{2,1,0:T(8,128)(2,1)}, bf16[16,16,256]{2,1,0:T(8,128)(2,1)S(1)}, u32[]{:S(2)}, u32[]{:S(2)}) collective-permute-start(bf16[16,16,256]{2,1,0:T(8,128)(2,1)} %get-tuple-element.72), channel_id=1, source_target_pairs={{0,4},{2,6},{4,0},{6,2},{8,12},{10,14},{12,8},{14,10},{1,5},{3,7},... | collective-permute-start | bytes 393224 | tf_op jit(solution)/shard_map/ppermute | solution.py:326
  61.0 14.1 %collective-permute-start.6 = (bf16[16,16,256]{2,1,0:T(8,128)(2,1)}, bf16[16,16,256]{2,1,0:T(8,128)(2,1)S(1)}, u32[]{:S(2)}, u32[]{:S(2)}) collective-permute-start(bf16[16,16,256]{2,1,0:T(8,128)(2,1)} %get-tuple-element.73), channel_id=1, source_target_pairs={{0,6},{2,4},{4,2},{6,0},{8,14},{10,12},{12,10},{14,8},{1,7},{3,5},... | collective-permute-start | bytes 393224 | tf_op jit(solution)/shard_map/ppermute | solution.py:326
  79.3 3.1 %collective-permute-start.16 = (bf16[64,16,256]{2,1,0:T(8,128)(2,1)}, bf16[64,16,256]{2,1,0:T(8,128)(2,1)S(1)}, u32[]{:S(2)}, u32[]{:S(2)}) collective-permute-start(bf16[64,16,256]{2,1,0:T(8,128)(2,1)} %shard_map.124), channel_id=1, source_target_pairs={{0,1},{1,0},{2,3},{3,2},{4,5},{5,4},{6,7},{7,6},{8,9},{9,8},{10,11... | collective-permute-start | bytes 1572872 | tf_op jit(solution)/shard_map/ppermute | solution.py:323
  104.7 1.6 %collective-permute-start.17 = (bf16[32,512]{1,0:T(8,128)(2,1)}, bf16[32,512]{1,0:T(8,128)(2,1)S(1)}, u32[]{:S(2)}, u32[]{:S(2)}) collective-permute-start(bf16[32,512]{1,0:T(8,128)(2,1)} %shard_map.125.here_ref), channel_id=1, source_target_pairs={{0,1},{1,0},{2,3},{3,2},{4,5},{5,4},{6,7},{7,6},{8,9},{9,8},{10,11... | collective-permute-start | bytes 98312 | tf_op jit(solution)/shard_map/ppermute | solution.py:323
  (13 other events, 59.1 us)

commit v8 on v6

--- a/solution.py
+++ b/solution.py
@@ -166,7 +166,8 @@
     length,
     head_dim,
     core_ref,
-    scale_ref,
+    scale_a_ref,
+    scale_b_ref,
     gain_attn_ref,
     gain_mlp_ref,
     *refs,
@@ -174,7 +175,7 @@
     own_held_ref, far_held_ref, *held_refs = refs[:14]
     result_ref, qkv_ref, out_ref, in_ref, back_ref, bias_ref = refs[14:20]
     tokens_ref, normed_ref, heads_ref, mixed_ref, hidden_ref = refs[20:25]
-    inner_ref, bent_ref, pooled_ref, mean_ref, sems, token_sems = refs[25:]
+    pooled_ref, mean_ref, sems, token_sems = refs[25:]
     width, units = in_ref.shape
     wide = width // 2
     homes = [qkv_ref.at[:, pl.ds(k * wide, wide)] for k in range(4)]
@@ -198,126 +199,99 @@
     count = result_ref.shape[0]
     blocks = count // BLOCK
     tile = 256
-    pair_dim = 2 * head_dim
-    even = lax.broadcasted_iota(jnp.int32, (half, pair_dim), 1) < head_dim
+    scale_refs = (scale_a_ref, scale_b_ref)
+    lane_head = lax.broadcasted_iota(jnp.int32, (rows, wide), 1) // head_dim
     same = (
         lax.broadcasted_iota(jnp.int32, (half, half), 0) // length
         == lax.broadcasted_iota(jnp.int32, (half, half), 1) // length
     )
+    empty = jnp.zeros((half, half), jnp.bfloat16)
 
     def span(step, size):
         return pl.ds(pl.multiple_of(step * size, size), size)
 
-    def split(values):
-        zero = jnp.zeros_like(values)
-        return jnp.concatenate(
-            [jnp.where(even, values, zero), jnp.where(even, zero, values)], axis=0
+    def begin(step, carry):
+        images = pl.ds(step * 2 * BLOCK, 2 * BLOCK)
+        tokens = jnp.concatenate(
+            [tokens_ref[k, images].reshape(rows, -1).astype(jnp.float32) for k in range(2)], axis=1
         )
-
-    ones = split(jnp.ones((half, pair_dim), jnp.bfloat16))
-
-    def begin(step, carry):
-        images = pl.ds(step * 2, 2)
-        here = span(step, 2 * length)
-        tokens = [
-            tokens_ref[k, images].reshape(2 * length, -1).astype(jnp.float32) for k in range(2)
-        ]
-        tokens = jnp.concatenate(tokens, axis=1)
-        hidden_ref[here, :] = tokens
-        normed_ref[here, :] = norm_rows(tokens, gain_attn_ref[...]).astype(jnp.bfloat16)
+        hidden_ref[span(step, rows), :] = tokens
+        normed_ref[span(step, rows), :] = norm_rows(tokens, gain_attn_ref[...]).astype(jnp.bfloat16)
         return carry
 
     def project(step, carry):
-        here = span(step // 4, rows)
-        cut = span(step % 4, 2 * width // 4)
-        heads_ref[here, cut] = dot(normed_ref[here, :], qkv_ref[:, cut]).astype(jnp.bfloat16)
+        cut = span(step, tile)
+        heads_ref[:, cut] = dot(normed_ref[...], qkv_ref[:, cut]).astype(jnp.bfloat16)
         return carry
 
     def weigh(scores, factor):
         scores = jnp.where(same, scores, -1e30)
         top = jnp.max(scores, axis=1, keepdims=True)
-        return jnp.exp2((scores - top) * factor).astype(jnp.bfloat16)
-
-    def mix(query, key, value, factors):
-        scores = dot_nt(query, split(key))
-        weights = [weigh(scores[:, k * half : (k + 1) * half], factors[k]) for k in range(2)]
-        mixed = dot(jnp.concatenate(weights, axis=1), jnp.concatenate([split(value), ones], axis=1))
-        total = mixed[:, pair_dim:]
-        inverse = pl.reciprocal(total, approx=True)
-        inverse = inverse * (2.0 - total * inverse)
-        return (mixed[:, :pair_dim] * inverse).astype(jnp.bfloat16)
+        weights = jnp.exp2((scores - top) * factor)
+        return (weights * (1.0 / jnp.sum(weights, axis=1, keepdims=True))).astype(jnp.bfloat16)
 
     def attend(step, carry):
-        for index in range(width // pair_dim):
-            factors = [scale_ref[2 * index + k] * (LOG2E / head_dim**0.5) for k in range(2)]
-            cut = slice(index * pair_dim, (index + 1) * pair_dim)
-            beyond = slice(width + cut.start, width + cut.stop)
-            sides = [span(2 * step + k, half) for k in range(2)]
-            query = [heads_ref[side, cut] for side in sides]
-            value = [heads_ref[side, beyond] for side in sides]
-            for k in range(2):
-                mixed_ref[sides[k], cut] = mix(query[k], query[1 - k], value[1 - k], factors)
+        here = span(step, rows)
+        for core in range(2):
+            query = heads_ref[here, core * wide : (core + 1) * wide]
+            value = heads_ref[here, width + core * wide : width + (core + 1) * wide]
+            zero = jnp.zeros_like(query)
+            heads = range(wide // head_dim)
+            masked = [jnp.where(lane_head == head, query, zero) for head in heads]
+            scores = dot_nt(jnp.concatenate(masked, axis=0), query)
+            probs = []
+            for head in heads:
+                factor = scale_refs[core][head] * (LOG2E / head_dim**0.5)
+                at = head * rows
+                ahead = weigh(scores[at : at + half, half:], factor)
+                behind = weigh(scores[at + half : at + rows, :half], factor)
+                probs.append(jnp.concatenate([empty, ahead], axis=1))
+                probs.append(jnp.concatenate([behind, empty], axis=1))
+            mixed = dot(jnp.concatenate(probs, axis=0), value)
+            total = mixed[:rows]
+            for head in heads[1:]:
+                total = jnp.where(lane_head == head, mixed[head * rows : (head + 1) * rows], total)
+            mixed_ref[here, core * wide : (core + 1) * wide] = total.astype(jnp.bfloat16)
         return carry
 
     def join(step, carry):
-        here = span(step // 2, rows)
-        cut = span(step % 2, width // 2)
-        hidden_ref[here, cut] += dot(mixed_ref[here, :], out_ref[:, cut])
+        cut = span(step, tile)
+        hidden_ref[:, cut] += dot(mixed_ref[...], out_ref[:, cut])
         return carry
 
     def middle(step, carry):
-        total = 0.0
-        for side in range(2):
-            at = (step // BLOCK * 2 + side) * BLOCK + step % BLOCK
-            here = span(at, length)
-            hidden = hidden_ref[here, :]
-            total = total + jnp.sum(hidden, axis=0, keepdims=True)
-            normed_ref[here, :] = norm_rows(hidden, gain_mlp_ref[...]).astype(jnp.bfloat16)
-        mean_ref[pl.ds(step, 1), :] = total
-        return carry
-
-    long = inner_ref.shape[1]
-    pairs = long // (2 * length)
-    row = lax.broadcasted_iota(jnp.int32, (pairs, long), 1)
-    row_pair = row // rows * BLOCK + row % half // length
-    pool = jnp.where(row_pair == lax.broadcasted_iota(jnp.int32, row.shape, 0), 1.0, 0.0)
-    pool = pool.astype(jnp.bfloat16)
-    tiles = units // tile
-    steps = count // pairs * tiles
-    piece = 32
+        here = span(step, rows)
+        hidden = hidden_ref[here, :]
+        mean_ref[span(step, BLOCK), :] = jnp.sum(
+            hidden.reshape(2, BLOCK, length, -1), axis=(0, 2)
+        )
+        normed_ref[here, :] = norm_rows(hidden, gain_mlp_ref[...]).astype(jnp.bfloat16)
+        return carry
 
     def expand(step, carry):
-        new = lax.rem(step, steps)
-        here = span(new // tiles, long)
-        cut = span(lax.rem(new, tiles), tile)
-        inner_ref[lax.rem(step, 2)] = dot(normed_ref[here, :], in_ref[:, cut])
-        pooled = dot(pool, bent_ref[lax.rem(step, 2)])
-        last = lax.rem(step + steps - 1, steps)
-        bias = bias_ref[:, span(lax.rem(last, tiles), tile)]
-        for at in range(0, long, piece):
-            inner = inner_ref[lax.rem(step + 1, 2), at : at + piece, :] + bias
-            inner = inner.astype(jnp.bfloat16)
-            cubic = inner * inner * jnp.bfloat16(0.0356774081) + jnp.bfloat16(0.7978845608)
-            bent = (jnp.tanh(inner * cubic) + jnp.bfloat16(1.0)) * inner
-            bent_ref[lax.rem(step + 1, 2), at : at + piece, :] = bent
-        old = lax.rem(step + steps - 2, steps)
-        pooled_ref[span(old // tiles, pairs), span(lax.rem(old, tiles), tile)] = pooled
+        cut = span(step, tile)
+        inner = dot(normed_ref[...], in_ref[:, cut])
+        for index in range(blocks):
+            piece = inner[index * rows : (index + 1) * rows] + bias_ref[:, cut]
+            bent = jnp.tanh(piece * (0.7978845608028654 + 0.035677408136300125 * (piece * piece)))
+            bent = (piece * bent + piece).reshape(2, BLOCK, length, -1)
+            pooled_ref[index * BLOCK : (index + 1) * BLOCK, cut] = jnp.sum(bent, axis=(0, 2))
         return carry
 
     for load in token_loads:
         load.wait()
-    lax.fori_loop(0, count, begin, 0, unroll=8)
+    lax.fori_loop(0, blocks, begin, 0)
     for load in loads[:4]:
         load.wait()
-    lax.fori_loop(0, blocks * 4, project, 0, unroll=2)
+    lax.fori_loop(0, 2 * width // tile, project, 0)
     lax.fori_loop(0, blocks, attend, 0)
     for load in loads[4:6]:
         load.wait()
-    lax.fori_loop(0, blocks * 2, join, 0, unroll=2)
-    lax.fori_loop(0, count, middle, 0, unroll=8)
+    lax.fori_loop(0, width // tile, join, 0)
+    lax.fori_loop(0, blocks, middle, 0)
     for load in loads[6:10]:
         load.wait()
-    lax.fori_loop(0, steps + 2, expand, 0)
+    lax.fori_loop(0, units // tile, expand, 0)
     for load in loads[10:]:
         load.wait()
     pooled = pooled_ref[...] * (0.25 / length)
@@ -390,6 +364,10 @@
         + [images(plan.extra)] * (plan.half if plan.extra else 0),
         in_specs=[smem, smem, vmem],
     )(shard, incoming, image_tokens)
+    if plan.extra:
+        served, near, chunks = lax.optimization_barrier((served, near, chunks))
+    returned = lax.all_to_all(served, "shard", split_axis=0, concat_axis=0, tiled=True)
+    sources = [returned.reshape(-1, length, features)]
     weights = (w_qk, w_value, w_out, w_in, w_back, bias_in, logit_scale)
     if plan.extra:
         first, second = pl.pallas_call(
@@ -397,12 +375,6 @@
             out_shape=[images(plan.part)] * 2,
             in_specs=[smem, smem] + [vmem] * plan.half,
         )(shard, incoming, *chunks)
-        served, near, first, second, incoming, weights = lax.optimization_barrier(
-            (served, near, first, second, incoming, weights)
-        )
-    returned = lax.all_to_all(served, "shard", split_axis=0, concat_axis=0, tiled=True)
-    sources = [returned.reshape(-1, length, features)]
-    if plan.extra:
         first = across(first, plan.half)
         near = [near[0]] + [across(near[k], k) for k in range(1, plan.half)]
         crowded = jnp.max(jnp.sum(incoming[:, 0, plan.capacity :], axis=1)) > plan.part
@@ -411,12 +383,15 @@
         for _ in range(groups - 1):
             passed = lax.ppermute(passed, "groups", [(k, (k + 1) % groups) for k in range(groups)])
             crowded = jnp.maximum(crowded, passed)
+        sources += [*near, first]
+    swapped = [swap(w) for w in weights]
+    sources, swapped = lax.optimization_barrier((sources, swapped))
+    if plan.extra:
+        second, sources = lax.optimization_barrier((second, sources))
         second = lax.cond(
             crowded > 0, lambda part: across(part, plan.half), lambda part: part, second
         )
-        sources += [*near, first, second]
-    swapped = [swap(w) for w in weights]
-    sources, swapped = lax.optimization_barrier((sources, swapped))
+        sources = [*sources, second]
     far_qk, far_value, far_out, far_in, far_back, far_bias, far_scale = swapped
 
     def pick(core):
@@ -435,11 +410,10 @@
     matrices = [w_qk, far_qk, w_value, far_value, w_out, far_out, w_in, far_in]
     matrices += [bias_in.reshape(1, -1), far_bias.reshape(1, -1), w_back, far_back]
     token_count = pair_count * length
-    long = token_count // 2
     here = pl.pallas_call(
         functools.partial(compare_kernel, length, head_dim),
         out_shape=jax.ShapeDtypeStruct((mine, width), jnp.bfloat16),
-        in_specs=[smem] * 2 + [vmem] * 2 + [hbm] * 14,
+        in_specs=[smem] * 3 + [vmem] * 2 + [hbm] * 14,
         out_specs=vmem,
         scratch_shapes=[
             pltpu.VMEM((width, 2 * width), jnp.bfloat16),
@@ -452,8 +426,6 @@
             pltpu.VMEM((token_count, 2 * width), jnp.bfloat16),
             pltpu.VMEM((token_count, width), jnp.bfloat16),
             pltpu.VMEM((token_count, width), jnp.float32),
-            pltpu.VMEM((2, long, 256), jnp.float32),
-            pltpu.VMEM((2, long, 256), jnp.bfloat16),
             pltpu.VMEM((mine, units), jnp.float32),
             pltpu.VMEM((mine, width), jnp.float32),
             pltpu.SemaphoreType.DMA((12,)),
@@ -467,7 +439,8 @@
         ),
     )(
         core,
-        jnp.concatenate([logit_scale, far_scale]),
+        logit_scale,
+        far_scale,
         gain_attn.reshape(1, -1),
         gain_mlp.reshape(1, -1),
         own,

time: 104 us -> 96.4 us (0.927)
  waiting for transfers between devices: 27.1 us -> 19.3 us
  starting transfers between devices: 17.6 us -> 21.7 us
  Pallas kernels: 37.9 us -> 35.6 us
    ppermute x7, waiting for transfers between devices: 21.2 us -> 15.7 us  [across(): lax.ppermute(values, 'shard', [(k, k ^ distance) for k in range(owner_cou...]
    ppermute x7, starting transfers between devices: 9.76 us -> 13.4 us  [across(): lax.ppermute(values, 'shard', [(k, k ^ distance) for k in range(owner_cou...]
    pallas_call x1, Pallas kernels: 22.7 us -> 20.3 us  [on_device(): pl.pallas_call(functools.partial(compare_kernel, length, head_dim), out_s...]
    ppermute x9, waiting for transfers between devices: 5.01 us -> 2.86 us  [swap(): return lax.ppermute(values, 'mp', [(0, 1), (1, 0)])]
    unnamed x34 -> x36, local copies, waits for them, and re-layouts: 2.42 us -> 1.88 us
  transfers between devices with their start and end apart: 18 -> 18, of which waited for: 10 -> 10; matrix products, arithmetic and copies ran while one was open for 2% -> 1% of each run, Pallas kernels for 6% -> 8%
where the time goes in v8:
time: 96.4 us; the launch traced here: 95.9 us
  Pallas kernels  35.6 us (37%)
  starting transfers between devices  21.7 us (23%)
  waiting for transfers between devices  19.3 us (20%)
  blocking collectives  13.6 us (14%)
  other arithmetic  2.35 us (2%)
  local copies, waits for them, and re-layouts  1.88 us (2%)
  between operations  1.5 us (2%)
    pallas_call x1, Pallas kernels, on_device(): pl.pallas_call(functools.partial(compare_kernel, length, head_dim), out_s...  20.3 us
    ppermute x7, waiting for transfers between devices, across(): lax.ppermute(values, 'shard', [(k, k ^ distance) for k in range(owner_cou...  15.7 us
    all_to_all x1, blocking collectives, on_device(): lax.all_to_all(wanted, 'shard', split_axis=0, concat_axis=0, tiled=True)  13.6 us
    ppermute x7, starting transfers between devices, across(): lax.ppermute(values, 'shard', [(k, k ^ distance) for k in range(owner_cou...  13.4 us
    pallas_call x2, Pallas kernels, pick(): pl.pallas_call(pick_kernel, out_shape=images(pair_count), in_specs=[smem,...  6.08 us
    all_to_all x1, starting transfers between devices, on_device(): lax.all_to_all(served, 'shard', split_axis=0, concat_axis=0, tiled=True)  3.56 us
    pallas_call x1, Pallas kernels, on_device(): pl.pallas_call(functools.partial(serve_kernel, plan), out_shape=[images(o...  2.91 us
    ppermute x9, waiting for transfers between devices, swap(): return lax.ppermute(values, 'mp', [(0, 1), (1, 0)])  2.86 us
  transfers between devices with their start and end apart: 18, of which 10 were waited for; matrix products, arithmetic and copies ran while one was open for 1% of the time, Pallas kernels for 8%

profile of v8, /device:TPU:0, one launch (start us, length us, event | category | flops | bytes accessed | tf_op | source)
XLA Modules:
  0.0 95.9 jit_solution(12296267187486190332)
XLA Ops:
  0.0 1.8 %shard_map.118 = (s32[8,1,36]{2,1,0:T(1,128)}, s32[1,128]{1,0:T(1,128)}) custom-call(s32[1]{0:T(128)} %bitcast.2.shard_ref, s32[2,64]{1,0:T(2,128)} %bitcast.12, s32[2,64]{1,0:T(2,128)} %bitcast.13), custom_call_target="tpu_custom_call" | custom-call | tf_op jit(solution)/shard_map/pallas_call | solution.py:344
  1.8 13.6 %all_to_all.10.incoming_ref = s32[8,1,36]{2,1,0:T(1,128)} all-to-all(s32[8,1,36]{2,1,0:T(1,128)} %get-tuple-element.57), channel_id=1, replica_groups=mesh['groups'=2,'shard'=8,'mp'=2] {'shard'}, dimensions={0} | all-to-all | bytes 2304 | tf_op jit(solution)/shard_map/all_to_all | solution.py:352
  15.4 2.5 %shard_map.119 = (bf16[16,16,256]{2,1,0:T(8,128)(2,1)}, bf16[16,16,256]{2,1,0:T(8,128)(2,1)}, bf16[16,16,256]{2,1,0:T(8,128)(2,1)}, bf16[16,16,256]{2,1,0:T(8,128)(2,1)}) custom-call(s32[1]{0:T(128)} %bitcast.2.shard_ref, s32[8,1,36]{2,1,0:T(1,128)} %all_to_all.10.incoming_ref, bf16[256,16,256]{2,1,0:T(8,128)(2,1)} %tokens_ref.3), custom_call_target="tpu_custom_call" | custom-call | tf_op jit(solution)/shard_map/pallas_call | solution.py:354
  17.9 0.8 collective-permute-start.1
  19.2 2.2 %collective-permute-start.3 = (bf16[16,16,256]{2,1,0:T(8,128)(2,1)}, bf16[16,16,256]{2,1,0:T(8,128)(2,1)S(1)}, u32[]{:S(2)}, u32[]{:S(2)}) collective-permute-start(bf16[16,16,256]{2,1,0:T(8,128)(2,1)} %get-tuple-element.71), channel_id=1, source_target_pairs={{0,6},{2,4},{4,2},{6,0},{8,14},{10,12},{12,10},{14,8},{1,7},{3,5},... | collective-permute-start | bytes 393224 | tf_op jit(solution)/shard_map/ppermute | solution.py:335
  21.4 2.9 %shard_map.120 = (bf16[8,16,16,256]{3,2,1,0:T(8,128)(2,1)}, bf16[16,16,256]{2,1,0:T(8,128)(2,1)}, bf16[16,16,256]{2,1,0:T(8,128)(2,1)}, bf16[16,16,256]{2,1,0:T(8,128)(2,1)}, bf16[16,16,256]{2,1,0:T(8,128)(2,1)}) custom-call(s32[1]{0:T(128)} %bitcast.2.shard_ref, s32[8,1,36]{2,1,0:T(1,128)} %all_to_all.10.incoming_ref, bf16[256,16,256]{2,1,0:T(8,128)(2,1)} %tokens_ref.3), custom_call_target="tpu_custom_call" | custom-call | tf_op jit(solution)/shard_map/pallas_call | solution.py:361
  24.5 1.6 %collective-permute-done.3.refs_3_ = bf16[16,16,256]{2,1,0:T(8,128)(2,1)S(1)} collective-permute-done((bf16[16,16,256]{2,1,0:T(8,128)(2,1)}, bf16[16,16,256]{2,1,0:T(8,128)(2,1)S(1)}, u32[]{:S(2)}, u32[]{:S(2)}) %collective-permute-start.3) | collective-permute-done | bytes 131104 | tf_op jit(solution)/shard_map/ppermute | solution.py:335
  26.2 3.6 %all-to-all-start.1 = ((bf16[8,16,16,256]{3,2,1,0:T(8,128)(2,1)}), bf16[8,16,16,256]{3,2,1,0:T(8,128)(2,1)S(1)}, u32[]{:S(2)}, u32[]{:S(2)}) async-start(bf16[8,16,16,256]{3,2,1,0:T(8,128)(2,1)} %get-tuple-element.72), calls=%async_computation.1 | async-start | bytes 2097152 | tf_op jit(solution)/shard_map/all_to_all | solution.py:369
  33.1 2.8 %collective-permute-start.15 = (s32[]{:T(128)}, s32[]{:T(128)}, u32[]{:S(2)}, u32[]{:S(2)}) collective-permute-start(s32[]{:T(128)} %convert_element_type.6), channel_id=1, source_target_pairs={{0,16},{16,0},{1,17},{17,1},{2,18},{18,2},{3,19},{19,3},{4,20},{20... | collective-permute-start | bytes 20 | tf_op jit(solution)/shard_map/ppermute | solution.py:384
  36.6 1.2 %collective-permute-done.13 = f32[1024]{0:T(1024)S(1)} collective-permute-done((f32[1024]{0:T(1024)S(1)}, f32[1024]{0:T(1024)S(1)}, u32[]{:S(2)}, u32[]{:S(2)}) %collective-permute-start.13) | collective-permute-done | bytes 4128 | tf_op jit(solution)/shard_map/ppermute | solution.py:332
  38.0 2.0 %shard_map.121 = (bf16[32,16,256]{2,1,0:T(8,128)(2,1)}, bf16[32,16,256]{2,1,0:T(8,128)(2,1)S(1)}) custom-call(s32[1]{0:T(128)} %bitcast.2.shard_ref, s32[8,1,36]{2,1,0:T(1,128)} %all_to_all.10.incoming_ref, bf16[16,16,256]{2,1,0:T(8,128)(2,1)} %get-tuple-element.77.refs_0_, bf16[16,16,256]{2,1,0:T(8,128)(2,1)} %copy-done.5, bf16[16,16,256]{2,1,0:T(8,128)(2,1)} %copy-done.6, ...), custom_call_target="tpu_custom_call" | custom-call | tf_op jit(solution)/shard_map/pallas_call | solution.py:373
  40.0 1.9 %collective-permute-start.4 = (bf16[16,16,256]{2,1,0:T(8,128)(2,1)}, bf16[16,16,256]{2,1,0:T(8,128)(2,1)S(1)}, u32[]{:S(2)}, u32[]{:S(2)}) collective-permute-start(bf16[16,16,256]{2,1,0:T(8,128)(2,1)} %get-tuple-element.74), channel_id=1, source_target_pairs={{0,2},{2,0},{4,6},{6,4},{8,10},{10,8},{12,14},{14,12},{1,3},{3,1},... | collective-permute-start | bytes 393224 | tf_op jit(solution)/shard_map/ppermute | solution.py:335
  41.9 2.4 %collective-permute-start.7 = (bf16[32,16,256]{2,1,0:T(8,128)(2,1)}, bf16[32,16,256]{2,1,0:T(8,128)(2,1)S(1)}, u32[]{:S(2)}, u32[]{:S(2)}) collective-permute-start(bf16[32,16,256]{2,1,0:T(8,128)(2,1)} %get-tuple-element.81), channel_id=1, source_target_pairs={{0,8},{2,10},{4,12},{6,14},{8,0},{10,2},{12,4},{14,6},{1,9},{3,11}... | collective-permute-start | bytes 786440 | tf_op jit(solution)/shard_map/ppermute | solution.py:335
  44.3 1.5 %collective-permute-start.5 = (bf16[16,16,256]{2,1,0:T(8,128)(2,1)}, bf16[16,16,256]{2,1,0:T(8,128)(2,1)S(1)}, u32[]{:S(2)}, u32[]{:S(2)}) collective-permute-start(bf16[16,16,256]{2,1,0:T(8,128)(2,1)} %get-tuple-element.75), channel_id=1, source_target_pairs={{0,4},{2,6},{4,0},{6,2},{8,12},{10,14},{12,8},{14,10},{1,5},{3,7},... | collective-permute-start | bytes 393224 | tf_op jit(solution)/shard_map/ppermute | solution.py:335
  46.2 4.1 %collective-permute-start.6 = (bf16[16,16,256]{2,1,0:T(8,128)(2,1)}, bf16[16,16,256]{2,1,0:T(8,128)(2,1)S(1)}, u32[]{:S(2)}, u32[]{:S(2)}) collective-permute-start(bf16[16,16,256]{2,1,0:T(8,128)(2,1)} %get-tuple-element.76), channel_id=1, source_target_pairs={{0,6},{2,4},{4,2},{6,0},{8,14},{10,12},{12,10},{14,8},{1,7},{3,5},... | collective-permute-start | bytes 393224 | tf_op jit(solution)/shard_map/ppermute | solution.py:335
  50.9 3.3 %collective-permute-done.5.refs_3_ = bf16[16,16,256]{2,1,0:T(8,128)(2,1)S(1)} collective-permute-done((bf16[16,16,256]{2,1,0:T(8,128)(2,1)}, bf16[16,16,256]{2,1,0:T(8,128)(2,1)S(1)}, u32[]{:S(2)}, u32[]{:S(2)}) %collective-permute-start.5) | collective-permute-done | bytes 131104 | tf_op jit(solution)/shard_map/ppermute | solution.py:335
  54.1 2.0 %collective-permute-done.6.refs_4_ = bf16[16,16,256]{2,1,0:T(8,128)(2,1)S(1)} collective-permute-done((bf16[16,16,256]{2,1,0:T(8,128)(2,1)}, bf16[16,16,256]{2,1,0:T(8,128)(2,1)S(1)}, u32[]{:S(2)}, u32[]{:S(2)}) %collective-permute-start.6) | collective-permute-done | bytes 131104 | tf_op jit(solution)/shard_map/ppermute | solution.py:335
  56.2 8.2 %collective-permute-done.7.refs_5_ = bf16[32,16,256]{2,1,0:T(8,128)(2,1)S(1)} collective-permute-done((bf16[32,16,256]{2,1,0:T(8,128)(2,1)}, bf16[32,16,256]{2,1,0:T(8,128)(2,1)S(1)}, u32[]{:S(2)}, u32[]{:S(2)}) %collective-permute-start.7) | collective-permute-done | bytes 262176 | tf_op jit(solution)/shard_map/ppermute | solution.py:335
  65.5 3.0 %shard_map.123 = bf16[64,16,256]{2,1,0:T(8,128)(2,1)} custom-call(s32[1]{0:T(128)S(6)} %sub.3.core_ref, s32[1,128]{1,0:T(1,128)} %get-tuple-element.83.list_ref, bf16[128,16,256]{2,1,0:T(8,128)(2,1)} %bitcast.10, bf16[16,16,256]{2,1,0:T(8,128)(2,1)} %get-tuple-element.92.refs_1_, bf16[16,16,256]{2,1,0:T(8,128)(2,1)} %copy-done.2, ...), custom_call_target="tpu_custom_call" | custom-call | tf_op jit(solution)/shard_map/pallas_call | solution.py:398
  68.6 3.0 %shard_map.122.refs_0_ = bf16[64,16,256]{2,1,0:T(8,128)(2,1)} custom-call(s32[1]{0:T(128)} %bitcast.core_ref, s32[1,128]{1,0:T(1,128)} %get-tuple-element.83.list_ref, bf16[128,16,256]{2,1,0:T(8,128)(2,1)} %bitcast.11, bf16[16,16,256]{2,1,0:T(8,128)(2,1)} %get-tuple-element.92.refs_1_, bf16[16,16,256]{2,1,0:T(8,128)(2,1)} %copy-done.2, ...), custom_call_target="tpu_custom_call" | custom-call | tf_op jit(solution)/shard_map/pallas_call | solution.py:398
  71.7 0.8 copy-done.10
  72.5 20.3 %shard_map.124 = bf16[32,512]{1,0:T(8,128)(2,1)} custom-call(s32[1]{0:T(128)} %bitcast.core_ref, f32[4]{0:T(128)} %scale_a_ref.1, f32[4]{0:T(128)} %copy-done.17, f32[1,512]{1,0:T(1,128)} %bitcast.16, f32[1,512]{1,0:T(1,128)} %bitcast.17, bf16[64,16,256]{2,1,0:T(8,128)(2,1)} %shard_map.122.refs_0_, bf16[64,16,256]{2,1,0:T(8,128)(2,1)} %copy-done.10, ...), custom_call_target="tpu_custom_call" | custom-call | flops 3758096384 | bytes 8388608 | tf_op jit(solution)/shard_map/pallas_call | solution.py:413
  93.4 1.1 %collective-permute-done.17 = bf16[32,512]{1,0:T(8,128)(2,1)S(1)} collective-permute-done((bf16[32,512]{1,0:T(8,128)(2,1)}, bf16[32,512]{1,0:T(8,128)(2,1)S(1)}, u32[]{:S(2)}, u32[]{:S(2)}) %collective-permute-start.17) | collective-permute-done | bytes 32800 | tf_op jit(solution)/shard_map/ppermute | solution.py:332
  94.5 0.8 broadcast_select_fusion.1
  (61 shorter events, 7.1 us)
Async XLA Ops:
  17.9 18.8 %copy-start.14 = (f32[1024]{0:T(1024)S(1)}, f32[1024]{0:T(1024)}, u32[]{:S(2)}) copy-start(f32[1024]{0:T(1024)} %param.24) | copy-start | bytes 12292
  17.9 19.9 %copy-start.13 = (bf16[256,512]{1,0:T(8,128)(2,1)S(1)}, bf16[256,512]{1,0:T(8,128)(2,1)}, u32[]{:S(2)}) copy-start(bf16[256,512]{1,0:T(8,128)(2,1)} %refs_6_.1) | copy-start | bytes 786436
  17.9 6.6 %collective-permute-start.1 = (bf16[16,16,256]{2,1,0:T(8,128)(2,1)}, bf16[16,16,256]{2,1,0:T(8,128)(2,1)S(1)}, u32[]{:S(2)}, u32[]{:S(2)}) collective-permute-start(bf16[16,16,256]{2,1,0:T(8,128)(2,1)} %get-tuple-element.69), channel_id=1, source_target_pairs={{0,2},{2,0},{4,6},{6,4},{8,10},{10,8},{12,14},{14,12},{1,3},{3,1},... | collective-permute-start | bytes 393224 | tf_op jit(solution)/shard_map/ppermute | solution.py:335
  18.7 5.9 %collective-permute-start.2 = (bf16[16,16,256]{2,1,0:T(8,128)(2,1)}, bf16[16,16,256]{2,1,0:T(8,128)(2,1)S(1)}, u32[]{:S(2)}, u32[]{:S(2)}) collective-permute-start(bf16[16,16,256]{2,1,0:T(8,128)(2,1)} %get-tuple-element.70), channel_id=1, source_target_pairs={{0,4},{2,6},{4,0},{6,2},{8,12},{10,14},{12,8},{14,10},{1,5},{3,7},... | collective-permute-start | bytes 393224 | tf_op jit(solution)/shard_map/ppermute | solution.py:335
  19.2 6.9 %collective-permute-start.3 = (bf16[16,16,256]{2,1,0:T(8,128)(2,1)}, bf16[16,16,256]{2,1,0:T(8,128)(2,1)S(1)}, u32[]{:S(2)}, u32[]{:S(2)}) collective-permute-start(bf16[16,16,256]{2,1,0:T(8,128)(2,1)} %get-tuple-element.71), channel_id=1, source_target_pairs={{0,6},{2,4},{4,2},{6,0},{8,14},{10,12},{12,10},{14,8},{1,7},{3,5},... | collective-permute-start | bytes 393224 | tf_op jit(solution)/shard_map/ppermute | solution.py:335
  24.5 13.4 %copy-start.5 = (bf16[16,16,256]{2,1,0:T(8,128)(2,1)}, bf16[16,16,256]{2,1,0:T(8,128)(2,1)S(1)}, u32[]{:S(2)}) copy-start(bf16[16,16,256]{2,1,0:T(8,128)(2,1)S(1)} %collective-permute-done.1.refs_1_) | copy-start | bytes 393220
  26.2 38.2 %all-to-all-start.1 = ((bf16[8,16,16,256]{3,2,1,0:T(8,128)(2,1)}), bf16[8,16,16,256]{3,2,1,0:T(8,128)(2,1)S(1)}, u32[]{:S(2)}, u32[]{:S(2)}) async-start(bf16[8,16,16,256]{3,2,1,0:T(8,128)(2,1)} %get-tuple-element.72), calls=%async_computation.1 | async-start | bytes 2097152 | tf_op jit(solution)/shard_map/all_to_all | solution.py:369
  29.7 34.7 %collective-permute-start.11 = (bf16[512,1024]{1,0:T(8,128)(2,1)S(1)}, bf16[512,1024]{1,0:T(8,128)(2,1)}, u32[]{:S(2)}, u32[]{:S(2)}) collective-permute-start(bf16[512,1024]{1,0:T(8,128)(2,1)S(1)} %copy-done.9), channel_id=1, source_target_pairs={{0,1},{1,0},{2,3},{3,2},{4,5},{5,4},{6,7},{7,6},{8,9},{9,8},{10,11... | collective-permute-start | bytes 3145736 | tf_op jit(solution)/shard_map/ppermute | solution.py:332
  29.8 34.6 %collective-permute-start.12 = (bf16[1024,512]{1,0:T(8,128)(2,1)}, bf16[1024,512]{1,0:T(8,128)(2,1)}, u32[]{:S(2)}, u32[]{:S(2)}) collective-permute-start(bf16[1024,512]{1,0:T(8,128)(2,1)} %refs_12_.1), channel_id=1, source_target_pairs={{0,1},{1,0},{2,3},{3,2},{4,5},{5,4},{6,7},{7,6},{8,9},{9,8},{10,11... | collective-permute-start | bytes 3145736 | tf_op jit(solution)/shard_map/ppermute | solution.py:332
  30.3 9.7 %collective-permute-start.8 = (bf16[512,256]{1,0:T(8,128)(2,1)S(1)}, bf16[512,256]{1,0:T(8,128)(2,1)}, u32[]{:S(2)}, u32[]{:S(2)}) collective-permute-start(bf16[512,256]{1,0:T(8,128)(2,1)S(1)} %copy-done.11), channel_id=1, source_target_pairs={{0,1},{1,0},{2,3},{3,2},{4,5},{5,4},{6,7},{7,6},{8,9},{9,8},{10,11... | collective-permute-start | bytes 786440 | tf_op jit(solution)/shard_map/ppermute | solution.py:332
  30.4 11.5 %collective-permute-start.9 = (bf16[512,256]{1,0:T(8,128)(2,1)S(1)}, bf16[512,256]{1,0:T(8,128)(2,1)}, u32[]{:S(2)}, u32[]{:S(2)}) collective-permute-start(bf16[512,256]{1,0:T(8,128)(2,1)S(1)} %copy-done.12), channel_id=1, source_target_pairs={{0,1},{1,0},{2,3},{3,2},{4,5},{5,4},{6,7},{7,6},{8,9},{9,8},{10,11... | collective-permute-start | bytes 786440 | tf_op jit(solution)/shard_map/ppermute | solution.py:332
  30.8 2.3 %collective-permute-start.14 = (f32[4]{0:T(128)S(1)}, f32[4]{0:T(128)S(1)}, u32[]{:S(2)}, u32[]{:S(2)}) collective-permute-start(f32[4]{0:T(128)S(1)} %copy-done.16), channel_id=1, source_target_pairs={{0,1},{1,0},{2,3},{3,2},{4,5},{5,4},{6,7},{7,6},{8,9},{9,8},{10,11... | collective-permute-start | bytes 56 | tf_op jit(solution)/shard_map/ppermute | solution.py:332
  33.1 38.5 %copy-start.17 = (f32[4]{0:T(128)}, f32[4]{0:T(128)S(1)}, u32[]{:S(2)}) copy-start(f32[4]{0:T(128)S(1)} %collective-permute-done.14.scale_b_ref) | copy-start | bytes 52
  33.1 3.5 %collective-permute-start.15 = (s32[]{:T(128)}, s32[]{:T(128)}, u32[]{:S(2)}, u32[]{:S(2)}) collective-permute-start(s32[]{:T(128)} %convert_element_type.6), channel_id=1, source_target_pairs={{0,16},{16,0},{1,17},{17,1},{2,18},{18,2},{3,19},{19,3},{4,20},{20... | collective-permute-start | bytes 20 | tf_op jit(solution)/shard_map/ppermute | solution.py:384
  36.6 1.2 %collective-permute-start.13 = (f32[1024]{0:T(1024)S(1)}, f32[1024]{0:T(1024)S(1)}, u32[]{:S(2)}, u32[]{:S(2)}) collective-permute-start(f32[1024]{0:T(1024)S(1)} %copy-done.14), channel_id=1, source_target_pairs={{0,1},{1,0},{2,3},{3,2},{4,5},{5,4},{6,7},{7,6},{8,9},{9,8},{10,11... | collective-permute-start | bytes 12296 | tf_op jit(solution)/shard_map/ppermute | solution.py:332
  37.8 33.9 %copy-start.15 = (f32[1024]{0:T(1024)}, f32[1024]{0:T(1024)S(1)}, u32[]{:S(2)}) copy-start(f32[1024]{0:T(1024)S(1)} %collective-permute-done.13) | copy-start | bytes 12292
  37.8 6.5 %collective-permute-start.10 = (bf16[256,512]{1,0:T(8,128)(2,1)S(1)}, bf16[256,512]{1,0:T(8,128)(2,1)}, u32[]{:S(2)}, u32[]{:S(2)}) collective-permute-start(bf16[256,512]{1,0:T(8,128)(2,1)S(1)} %copy-done.13), channel_id=1, source_target_pairs={{0,1},{1,0},{2,3},{3,2},{4,5},{5,4},{6,7},{7,6},{8,9},{9,8},{10,11... | collective-permute-start | bytes 786440 | tf_op jit(solution)/shard_map/ppermute | solution.py:332
  40.0 6.2 %collective-permute-start.4 = (bf16[16,16,256]{2,1,0:T(8,128)(2,1)}, bf16[16,16,256]{2,1,0:T(8,128)(2,1)S(1)}, u32[]{:S(2)}, u32[]{:S(2)}) collective-permute-start(bf16[16,16,256]{2,1,0:T(8,128)(2,1)} %get-tuple-element.74), channel_id=1, source_target_pairs={{0,2},{2,0},{4,6},{6,4},{8,10},{10,8},{12,14},{14,12},{1,3},{3,1},... | collective-permute-start | bytes 393224 | tf_op jit(solution)/shard_map/ppermute | solution.py:335
  41.9 22.5 %collective-permute-start.7 = (bf16[32,16,256]{2,1,0:T(8,128)(2,1)}, bf16[32,16,256]{2,1,0:T(8,128)(2,1)S(1)}, u32[]{:S(2)}, u32[]{:S(2)}) collective-permute-start(bf16[32,16,256]{2,1,0:T(8,128)(2,1)} %get-tuple-element.81), channel_id=1, source_target_pairs={{0,8},{2,10},{4,12},{6,14},{8,0},{10,2},{12,4},{14,6},{1,9},{3,11}... | collective-permute-start | bytes 786440 | tf_op jit(solution)/shard_map/ppermute | solution.py:335
  44.3 9.8 %collective-permute-start.5 = (bf16[16,16,256]{2,1,0:T(8,128)(2,1)}, bf16[16,16,256]{2,1,0:T(8,128)(2,1)S(1)}, u32[]{:S(2)}, u32[]{:S(2)}) collective-permute-start(bf16[16,16,256]{2,1,0:T(8,128)(2,1)} %get-tuple-element.75), channel_id=1, source_target_pairs={{0,4},{2,6},{4,0},{6,2},{8,12},{10,14},{12,8},{14,10},{1,5},{3,7},... | collective-permute-start | bytes 393224 | tf_op jit(solution)/shard_map/ppermute | solution.py:335
  46.1 18.3 %copy-start.2 = (bf16[16,16,256]{2,1,0:T(8,128)(2,1)}, bf16[16,16,256]{2,1,0:T(8,128)(2,1)S(1)}, u32[]{:S(2)}) copy-start(bf16[16,16,256]{2,1,0:T(8,128)(2,1)S(1)} %collective-permute-done.4.refs_2_) | copy-start | bytes 393220
  46.2 10.0 %collective-permute-start.6 = (bf16[16,16,256]{2,1,0:T(8,128)(2,1)}, bf16[16,16,256]{2,1,0:T(8,128)(2,1)S(1)}, u32[]{:S(2)}, u32[]{:S(2)}) collective-permute-start(bf16[16,16,256]{2,1,0:T(8,128)(2,1)} %get-tuple-element.76), channel_id=1, source_target_pairs={{0,6},{2,4},{4,2},{6,0},{8,14},{10,12},{12,10},{14,8},{1,7},{3,5},... | collective-permute-start | bytes 393224 | tf_op jit(solution)/shard_map/ppermute | solution.py:335
  68.5 3.1 %collective-permute-start.16 = (bf16[64,16,256]{2,1,0:T(8,128)(2,1)}, bf16[64,16,256]{2,1,0:T(8,128)(2,1)S(1)}, u32[]{:S(2)}, u32[]{:S(2)}) collective-permute-start(bf16[64,16,256]{2,1,0:T(8,128)(2,1)} %shard_map.123), channel_id=1, source_target_pairs={{0,1},{1,0},{2,3},{3,2},{4,5},{5,4},{6,7},{7,6},{8,9},{9,8},{10,11... | collective-permute-start | bytes 1572872 | tf_op jit(solution)/shard_map/ppermute | solution.py:332
  92.8 1.6 %collective-permute-start.17 = (bf16[32,512]{1,0:T(8,128)(2,1)}, bf16[32,512]{1,0:T(8,128)(2,1)S(1)}, u32[]{:S(2)}, u32[]{:S(2)}) collective-permute-start(bf16[32,512]{1,0:T(8,128)(2,1)} %shard_map.124), channel_id=1, source_target_pairs={{0,1},{1,0},{2,3},{3,2},{4,5},{5,4},{6,7},{7,6},{8,9},{9,8},{10,11... | collective-permute-start | bytes 98312 | tf_op jit(solution)/shard_map/ppermute | solution.py:332
  (12 other events, 109.4 us)
